TPU v7x, 128 devices: a whole 4x4x4 slice. The times are simulated.
128 devices in a mesh: slab: 64 (over x, z_hi, y, core), batch: 2 (over z_lo).
Axes of the slice: x: 4, y: 4, z: 4 (z_hi: 2, z_lo: 2; z = z_hi * 2 + z_lo), core: 2. Of those that a mesh axis runs over, the one named last changes fastest.
Arguments:
- field: bfloat16 [2, 16, 512, 256, 128], P('batch', None, 'slab'), may hold values from -6 to 6
- cotangent: bfloat16 [2, 16, 512, 256, 128], P('batch', None, 'slab'), may hold values from -6 to 6
- spectral_weight: bfloat16 [1024, 2, 16, 512], P('slab'), may hold values from -1 to 1
- point_weight: bfloat16 [16, 16], replicated, may hold values from -1.5 to 1.5
- point_bias: float32 [16], replicated, may hold values from -3 to 3
Outputs:
- input_grad: bfloat16 [2, 16, 512, 256, 128], P('batch', None, 'slab')
- grad_spec: float32 [1024, 2, 16, 512], P('slab')
- grad_point: float32 [16, 16], replicated
- grad_bias: float32 [16], replicated
All inputs are finite; a program needn't handle non-finite values.
Results may differ from a plain program's by a relative error of at most 0.018.
Values may be sent and summed in bfloat16 or wider, within the bound.
No kernel may reach another device: no remote copies, remote signals or barrier semaphores. Data moves between devices by JAX's collectives and lax.ppermute only.
A program may use at most 192 MiB of HBM per device.

v0:
```python
import math

import jax
import jax.numpy as jnp
from jax import lax
from jax.sharding import PartitionSpec as P

MX = 32
MY = 32
MZ = 32


def half_einsum(form, left, right):
    return jnp.einsum(form, left, right, preferred_element_type=jnp.float32)


def mode_freqs(number, length):
    indices = jnp.arange(number, dtype=jnp.int32)
    return jnp.where(indices < number // 2, indices, indices + (length - number))


def phase_grid(positions, frequencies, length):
    product = positions[:, None] * frequencies[None, :] % length
    return product.astype(jnp.float32) * (2.0 * math.pi / length)


def rotation(phases, orient):
    cosine = jnp.cos(phases)
    sine_part = orient * jnp.sin(phases)
    upper = jnp.stack([cosine, -sine_part], axis=1)
    lower = jnp.stack([sine_part, cosine], axis=1)
    return jnp.stack([upper, lower], axis=0).astype(jnp.bfloat16)


def plane_tables(rows_y, rows_z):
    phase_y = phase_grid(jnp.arange(rows_y, dtype=jnp.int32), mode_freqs(MY, rows_y), rows_y)
    phase_z = phase_grid(
        jnp.arange(rows_z, dtype=jnp.int32), jnp.arange(MZ, dtype=jnp.int32), rows_z
    )
    forward_y = jnp.stack([jnp.cos(phase_y), -jnp.sin(phase_y)], axis=1).astype(jnp.bfloat16)
    forward_z = rotation(phase_z, 1.0)
    inverse_z = rotation(phase_z.T, -1.0)
    inverse_y = jnp.stack([jnp.cos(phase_y).T, -jnp.sin(phase_y).T], axis=0).astype(jnp.bfloat16)
    return (forward_y, forward_z, inverse_z, inverse_y)


def yz_forward(slab_data, tables):
    partial_value = half_einsum("bcxyz,yrm->bcxrmz", slab_data, tables[0]).astype(jnp.bfloat16)
    spectrum = half_einsum("bcxrmz,rzsk->bcxsmk", partial_value, tables[1]).astype(jnp.bfloat16)
    return spectrum.reshape(spectrum.shape[:4] + (MY * MZ,))


def yz_inverse(planes_in, tables, factor):
    shaped = planes_in.reshape(planes_in.shape[:4] + (MY, MZ))
    rolled = half_einsum("boxsmk,skrz->boxrmz", shaped, tables[2]).astype(jnp.bfloat16)
    return factor * half_einsum("boxrmz,rmy->boxyz", rolled, tables[3])


def mix_modes(spectrum, weights_f):

    def apply(values, weight_part):
        return jnp.einsum("biap,pioa->boap", values, weight_part, precision=lax.Precision.HIGHEST)

    real_part, imag_part = (spectrum[:, :, 0], spectrum[:, :, 1])
    first = apply(real_part, weights_f[:, 0]) - apply(imag_part, weights_f[:, 1])
    second = apply(real_part, weights_f[:, 1]) + apply(imag_part, weights_f[:, 0])
    return jnp.stack([first, second], axis=2)


def adjoint_mix(spectrum, weights_f):

    def apply(values, weight_part):
        return jnp.einsum("boap,pioa->biap", values, weight_part, precision=lax.Precision.HIGHEST)

    real_part, imag_part = (spectrum[:, :, 0], spectrum[:, :, 1])
    first = apply(real_part, weights_f[:, 0]) + apply(imag_part, weights_f[:, 1])
    second = apply(imag_part, weights_f[:, 0]) - apply(real_part, weights_f[:, 1])
    return jnp.stack([first, second], axis=2)


def weight_grad(modes_in, modes_out):

    def apply(left, right):
        return jnp.einsum("biap,boap->pioa", left, right, precision=lax.Precision.HIGHEST)

    first = apply(modes_in[:, :, 0], modes_out[:, :, 0]) + apply(
        modes_in[:, :, 1], modes_out[:, :, 1]
    )
    second = apply(modes_in[:, :, 0], modes_out[:, :, 1]) - apply(
        modes_in[:, :, 1], modes_out[:, :, 0]
    )
    stacked = jnp.stack([first, second], axis=1)
    return stacked.reshape(
        stacked.shape[0], 2, stacked.shape[2], stacked.shape[3] * stacked.shape[4]
    )


def activation_grad(pre, upstream):
    _, pull = jax.vjp(lambda values: jax.nn.gelu(values, approximate=True), pre)
    return pull(upstream)[0]


def body(field, cotangent, spectral_weight, point_weight, point_bias):
    samples, channels, planes, rows_y, rows_z = field.shape
    total_x = planes * lax.axis_size("slab")
    total_samples = samples * lax.axis_size("batch")
    tables = plane_tables(rows_y, rows_z)
    freq_x = mode_freqs(MX, total_x)
    local_x = lax.axis_index("slab") * planes + jnp.arange(planes, dtype=jnp.int32)
    phase_local = phase_grid(local_x, freq_x, total_x)
    cells = total_x * rows_y * rows_z
    scale_f = 1.0 / math.sqrt(cells)
    scale_i = 1.0 / math.sqrt(MX * MY * MZ)
    scale_p = 1.0 / math.sqrt(total_samples * cells)
    scale_w = math.sqrt(MX * MY * MZ / (total_samples * cells))
    weights_f = spectral_weight.astype(jnp.float32).reshape(
        spectral_weight.shape[0], 2, channels, channels, MX
    )

    def to_modes(spectrum, factor):
        partial_value = factor * half_einsum(
            "bcxrp,rxsa->bcsap", spectrum, rotation(phase_local, 1.0)
        )
        return lax.psum_scatter(partial_value, "slab", scatter_dimension=4, tiled=True)

    def to_slabs(spectrum):
        table_local = rotation(phase_local.T, -1.0)
        return half_einsum(
            "bosap,sarx->boxrp", lax.all_gather(spectrum, "slab", axis=4, tiled=True), table_local
        ).astype(jnp.bfloat16)

    modes_u = to_modes(yz_forward(field, tables), scale_f)
    mixed = mix_modes(modes_u, weights_f).astype(jnp.bfloat16)
    back_v = to_slabs(mixed)
    pre = yz_inverse(back_v, tables, scale_i) + half_einsum("bixyz,io->boxyz", field, point_weight)
    pre = pre + point_bias[None, :, None, None, None]
    dpre = activation_grad(pre, cotangent.astype(jnp.float32)).astype(jnp.bfloat16)
    point_local = half_einsum("bixyz,boxyz->io", field, dpre)
    bias_local = jnp.sum(dpre.astype(jnp.float32), axis=(0, 2, 3, 4))
    point_total, bias_total = lax.psum((point_local, bias_local), ("slab", "batch"))
    modes_d = to_modes(yz_forward(dpre, tables), scale_i)
    spec_total = lax.psum(weight_grad(modes_u, modes_d).astype(jnp.bfloat16), "batch").astype(
        jnp.float32
    )
    back_d = to_slabs(adjoint_mix(modes_d, weights_f).astype(jnp.bfloat16))
    input_grad = yz_inverse(back_d, tables, scale_f) + half_einsum(
        "boxyz,io->bixyz", dpre, point_weight
    )
    return (
        input_grad.astype(jnp.bfloat16),
        scale_w * spec_total,
        scale_p * point_total,
        scale_p * bias_total,
    )


def solution(mesh):
    placed = (
        P("batch", None, "slab", None, None),
        P("batch", None, "slab", None, None),
        P("slab", None, None, None),
        P(),
        P(),
    )
    return jax.shard_map(
        body,
        mesh=mesh,
        in_specs=placed,
        out_specs=(P("batch", None, "slab", None, None), P("slab", None, None, None), P(), P()),
        check_vma=False,
    )
```

profile of v0, /device:TPU:1, one launch (start us, length us, event | category | flops | bytes accessed | tf_op | source)
XLA Modules:
  0.0 1079.7 jit_solution(6256380640119075778)
XLA Ops:
  7.2 0.0 copy-start
  7.2 0.0 reduce-scatter.3.cloned.1.call-start
  7.2 0.1 negate_convert_fusion.2
  7.3 0.1 fusion.126
  7.4 0.2 cosine_convert_fusion
  7.6 5.0 convert_bitcast_fusion.1
  12.6 3.1 fusion.55
  15.8 3.0 copy.60
  18.8 2.3 reshape.950
  21.2 0.1 negate_convert_fusion.4
  21.3 2.8 fusion.28
  24.1 14.3 %copy.61 = f32[1,16,2,32,1024]{3,1,2,0,4:T(8,128)} copy(f32[1,16,2,32,1024]{4,3,1,2,0:T(8,128)} %fusion.28) | data formatting | bytes 8388608 | tf_op jit(solution)/shard_map/mul | solution.py:121
  38.4 0.0 reduce-scatter.3.cloned.1.call-update
  38.5 0.0 all-gather.3.cloned.1.call-start
  38.5 1.0 copy-done.1
  39.5 1.2 reshape.931
  40.7 353.1 %reduce-scatter.3.cloned.1.call-done = f32[1,16,2,32,16]{3,1,2,0,4:T(8,128)} async-done(((f32[1,16,2,32,1024]{3,1,2,0,4:T(8,128)}), f32[1,16,2,32,16]{3,1,2,0,4:T(8,128)}) %reduce-scatter.3.cloned.1.call-update) | async-done | bytes 65552 | tf_op jit(solution)/shard_map/reduce_scatter | solution.py:124
  393.8 1.0 slice_bitcast_fusion.7
  394.8 1.2 fusion.31
  396.0 0.7 pad_maximum_fusion.1
  396.7 0.0 all-gather.3.cloned.1.call-update
  396.7 0.0 reduce-scatter.5.cloned.1.call-start
  396.8 0.1 fusion.124
  396.9 0.1 negate_convert_fusion.5
  397.0 0.1 negate_convert_fusion.3
  397.1 0.0 copy-start.2
  397.1 0.0 copy-start.4
  397.1 0.2 cosine_convert_fusion.1
  397.4 12.4 %fusion.25 = f32[16,8,256,128]{3,0,2,1:T(8,128)} fusion(bf16[16,8,256,128]{3,2,1,0:T(8,128)(2,1)} %bitcast.408, bf16[16,16]{1,0:T(8,128)(2,1)S(1)} %copy-done), kind=kOutput, calls=%fused_computation.32 | convolution fusion | flops 134217728 | bytes 25166336 | tf_op jit(solution)/shard_map/bixyz,io->boxyz/dot_general | solution.py:14
  409.8 74.5 %all-gather.3.cloned.1.call-done = bf16[1,16,2,32,1024]{3,1,2,0,4:T(8,128)(2,1)} async-done(((bf16[1,16,2,32,16]{3,1,2,0,4:T(8,128)(2,1)}), bf16[1,16,2,32,1024]{3,1,2,0,4:T(8,128)(2,1)}) %all-gather.3.cloned.1.call-update) | async-done | bytes 2097168 | tf_op jit(solution)/shard_map/all_gather | solution.py:129
  484.3 9.3 copy.62
  493.7 2.0 fusion.81
  495.7 2.6 reshape.934
  498.3 21.4 %convert_reduce_fusion = (f32[16]{0:T(128)S(1)}, bf16[1,16,8,256,128]{4,3,2,1,0:T(8,128)(2,1)}) fusion(f32[16]{0:T(128)S(1)} %copy-done.10, f32[16,8,256,128]{3,0,2,1:T(8,128)} %fusion.25, bf16[16,8,2,32,32]{4,3,1,0,2:T(8,128)(2,1)} %reshape.934, bf16[1,32,2,128]{3,1,0,2:T(8,128)(2,1)S(1)} %get-tuple-element.41, ...), kind=kOutput, calls=%fused_computation.22 | convolution fusion | flops 781320192 | bytes 34144384 | tf_op jit(solution)/shard_map/boxrmz,rmy->boxyz/dot_general | solution.py:14
  519.8 5.0 convert_bitcast_fusion
  524.8 3.2 fusion.58
  527.9 16.4 %copy.69 = bf16[1,16,8,2,32,32]{5,4,2,3,1,0:T(8,128)(2,1)} copy(bf16[1,16,8,2,32,32]{4,5,2,1,3,0:T(8,128)(2,1)} %fusion.58) | data formatting | bytes 1048576 | tf_op jit(solution)/shard_map/convert_element_type | solution.py:49
  544.3 3.5 reshape.972
  547.9 2.7 fusion.27
  550.6 14.3 %copy.70 = f32[1,16,2,32,1024]{3,1,2,0,4:T(8,128)} copy(f32[1,16,2,32,1024]{4,3,1,2,0:T(8,128)} %fusion.27) | data formatting | bytes 8388608 | tf_op jit(solution)/shard_map/mul | solution.py:121
  564.9 0.0 reduce-scatter.5.cloned.1.call-update
  564.9 0.0 all-reduce.3.cloned.1.call-start
  565.0 349.2 %reduce-scatter.5.cloned.1.call-done = f32[1,16,2,32,16]{3,1,2,0,4:T(8,128)} async-done(((f32[1,16,2,32,1024]{3,1,2,0,4:T(8,128)}), f32[1,16,2,32,16]{3,1,2,0,4:T(8,128)}) %reduce-scatter.5.cloned.1.call-update) | async-done | bytes 65552 | tf_op jit(solution)/shard_map/reduce_scatter | solution.py:124
  914.2 1.7 slice_bitcast_fusion.3
  915.8 1.6 fusion.92
  917.4 2.2 stack.181
  919.6 1.8 stack.182
  921.4 1.8 pad_maximum_fusion
  923.2 0.0 all-reduce.3.cloned.1.call-update
  923.2 0.0 all-gather.5.cloned.1.call-start
  923.2 3.2 fusion.35
  926.5 0.7 pad_maximum_fusion.2
  927.2 0.0 all-gather.5.cloned.1.call-update
  927.2 15.2 %fusion.87 = f32[16,16]{0,1:T(8,128)S(1)} fusion(bf16[16,8,256,128]{3,2,1,0:T(8,128)(2,1)} %bitcast.409, bf16[16,8,256,128]{3,2,1,0:T(8,128)(2,1)} %bitcast.410), kind=kOutput, calls=%fused_computation.84 | convolution fusion | flops 134217728 | bytes 16778240 | tf_op jit(solution)/shard_map/bixyz,boxyz->io/dot_general | solution.py:14
  942.4 70.8 %all-reduce = (f32[16,16]{0,1:T(8,128)S(1)}, f32[16]{0:T(128)S(1)}) all-reduce(f32[16,16]{0,1:T(8,128)S(1)} %fusion.87, f32[16]{0:T(128)S(1)} %get-tuple-element.58), channel_id=1, replica_groups=mesh['slab'=64,'batch'=2] {'slab','batch'}, use_global_device_ids=true, to_apply=%region_3.4 | all-reduce | flops 272 | bytes 2176 | tf_op jit(solution)/shard_map/psum | solution.py:140
  1013.2 0.7 copy.78
  1013.8 0.5 broadcast_multiply_fusion.1
  1014.4 14.2 %fusion.22 = f32[8,256,128,16]{2,3,1,0:T(8,128)} fusion(bf16[16,8,256,128]{3,2,1,0:T(8,128)(2,1)} %bitcast.411, bf16[16,16]{1,0:T(8,128)(2,1)S(1)} %copy-done), kind=kOutput, calls=%fused_computation.29 | convolution fusion | flops 134217728 | bytes 25166336 | tf_op jit(solution)/shard_map/boxyz,io->bixyz/dot_general | solution.py:14
  1028.5 2.2 convert_multiply_fusion.10
  1030.7 18.8 %all-gather.5.cloned.1.call-done = bf16[1,16,2,32,1024]{3,1,2,0,4:T(8,128)(2,1)} async-done(((bf16[1,16,2,32,16]{3,1,2,0,4:T(8,128)(2,1)}), bf16[1,16,2,32,1024]{3,1,2,0,4:T(8,128)(2,1)}) %all-gather.5.cloned.1.call-update) | async-done | bytes 2097168 | tf_op jit(solution)/shard_map/all_gather | solution.py:129
  1049.5 8.3 copy.71
  1057.8 0.4 fusion.84
  1058.3 1.6 reshape.942
  1059.9 12.8 %fusion.12 = bf16[1,16,8,256,128]{4,3,2,1,0:T(8,128)(2,1)} fusion(f32[8,256,128,16]{2,3,1,0:T(8,128)} %fusion.22, bf16[16,8,2,32,32]{4,3,1,0,2:T(8,128)(2,1)S(1)} %reshape.942, bf16[1,32,2,128]{3,1,0,2:T(8,128)(2,1)S(1)} %copy-done.5, bf16[1,32,2,128]{3,1,0,2:T(8,128)(2,1)S(1)} %copy-done.3, bf16[1,32,256]{2,1,0:T(8,128)(2,1)S(1)} %copy-done.9, ...), kind=kOutput, calls=%fused_computation.17 | convolution fusion | flops 684851200 | bytes 25755648 | tf_op jit(solution)/shard_map/boxrmz,rmy->boxyz/dot_general | solution.py:14
  (31 shorter events, 0.2 us)
Async XLA Ops:
  7.2 390.2 %copy-start = (bf16[16,16]{1,0:T(8,128)(2,1)S(1)}, bf16[16,16]{1,0:T(8,128)(2,1)}, u32[]{:S(2)}) copy-start(bf16[16,16]{1,0:T(8,128)(2,1)} %param.8) | copy-start | bytes 1540
  7.2 386.6 %reduce-scatter.3.cloned.1.call-start = ((), (), s32[]{:S(2)}) async-start(), calls=%async_computation.2 | async-start | bytes 17039360 | tf_op jit(solution)/shard_map/reduce_scatter | solution.py:124
  38.4 1.0 copy-start.1
  38.5 445.9 %all-gather.3.cloned.1.call-start = ((), (), s32[]{:S(2)}) async-start(), calls=%async_computation.3 | async-start | bytes 8519680 | tf_op jit(solution)/shard_map/all_gather | solution.py:129
  396.7 517.5 %reduce-scatter.5.cloned.1.call-start = ((), (), s32[]{:S(2)}) async-start(), calls=%async_computation.4 | async-start | bytes 17039360 | tf_op jit(solution)/shard_map/reduce_scatter | solution.py:124
  397.1 101.2 %copy-start.2 = (bf16[1,32,2,128]{3,1,0,2:T(8,128)(2,1)}, bf16[1,32,2,128]{3,1,0,2:T(8,128)(2,1)S(1)}, u32[]{:S(2)}) copy-start(bf16[1,32,2,128]{3,1,0,2:T(8,128)(2,1)S(1)} %get-tuple-element.40) | copy-start | bytes 49156
  397.1 101.2 %copy-start.4 = (bf16[1,32,2,128]{3,1,0,2:T(8,128)(2,1)}, bf16[1,32,2,128]{3,1,0,2:T(8,128)(2,1)S(1)}, u32[]{:S(2)}) copy-start(bf16[1,32,2,128]{3,1,0,2:T(8,128)(2,1)S(1)} %get-tuple-element.41) | copy-start | bytes 49156
  397.3 101.0 %copy-start.6 = (bf16[1,32,256]{2,1,0:T(8,128)(2,1)}, bf16[1,32,256]{2,1,0:T(8,128)(2,1)S(1)}, u32[]{:S(2)}) copy-start(bf16[1,32,256]{2,1,0:T(8,128)(2,1)S(1)} %get-tuple-element.54) | copy-start | bytes 49156
  397.4 101.0 %copy-start.8 = (bf16[1,32,256]{2,1,0:T(8,128)(2,1)}, bf16[1,32,256]{2,1,0:T(8,128)(2,1)S(1)}, u32[]{:S(2)}) copy-start(bf16[1,32,256]{2,1,0:T(8,128)(2,1)S(1)} %get-tuple-element.55) | copy-start | bytes 49156
  493.7 4.7 copy-start.10
  564.9 463.6 %all-reduce.3.cloned.1.call-start = ((), (), s32[]{:S(2)}) async-start(), calls=%async_computation.6 | async-start | bytes 1048576 | tf_op jit(solution)/shard_map/psum | solution.py:142
  923.2 126.3 %all-gather.5.cloned.1.call-start = ((), (), s32[]{:S(2)}) async-start(), calls=%async_computation.5 | async-start | bytes 8519680 | tf_op jit(solution)/shard_map/all_gather | solution.py:129
  1057.8 2.1 copy-start.3
  1057.8 2.1 copy-start.5
  1057.8 2.1 copy-start.7
  1057.8 2.1 copy-start.9
Sparse Core Ops, SparseCore 0:
  38.6 355.1 reduce-scatter.2
  397.5 86.7 all-gather.2
  565.0 349.1 reduce-scatter.4
  923.3 37.4 all-reduce.2
  964.3 85.1 all-gather.4
where the time goes:
time: 1090 us; the launch traced here: 1080 us
  waiting for transfers between devices  796 us (73%)
  matrix products  100 us (9%)
  local copies, waits for them, and re-layouts  85.3 us (8%)
  blocking collectives  70.8 us (6%)
  between operations  14.6 us (1%)
  other arithmetic  12.9 us (1%)
    reduce_scatter x2, waiting for transfers between devices, to_modes(): lax.psum_scatter(partial_value, 'slab', scatter_dimension=4, tiled=True)  702 us
    dot_general x13, matrix products, half_einsum(): return jnp.einsum(form, left, right, preferred_element_type=jnp.float32)  100 us
    all_gather x2, waiting for transfers between devices, to_slabs(): lax.all_gather(spectrum, 'slab', axis=4, tiled=True)  93.3 us
    psum x1, blocking collectives, body(): lax.psum((point_local, bias_local), ('slab', 'batch'))  70.8 us
    mul x2, local copies, waits for them, and re-layouts, to_modes(): factor * half_einsum('bcxrp,rxsa->bcsap', spectrum, rotation(phase_local,...  28.7 us
  transfers between devices with their start and end apart: 5, of which 4 were waited for; matrix products, arithmetic and copies ran while one was open for 5% of the time, Pallas kernels for 0%

commit v1 on v0

v1 whole, which is shorter than its diff:
```python
import math

import jax
import jax.numpy as jnp
import numpy as np
from jax import lax
from jax.experimental import pallas as pl
from jax.experimental.pallas import tpu as pltpu
from jax.sharding import PartitionSpec as P

C = 16
X = 8
NY = 256
NZ = 128
NX = 512
MODES = 32
SLABS = 64
CELLS = NX * NY * NZ
SCALE_F = 1.0 / math.sqrt(CELLS)
SCALE_I = 1.0 / math.sqrt(MODES**3)
SCALE_P = 1.0 / math.sqrt(2 * CELLS)
SCALE_W = math.sqrt(MODES**3 / (2 * CELLS))
GELU_A = math.sqrt(2.0 / math.pi)
GK = (GELU_A * 0.044715) ** (1.0 / 3.0)
GA = GELU_A / GK
BOTH = ("slab", "batch")
F32 = jnp.float32
BF16 = jnp.bfloat16
MIB = 1 << 20


def freqs(number, length):
    index = np.arange(number)
    return np.where(index < number // 2, index, index + length - number)


def angles(length, frequencies):
    product = (np.arange(length)[:, None] * frequencies[None, :]) % length
    return product * (2.0 * math.pi / length)


def tables():
    thy = angles(NY, freqs(MODES, NY))
    thz = angles(NZ, np.arange(MODES))
    thx = angles(NX, freqs(MODES, NX))
    ty = np.concatenate([np.cos(thy).T, -np.sin(thy).T], axis=0)
    cos, sin = np.cos(thz), np.sin(thz)
    rot = np.zeros((2, NZ, 2, MODES))
    rot[0, :, 0], rot[1, :, 0] = cos, sin
    rot[1, :, 1], rot[0, :, 1] = cos, -sin
    zb = rot.reshape(2, NZ, 2, 4, 8).transpose(0, 1, 3, 2, 4)[:, :, :, :, None, :]
    zb = np.broadcast_to(zb, (2, NZ, 4, 2, 8, 8)).reshape(2 * NZ, 512)
    cs = np.stack([np.cos(thx), np.sin(thx)]).reshape(2, SLABS, X, MODES)
    tx = np.zeros((2, 2, 4, MODES, SLABS, 2, X))
    txi = np.zeros((SLABS, 2, X, 2, 2, MODES))
    for half in range(2):
        tx[half, :, :, :, :, half] = cs.transpose(0, 3, 1, 2)[:, None]
        txi[:, half, :, half] = cs.transpose(1, 2, 0, 3)
    return tuple(
        np.asarray(t, np.float32).astype(BF16)
        for t in (ty, ty.T, zb, tx.reshape(512, 1024), txi.reshape(1024, 128))
    )


def dot(left, right):
    return jnp.dot(left, right, preferred_element_type=F32)


def dot_nt(left, right):
    return lax.dot_general(left, right, (((1,), (1,)), ((), ())), preferred_element_type=F32)


def build_z(zb_ref, zf_ref):
    table = zb_ref[...].astype(F32)
    channel = (lax.broadcasted_iota(jnp.int32, (2 * NZ, 512), 1) // 8) % 8
    for c in range(8):
        zf_ref[c * 256 : (c + 1) * 256, :] = jnp.where(channel == c, table, 0.0).astype(BF16)


def z_forward(planes_ref, zf_ref, wide_ref, out_ref):
    for half in range(2):
        result = dot(planes_ref[half * 256 : (half + 1) * 256, :], zf_ref[...])
        for x in range(X):
            for kq in range(4):
                wide_ref[pl.ds(kq * 16 + half * 8 + x, 32, stride=64), :] = result[
                    x * 32 : (x + 1) * 32, kq * 128 : (kq + 1) * 128
                ]
    out_ref[...] = wide_ref[...].astype(BF16).reshape(128, 16, 128)


def z_inverse(in_ref, zf_ref, wide_ref, gather_ref, rolled_ref):
    wide_ref[...] = in_ref[...].astype(F32).reshape(2048, 128)
    for half in range(2):
        for x in range(X):
            for kq in range(4):
                row = (half * 8 + x) * 32
                gather_ref[row : row + 32, kq * 128 : (kq + 1) * 128] = wide_ref[
                    pl.ds(kq * 16 + half * 8 + x, 32, stride=64), :
                ].astype(BF16)
    for c in range(8):
        rolled_ref[:, c * 256 : (c + 1) * 256] = dot_nt(
            gather_ref[...], zf_ref[c * 256 : (c + 1) * 256, :]
        ).astype(BF16)


def y_forward(ty_ref, pair, planes_ref, x, op):
    result = dot(ty_ref[...], pair)
    half, first = op // 4, (op % 4) * 2
    rows = pl.ds(pl.multiple_of(half * 256 + x * 32, 32), 32)
    for j in range(2):
        for part in range(2):
            column = (first + j) * 256 + part * 128
            planes_ref[rows, column : column + 128] = result[
                part * 32 : (part + 1) * 32, j * 128 : (j + 1) * 128
            ].astype(BF16)
    return result


def y_inverse(tyt_ref, rolled_ref, x, op):
    half, first = op // 4, (op % 4) * 2
    rows = pl.ds(pl.multiple_of(half * 256 + x * 32, 32), 32)
    blocks = []
    for j in range(2):
        column = (first + j) * 256
        blocks.append(
            jnp.concatenate(
                [
                    rolled_ref[rows, column : column + 128],
                    rolled_ref[rows, column + 128 : column + 256],
                ],
                axis=0,
            )
        )
    return dot(tyt_ref[...], jnp.concatenate(blocks, axis=1))


def field_kernel(field_ref, ty_ref, zb_ref, out_ref, zf_ref, planes_ref, wide_ref):
    x = pl.program_id(0)

    @pl.when(x == 0)
    def _():
        build_z(zb_ref, zf_ref)

    for op in range(8):
        pair = jnp.concatenate([field_ref[2 * op], field_ref[2 * op + 1]], axis=1)
        y_forward(ty_ref, pair, planes_ref, x, op)

    @pl.when(x == X - 1)
    def _():
        z_forward(planes_ref, zf_ref, wide_ref, out_ref)


def y_blocks(ref):
    return jnp.concatenate(
        [ref[:, b * 16 : (b + 1) * 16, :].reshape(256, 128) for b in range(16)], axis=1
    )


def map_kernel(scale, in_ref, kron_ref, bias_ref, out_ref):
    for b in range(8):
        pair = jnp.concatenate(
            [in_ref[:, y : y + 16, :].reshape(256, 128) for y in (b * 32, b * 32 + 16)], axis=1
        )
        result = dot(kron_ref[...], pair)
        if bias_ref is not None:
            result = result + bias_ref[...]
        result = (result * scale).astype(BF16)
        for j in range(2):
            y = b * 32 + j * 16
            out_ref[:, y : y + 16, :] = result[:, j * 128 : (j + 1) * 128].reshape(C, 16, 128)


def pre_kernel(in_ref, kron_ref, bias_ref, out_ref):
    map_kernel(GK, in_ref, kron_ref, bias_ref, out_ref)


def back_kernel(in_ref, kron_ref, out_ref):
    map_kernel(0.5, in_ref, kron_ref, None, out_ref)


def signal_kernel(
    in_ref, pre_ref, cot_ref, ty_ref, tyt_ref, zb_ref,
    dpre_ref, out_ref, bias_ref,
    zf_ref, planes_ref, wide_ref, gather_ref, rolled_ref,
):
    x = pl.program_id(0)

    @pl.when(x == 0)
    def _():
        build_z(zb_ref, zf_ref)
        z_inverse(in_ref, zf_ref, wide_ref, gather_ref, rolled_ref)
        bias_ref[...] = jnp.zeros_like(bias_ref)

    for op in range(8):
        back = y_inverse(tyt_ref, rolled_ref, x, op)
        pair = []
        for j in range(2):
            o = 2 * op + j
            h = back[:, j * 128 : (j + 1) * 128] + pre_ref[o].astype(F32)
            square = h * h
            t = jnp.tanh(h * (square + GA))
            slope = h * (square * 3.0 + GA)
            d = (1.0 + t) * (1.0 + (1.0 - t) * slope) * cot_ref[o].astype(F32)
            d = d.astype(BF16)
            dpre_ref[o] = d
            pair.append(d)
        result = y_forward(ty_ref, jnp.concatenate(pair, axis=1), planes_ref, x, op)
        bias_ref[op : op + 1, :] += result[0:1, :]

    @pl.when(x == X - 1)
    def _():
        z_forward(planes_ref, zf_ref, wide_ref, out_ref)


def final_kernel(
    in_ref, mapped_ref, tyt_ref, zb_ref, out_ref, zf_ref, wide_ref, gather_ref, rolled_ref
):
    x = pl.program_id(0)

    @pl.when(x == 0)
    def _():
        build_z(zb_ref, zf_ref)
        z_inverse(in_ref, zf_ref, wide_ref, gather_ref, rolled_ref)

    for op in range(8):
        back = y_inverse(tyt_ref, rolled_ref, x, op)
        for j in range(2):
            o = 2 * op + j
            out_ref[o] = (back[:, j * 128 : (j + 1) * 128] + mapped_ref[o].astype(F32)).astype(BF16)


def x_forward(in_ref, tx_ref, scale, modes_ref):
    data = jnp.concatenate([in_ref[:, b].reshape(1024, 128) for b in range(2)], axis=1)
    raw = dot(tx_ref[...], data)
    lane = lax.broadcasted_iota(jnp.int32, (128, 128), 1)
    sign = jnp.where(lane < 64, scale, -scale)
    for half in range(2):
        for b in range(2):
            cosine = raw[half * 256 : half * 256 + 128, b * 128 : (b + 1) * 128]
            sine = raw[half * 256 + 128 : half * 256 + 256, b * 128 : (b + 1) * 128]
            modes = cosine * scale + pltpu.roll(sine, 64, 1) * sign
            row = (half * 2 + b) * 128
            modes_ref[row : row + 128, :] = modes.T


def x_inverse(mixed, txi_ref, out_ref):
    lane = lax.broadcasted_iota(jnp.int32, (32, 128), 1)
    rows = []
    for half in range(2):
        turned = [mixed(half, b).T[:32] for b in range(2)]
        rows.append(jnp.concatenate(turned, axis=1))
        rows.append(
            jnp.concatenate(
                [jnp.where(lane < 64, -1.0, 1.0) * pltpu.roll(g, 64, 1) for g in turned], axis=1
            )
        )
    result = dot(txi_ref[...], jnp.concatenate(rows, axis=0).astype(BF16)).astype(BF16)
    for b in range(2):
        out_ref[:, b] = result[:, b * 128 : (b + 1) * 128].reshape(SLABS, 16, 128)


def mix_kernel(which_ref, in_ref, weight_ref, tx_ref, txi_ref, out_ref, modes_ref, mixed_ref):
    x_forward(in_ref, tx_ref, SCALE_F, modes_ref)
    first = which_ref[0] * 8
    for p in range(8):
        real = weight_ref[first + p, 0].astype(F32)
        imag = weight_ref[first + p, 1].astype(F32)
        for b in range(2):
            u = [
                [modes_ref[pl.ds((half * 2 + b) * 128 + s * 64 + p, 8, stride=8), :] for s in range(2)]
                for half in range(2)
            ]
            for q in range(4):
                total = [0.0, 0.0]
                for half in range(2):
                    w0 = real[half * 8 : half * 8 + 8, q * 128 : (q + 1) * 128]
                    w1 = imag[half * 8 : half * 8 + 8, q * 128 : (q + 1) * 128]
                    u0, u1 = u[half]
                    total[0] = total[0] + (u0 * w0 - u1 * w1)
                    total[1] = total[1] + (u0 * w1 + u1 * w0)
                for s in range(2):
                    row = (b * 2 + s) * 8 + p
                    mixed_ref[row : row + 1, q * 128 : (q + 1) * 128] = jnp.sum(
                        total[s], axis=0, keepdims=True
                    ) * (SCALE_I * GK)

    def mixed(half, b):
        pieces = []
        for s in range(2):
            row = (b * 2 + s) * 8
            for c in range(8):
                q, r = divmod(half * 8 + c, 4)
                piece = mixed_ref[row : row + 8, q * 128 : (q + 1) * 128]
                pieces.append(pltpu.roll(piece, (128 - 32 * r) % 128, 1) if r else piece)
        return jnp.concatenate(pieces, axis=0)

    x_inverse(mixed, txi_ref, out_ref)


def adjoint_kernel(
    which_ref, in_ref, weight_ref, tx_ref, txi_ref, out_ref, rows_ref, modes_ref, mixed_ref
):
    x_forward(in_ref, tx_ref, 0.5 * SCALE_I, modes_ref)
    group = lax.broadcasted_iota(jnp.int32, (8, 128), 1) // 32
    for b in range(2):
        for s in range(2):
            for q in range(4):
                half, c = q // 2, (q % 2) * 4
                row = (half * 2 + b) * 128 + s * 64 + c * 8
                value = modes_ref[row : row + 8, :]
                for r in range(1, 4):
                    value = jnp.where(group == r, modes_ref[row + 8 * r : row + 8 * r + 8, :], value)
                row = (b * 2 + s) * 8
                rows_ref[row : row + 8, q * 128 : (q + 1) * 128] = value
    first = which_ref[0] * 8
    for p in range(8):
        real = weight_ref[first + p, 0].astype(F32)
        imag = weight_ref[first + p, 1].astype(F32)
        for b in range(2):
            d0 = rows_ref[b * 16 + p : b * 16 + p + 1, :]
            d1 = rows_ref[b * 16 + 8 + p : b * 16 + 8 + p + 1, :]
            total0 = real * d0 + imag * d1
            total1 = real * d1 - imag * d0
            for s, total in enumerate((total0, total1)):
                folded = sum(total[:, q * 128 : (q + 1) * 128] for q in range(4))
                folded = folded + pltpu.roll(folded, 64, 1)
                folded = folded + pltpu.roll(folded, 32, 1)
                for half in range(2):
                    mixed_ref[pl.ds((half * 2 + b) * 128 + s * 64 + p, 8, stride=8), :] = (
                        folded[half * 8 : half * 8 + 8] * SCALE_F
                    )

    def mixed(half, b):
        row = (half * 2 + b) * 128
        return mixed_ref[row : row + 128, :]

    x_inverse(mixed, txi_ref, out_ref)


def spec_kernel(which_ref, u_ref, v_ref, d_ref, e_ref, out_ref):
    mine = which_ref[0] * 8
    other = 8 - mine
    for start, modes_ref, rows_ref in ((mine, u_ref, d_ref), (other, v_ref, e_ref)):
        for p in range(8):
            for half in range(2):
                u = [
                    [
                        modes_ref[pl.ds((half * 2 + b) * 128 + s * 64 + p, 8, stride=8), :] * SCALE_W
                        for s in range(2)
                    ]
                    for b in range(2)
                ]
                for q in range(4):
                    real = imag = 0.0
                    for b in range(2):
                        d0 = rows_ref[b * 16 + p : b * 16 + p + 1, q * 128 : (q + 1) * 128]
                        d1 = rows_ref[b * 16 + 8 + p : b * 16 + 9 + p, q * 128 : (q + 1) * 128]
                        real = real + (u[b][0] * d0 + u[b][1] * d1)
                        imag = imag + (u[b][0] * d1 - u[b][1] * d0)
                    lanes = slice(q * 128, (q + 1) * 128)
                    out_ref[start + p, 0, half * 8 : half * 8 + 8, lanes] = real
                    out_ref[start + p, 1, half * 8 : half * 8 + 8, lanes] = imag


def point_kernel(field_ref, dpre_ref, bias_ref, out_ref, acc_ref):
    x = pl.program_id(0)

    @pl.when(x == 0)
    def _():
        acc_ref[...] = jnp.zeros_like(acc_ref)

    acc_ref[...] += dot_nt(y_blocks(field_ref), y_blocks(dpre_ref))

    @pl.when(x == X - 1)
    def _():
        row = lax.broadcasted_iota(jnp.int32, (256, 256), 0) % 16
        column = lax.broadcasted_iota(jnp.int32, (256, 256), 1) % 16
        kept = jnp.where(row == column, acc_ref[...], 0.0)
        left = lax.broadcasted_iota(jnp.int32, (256, 128), 0) // 16
        fold = jnp.where(left == lax.broadcasted_iota(jnp.int32, (256, 128), 1), 1.0, 0.0)
        rows = jnp.concatenate(
            [jnp.sum(kept[i * 16 : (i + 1) * 16], axis=0, keepdims=True) for i in range(16)], axis=0
        )
        out_ref[0:16, :] = jnp.dot(
            rows, fold, preferred_element_type=F32, precision=lax.Precision.HIGHEST
        )
        lane = lax.broadcasted_iota(jnp.int32, (8, 128), 1)
        even = jnp.sum(bias_ref[:, 0:128], axis=1, keepdims=True)
        odd = jnp.sum(bias_ref[:, 128:256], axis=1, keepdims=True)
        out_ref[16:24, :] = jnp.where(lane == 0, even, jnp.where(lane == 1, odd, 0.0))


def whole(shape):
    return pl.BlockSpec(shape, lambda *_: (0,) * len(shape))


def by_plane():
    return pl.BlockSpec((None, C, NY, NZ), lambda x: (x, 0, 0, 0))


def by_plane_given():
    return pl.BlockSpec((None, C, None, NY, NZ), lambda x: (0, 0, x, 0, 0))


SMEM = pl.BlockSpec(memory_space=pltpu.SMEM)
BUFFER = (128, 16, 128)
GROUPED = (SLABS, 2, 16, 128)
PLANES = (X, C, NY, NZ)


def call(kernel, out_shape, grid, in_specs, out_specs, scratch, flops, moved, limit, name):
    return pl.pallas_call(
        kernel,
        out_shape=out_shape,
        grid=grid,
        in_specs=in_specs,
        out_specs=out_specs,
        scratch_shapes=scratch,
        compiler_params=pltpu.CompilerParams(vmem_limit_bytes=limit * MIB),
        cost_estimate=pl.CostEstimate(flops=flops, bytes_accessed=moved, transcendentals=0),
        name=name,
    )


def struct(shape, dtype):
    return jax.ShapeDtypeStruct(shape, dtype)


def exchange(buffer):
    return lax.all_to_all(buffer, BOTH, 0, 0, tiled=True)


def slab_index(x, z, y, c):
    return ((x * 2 + z) * 4 + y) * 2 + c


def total_over_devices(value):
    sizes = (4, 2, 4, 2)
    places = [(x, z, y, c) for x in range(4) for z in range(2) for y in range(4) for c in range(2)]
    for axis, step in ((3, 1), (2, 1), (2, 2), (0, 1), (0, 2), (1, 1)):
        pairs = []
        for place in places:
            other = list(place)
            other[axis] = (other[axis] ^ step) % sizes[axis]
            pairs.append((slab_index(*place), slab_index(*other)))
        value = value + lax.ppermute(value, "slab", pairs)
    return value + lax.ppermute(value, "batch", [(0, 1), (1, 0)])


def body(field, cotangent, spectral_weight, point_weight, point_bias):
    ty, tyt, zb, tx, txi = (jnp.asarray(t) for t in tables())
    which = lax.axis_index("batch").astype(jnp.int32).reshape(1)
    eye = jnp.eye(16, dtype=BF16)
    kron = jnp.kron(point_weight.T, eye)
    kron_back = jnp.kron(point_weight, eye)
    bias_column = jnp.repeat(point_bias, 16).reshape(256, 1)
    zf = pltpu.VMEM((2048, 512), BF16)
    planes = pltpu.VMEM((512, 2048), BF16)
    wide = pltpu.VMEM((2048, 128), F32)
    gather = pltpu.VMEM((512, 512), BF16)
    table_specs = {"ty": whole((64, NY)), "tyt": whole((NY, 64)), "zb": whole((256, 512))}
    big = 8 * MIB

    sent = call(
        field_kernel, struct(BUFFER, BF16), (X,),
        [by_plane_given(), table_specs["ty"], table_specs["zb"]], whole(BUFFER),
        [zf, planes, wide], 2 * 10**9, big, 32, "field_planes",
    )(field, ty, zb)
    got = exchange(sent)
    pre = call(
        pre_kernel, struct(PLANES, BF16), (X,),
        [by_plane_given(), whole((256, 256)), whole((256, 1))], by_plane(),
        [], 2 * 10**9, 2 * big, 32, "point_map",
    )(field, kron, bias_column)
    back, modes_u = call(
        mix_kernel, (struct(GROUPED, BF16), struct((512, 128), F32)), (),
        [SMEM] + [pl.BlockSpec(memory_space=pltpu.VMEM)] * 4,
        (pl.BlockSpec(memory_space=pltpu.VMEM),) * 2,
        [pltpu.VMEM((32, 512), F32)], 10**9, 3 * MIB, 32, "mix_modes",
    )(which, got.reshape(GROUPED), spectral_weight, tx, txi)
    got = exchange(back.reshape(BUFFER))
    other_u = lax.ppermute(modes_u, "batch", [(0, 1), (1, 0)])
    dpre, sent, bias_rows = call(
        signal_kernel,
        (struct(PLANES, BF16), struct(BUFFER, BF16), struct((8, 256), F32)), (X,),
        [whole(BUFFER), by_plane(), by_plane_given(), table_specs["ty"], table_specs["tyt"],
         table_specs["zb"]],
        (by_plane(), whole(BUFFER), whole((8, 256))),
        [zf, planes, wide, gather, planes], 6 * 10**9, 3 * big, 48, "signal",
    )(got, pre, cotangent, ty, tyt, zb)
    got = exchange(sent)
    partial = call(
        point_kernel, struct((24, 128), F32), (X,),
        [by_plane_given(), by_plane(), whole((8, 256))], whole((24, 128)),
        [pltpu.VMEM((256, 256), F32)], 2 * 10**9, 2 * big, 32, "point_gradient",
    )(field, dpre, bias_rows)
    totals = total_over_devices(partial)
    back, rows_d = call(
        adjoint_kernel, (struct(GROUPED, BF16), struct((32, 512), F32)), (),
        [SMEM] + [pl.BlockSpec(memory_space=pltpu.VMEM)] * 4,
        (pl.BlockSpec(memory_space=pltpu.VMEM),) * 2,
        [pltpu.VMEM((512, 128), F32), pltpu.VMEM((512, 128), F32)],
        10**9, 3 * MIB, 32, "adjoint_modes",
    )(which, got.reshape(GROUPED), spectral_weight, tx, txi)
    got = exchange(back.reshape(BUFFER))
    other_d = lax.ppermute(rows_d, "batch", [(0, 1), (1, 0)])
    mapped = call(
        back_kernel, struct(PLANES, BF16), (X,),
        [by_plane(), whole((256, 256))], by_plane(),
        [], 2 * 10**9, 2 * big, 32, "point_map_back",
    )(dpre, kron_back)
    grad_spec = call(
        spec_kernel, struct((16, 2, C, 512), F32), (),
        [SMEM] + [pl.BlockSpec(memory_space=pltpu.VMEM)] * 4,
        pl.BlockSpec(memory_space=pltpu.VMEM),
        [], 10**7, 2 * MIB, 32, "spectral_gradient",
    )(which, modes_u, other_u, rows_d, other_d)
    input_grad = call(
        final_kernel, struct((1, C, X, NY, NZ), BF16), (X,),
        [whole(BUFFER), by_plane(), table_specs["tyt"], table_specs["zb"]], by_plane_given(),
        [zf, wide, gather, planes], 4 * 10**9, 2 * big, 48, "input_gradient",
    )(got, mapped, tyt, zb)
    grad_point = (0.5 * SCALE_P) * totals[:16, :16]
    grad_bias = (0.5 * SCALE_P) * totals[16:24, :2].reshape(16)
    return input_grad, grad_spec, grad_point, grad_bias


def solution(mesh):
    planes = P("batch", None, "slab", None, None)
    return jax.shard_map(
        body,
        mesh=mesh,
        in_specs=(planes, planes, P("slab", None, None, None), P(), P()),
        out_specs=(planes, P("slab", None, None, None), P(), P()),
        check_vma=False,
    )
```

time: 1090 us -> 173 us (0.16)
  waiting for transfers between devices: 796 us -> 24.2 us
  matrix products: 100 us -> 0 us
  blocking collectives: 70.8 us -> 0 us
  Pallas kernels: 0 us -> 62.4 us
  local copies, waits for them, and re-layouts: 85.3 us -> 30.6 us
  starting transfers between devices: 0.21 us -> 51.2 us
  between operations: 14.6 us -> 0.83 us
    reduce_scatter x2 -> x0, waiting for transfers between devices: 702 us -> none  [to_modes(): lax.psum_scatter(partial_value, 'slab', scatter_dimension=4, tiled=True)]
    dot_general x13 -> x0, matrix products: 100 us -> none  [half_einsum(): return jnp.einsum(form, left, right, preferred_element_type=jnp.float32)]
    all_gather x2 -> x0, waiting for transfers between devices: 93.3 us -> none  [to_slabs(): lax.all_gather(spectrum, 'slab', axis=4, tiled=True)]
    psum x1 -> x0, blocking collectives: 70.8 us -> none  [body(): lax.psum((point_local, bias_local), ('slab', 'batch'))]
    pallas_call x0 -> x9, Pallas kernels: none -> 62.4 us  [the longest x1 25.6 us: body(): call(signal_kernel, (struct(PLANES, BF16), struct(BUFFER, BF16), struct((...]
    all_to_all x0 -> x4, starting transfers between devices: none -> 39.4 us  [exchange(): return lax.all_to_all(buffer, BOTH, 0, 0, tiled=True)]
    mul x2 -> x3, local copies, waits for them, and re-layouts: 28.7 us -> 5.02 us  [the longest x1 2.21 us: body(): kron = jnp.kron(point_weight.T, eye)]
    unnamed x23 -> x34, local copies, waits for them, and re-layouts: 1.68 us -> 25.3 us
  transfers between devices with their start and end apart: 5 -> 13, of which waited for: 4 -> 7; matrix products, arithmetic and copies ran while one was open for 5% -> 4% of each run, Pallas kernels for 0% -> 9%
where the time goes in v1:
time: 173 us; the launch traced here: 171 us
  Pallas kernels  62.4 us (36%)
  starting transfers between devices  51.2 us (30%)
  local copies, waits for them, and re-layouts  30.6 us (18%)
  waiting for transfers between devices  24.2 us (14%)
  other arithmetic  2.16 us (1%)
    all_to_all x4, starting transfers between devices, exchange(): return lax.all_to_all(buffer, BOTH, 0, 0, tiled=True)  39.4 us
    pallas_call x1, Pallas kernels, body(): call(signal_kernel, (struct(PLANES, BF16), struct(BUFFER, BF16), struct((...  25.6 us
    unnamed x34, local copies, waits for them, and re-layouts  25.3 us
    all_to_all x4, waiting for transfers between devices, exchange(): return lax.all_to_all(buffer, BOTH, 0, 0, tiled=True)  14.2 us
    pallas_call x1, Pallas kernels, body(): call(final_kernel, struct((1, C, X, NY, NZ), BF16), (X,), [whole(BUFFER),...  12 us
    ppermute x6, waiting for transfers between devices, total_over_devices(): value = value + lax.ppermute(value, 'slab', pairs)  8.98 us
    ppermute x6, starting transfers between devices, total_over_devices(): value = value + lax.ppermute(value, 'slab', pairs)  8.76 us
    pallas_call x1, Pallas kernels, body(): call(field_kernel, struct(BUFFER, BF16), (X,), [by_plane_given(), table_s...  6.16 us
  transfers between devices with their start and end apart: 13, of which 7 were waited for; matrix products, arithmetic and copies ran while one was open for 4% of the time, Pallas kernels for 9%

profile of v1, /device:TPU:1, one launch (start us, length us, event | category | flops | bytes accessed | tf_op | source)
XLA Modules:
  0.0 171.4 jit_solution(14196157746512679273)
XLA Ops:
  0.6 0.0 copy-start
  0.6 3.4 %copy-done = bf16[1,16,8,256,128]{4,3,2,1,0:T(8,128)(2,1)S(1)} copy-done((bf16[1,16,8,256,128]{4,3,2,1,0:T(8,128)(2,1)S(1)}, bf16[1,16,8,256,128]{4,3,2,1,0:T(8,128)(2,1)}, u32[]{:S(2)}) %copy-start) | copy-done | bytes 8388632
  4.0 0.9 copy-done.7
  5.0 0.8 copy-done.10
  5.7 0.0 copy-start.16
  5.7 6.2 %field_planes.1 = bf16[128,16,128]{2,1,0:T(8,128)(2,1)} custom-call(bf16[1,16,8,256,128]{4,3,2,1,0:T(8,128)(2,1)S(1)} %copy-done, bf16[64,256]{1,0:T(8,128)(2,1)S(1)} %copy-done.10, bf16[256,512]{1,0:T(8,128)(2,1)S(1)} %copy-done.7), custom_call_target="tpu_custom_call" | custom-call | flops 2000000000 | bytes 8388608 | tf_op jit(solution)/shard_map/field_planes/pallas_call | solution.py:464
  11.9 11.5 %all-to-all-start = ((bf16[128,16,128]{2,1,0:T(8,128)(2,1)}), bf16[128,16,128]{2,1,0:T(8,128)(2,1)S(1)}, u32[]{:S(2)}, u32[]{:S(2)}) async-start(bf16[128,16,128]{2,1,0:T(8,128)(2,1)} %field_planes.1), calls=%async_computation | async-start | bytes 1048576 | tf_op jit(solution)/shard_map/all_to_all | solution.py:430
  23.4 14.2 %all-to-all-done = bf16[128,16,128]{2,1,0:T(8,128)(2,1)S(1)} async-done(((bf16[128,16,128]{2,1,0:T(8,128)(2,1)}), bf16[128,16,128]{2,1,0:T(8,128)(2,1)S(1)}, u32[]{:S(2)}, u32[]{:S(2)}) %all-to-all-start) | async-done | bytes 524320 | tf_op jit(solution)/shard_map/all_to_all | solution.py:430
  37.6 0.0 copy-done.12
  37.6 0.0 copy-done.13
  37.6 0.0 copy-done.14
  37.6 2.4 %mix_modes.1 = (bf16[64,2,16,128]{3,2,1,0:T(8,128)(2,1)}, f32[512,128]{1,0:T(8,128)S(1)}) custom-call(s32[1]{0:T(128)} %bitcast.which_ref, bf16[64,2,16,128]{3,2,1,0:T(8,128)(2,1)S(1)} %bitcast.11, bf16[16,2,16,512]{3,2,1,0:T(8,128)(2,1)S(1)} %copy-done.12, bf16[512,1024]{1,0:T(8,128)(2,1)S(1)} %copy-done.13, bf16[1024,128]{1,0:T(8,128)(2,1)S(1)} %copy-done.14), custom_call_target="tpu_custom_call" | custom-call | flops 1000000000 | bytes 3145728 | tf_op jit(solution)/shard_map/mix_modes/pallas_call | solution.py:475
  40.0 3.9 %all-to-all-start.1 = ((bf16[128,16,128]{2,1,0:T(8,128)(2,1)}), bf16[128,16,128]{2,1,0:T(8,128)(2,1)S(1)}, u32[]{:S(2)}, u32[]{:S(2)}) async-start(bf16[128,16,128]{2,1,0:T(8,128)(2,1)} %bitcast.2), calls=%async_computation.1 | async-start | bytes 1048576 | tf_op jit(solution)/shard_map/all_to_all | solution.py:430
  43.9 0.0 copy-done.15
  43.9 0.1 copy.15
  44.0 0.0 copy-done.16
  44.0 0.1 broadcast_in_dim.9
  44.1 0.1 reshape_reshape.4.bias_ref
  44.2 1.5 broadcast_multiply_fusion
  45.7 2.2 %mul.56.kron_ref = bf16[256,256]{1,0:T(8,128)(2,1)S(1)} reshape(bf16[16,16,16,16]{3,2,1,0:T(8,128)(2,1)} %get-tuple-element.19) | data formatting | bytes 262144 | tf_op jit(solution)/shard_map/jit(kron)/mul | solution.py:454
  47.9 0.0 copy-start.1
  47.9 3.4 %copy-done.1 = bf16[1,16,8,256,128]{4,3,2,1,0:T(8,128)(2,1)S(1)} copy-done((bf16[1,16,8,256,128]{4,3,2,1,0:T(8,128)(2,1)S(1)}, bf16[1,16,8,256,128]{4,3,2,1,0:T(8,128)(2,1)}, u32[]{:S(2)}) %copy-start.1) | copy-done | bytes 8388632
  51.3 4.3 %point_map.1.pre_ref = bf16[8,16,256,128]{3,2,1,0:T(8,128)(2,1)S(1)} custom-call(bf16[1,16,8,256,128]{4,3,2,1,0:T(8,128)(2,1)S(1)} %copy-done.1, bf16[256,256]{1,0:T(8,128)(2,1)S(1)} %mul.56.kron_ref, f32[256,1]{1,0:T(8,128)S(1)} %reshape_reshape.4.bias_ref), custom_call_target="tpu_custom_call" | custom-call | flops 2000000000 | bytes 16777216 | tf_op jit(solution)/shard_map/point_map/pallas_call | solution.py:470
  55.6 0.0 copy-start.6
  55.6 3.4 %copy-done.6 = bf16[8,16,256,128]{3,2,1,0:T(8,128)(2,1)} copy-done((bf16[8,16,256,128]{3,2,1,0:T(8,128)(2,1)}, bf16[8,16,256,128]{3,2,1,0:T(8,128)(2,1)S(1)}, u32[]{:S(2)}) %copy-start.6) | copy-done | bytes 8388632
  59.0 0.0 all-to-all-done.1.in_ref
  59.0 0.0 copy-done.9
  59.0 0.0 copy-done.11
  59.0 25.6 %signal.1 = (bf16[8,16,256,128]{3,2,1,0:T(8,128)(2,1)}, bf16[128,16,128]{2,1,0:T(8,128)(2,1)}, f32[8,256]{1,0:T(8,128)S(1)}) custom-call(bf16[128,16,128]{2,1,0:T(8,128)(2,1)S(1)} %all-to-all-done.1.in_ref, bf16[8,16,256,128]{3,2,1,0:T(8,128)(2,1)} %copy-done.6, bf16[1,16,8,256,128]{4,3,2,1,0:T(8,128)(2,1)} %cot_ref.1, bf16[64,256]{1,0:T(8,128)(2,1)S(1)} %copy-done.11, ...), custom_call_target="tpu_custom_call" | custom-call | flops 6000000000 | bytes 25165824 | tf_op jit(solution)/shard_map/signal/pallas_call | solution.py:483
  84.7 9.8 %all-to-all-start.2 = ((bf16[128,16,128]{2,1,0:T(8,128)(2,1)}), bf16[128,16,128]{2,1,0:T(8,128)(2,1)S(1)}, u32[]{:S(2)}, u32[]{:S(2)}) async-start(bf16[128,16,128]{2,1,0:T(8,128)(2,1)} %get-tuple-element.12), calls=%async_computation.2 | async-start | bytes 1048576 | tf_op jit(solution)/shard_map/all_to_all | solution.py:430
  94.5 0.0 copy-start.2
  94.5 3.4 %copy-done.2 = bf16[1,16,8,256,128]{4,3,2,1,0:T(8,128)(2,1)S(1)} copy-done((bf16[1,16,8,256,128]{4,3,2,1,0:T(8,128)(2,1)S(1)}, bf16[1,16,8,256,128]{4,3,2,1,0:T(8,128)(2,1)}, u32[]{:S(2)}) %copy-start.2) | copy-done | bytes 8388632
  97.8 3.4 %copy-done.3 = bf16[8,16,256,128]{3,2,1,0:T(8,128)(2,1)S(1)} copy-done((bf16[8,16,256,128]{3,2,1,0:T(8,128)(2,1)S(1)}, bf16[8,16,256,128]{3,2,1,0:T(8,128)(2,1)}, u32[]{:S(2)}) %copy-start.3) | copy-done | bytes 8388632
  101.2 4.7 %point_gradient.1 = f32[24,128]{1,0:T(8,128)S(1)} custom-call(bf16[1,16,8,256,128]{4,3,2,1,0:T(8,128)(2,1)S(1)} %copy-done.2, bf16[8,16,256,128]{3,2,1,0:T(8,128)(2,1)S(1)} %copy-done.3, f32[8,256]{1,0:T(8,128)S(1)} %get-tuple-element.17.bias_ref), custom_call_target="tpu_custom_call" | custom-call | flops 2000000000 | bytes 16777216 | tf_op jit(solution)/shard_map/point_gradient/pallas_call | solution.py:492
  105.9 1.3 collective-permute-start.2
  107.3 0.8 collective-permute-done.2
  108.1 0.5 collective-permute-start.3
  108.6 2.0 %collective-permute-done.3 = f32[24,128]{1,0:T(8,128)S(1)} collective-permute-done((f32[24,128]{1,0:T(8,128)S(1)}, f32[24,128]{1,0:T(8,128)S(1)}, u32[]{:S(2)}, u32[]{:S(2)}) %collective-permute-start.3) | collective-permute-done | bytes 12320 | tf_op jit(solution)/shard_map/ppermute | solution.py:446
  110.6 2.0 %collective-permute-start.4 = (f32[24,128]{1,0:T(8,128)S(1)}, f32[24,128]{1,0:T(8,128)S(1)}, u32[]{:S(2)}, u32[]{:S(2)}) collective-permute-start(f32[24,128]{1,0:T(8,128)S(1)} %add.22), channel_id=1, source_target_pairs={{0,8},{2,10},{4,12},{6,14},{8,0},{10,2},{12,4},{14,6},{16,24},{18,... | collective-permute-start | bytes 36872 | tf_op jit(solution)/shard_map/ppermute | solution.py:446
  112.7 2.0 %collective-permute-done.4 = f32[24,128]{1,0:T(8,128)S(1)} collective-permute-done((f32[24,128]{1,0:T(8,128)S(1)}, f32[24,128]{1,0:T(8,128)S(1)}, u32[]{:S(2)}, u32[]{:S(2)}) %collective-permute-start.4) | collective-permute-done | bytes 12320 | tf_op jit(solution)/shard_map/ppermute | solution.py:446
  114.7 0.5 collective-permute-start.5
  115.2 2.0 %collective-permute-done.5 = f32[24,128]{1,0:T(8,128)S(1)} collective-permute-done((f32[24,128]{1,0:T(8,128)S(1)}, f32[24,128]{1,0:T(8,128)S(1)}, u32[]{:S(2)}, u32[]{:S(2)}) %collective-permute-start.5) | collective-permute-done | bytes 12320 | tf_op jit(solution)/shard_map/ppermute | solution.py:446
  117.2 2.0 %collective-permute-start.6 = (f32[24,128]{1,0:T(8,128)S(1)}, f32[24,128]{1,0:T(8,128)S(1)}, u32[]{:S(2)}, u32[]{:S(2)}) collective-permute-start(f32[24,128]{1,0:T(8,128)S(1)} %add.24), channel_id=1, source_target_pairs={{0,64},{2,66},{4,68},{6,70},{8,72},{10,74},{12,76},{14,78},{16,80}... | collective-permute-start | bytes 36872 | tf_op jit(solution)/shard_map/ppermute | solution.py:446
  119.3 2.0 %collective-permute-done.6 = f32[24,128]{1,0:T(8,128)S(1)} collective-permute-done((f32[24,128]{1,0:T(8,128)S(1)}, f32[24,128]{1,0:T(8,128)S(1)}, u32[]{:S(2)}, u32[]{:S(2)}) %collective-permute-start.6) | collective-permute-done | bytes 12320 | tf_op jit(solution)/shard_map/ppermute | solution.py:446
  121.3 2.4 %collective-permute-start.7 = (f32[24,128]{1,0:T(8,128)S(1)}, f32[24,128]{1,0:T(8,128)S(1)}, u32[]{:S(2)}, u32[]{:S(2)}) collective-permute-start(f32[24,128]{1,0:T(8,128)S(1)} %add.25), channel_id=1, source_target_pairs={{0,16},{2,18},{4,20},{6,22},{8,24},{10,26},{12,28},{14,30},{16,0},... | collective-permute-start | bytes 36872 | tf_op jit(solution)/shard_map/ppermute | solution.py:446
  123.7 2.2 %mul.59.kron_ref = bf16[256,256]{1,0:T(8,128)(2,1)S(1)} reshape(bf16[16,16,16,16]{3,2,1,0:T(8,128)(2,1)} %get-tuple-element.18) | data formatting | bytes 262144 | tf_op jit(solution)/shard_map/jit(kron)/mul | solution.py:455
  125.9 0.6 collective-permute-start
  126.6 0.0 collective-permute-done.7
  126.6 0.9 collective-permute-start.8
  127.5 0.0 all-to-all-done.2
  127.5 2.4 %adjoint_modes.1 = (bf16[64,2,16,128]{3,2,1,0:T(8,128)(2,1)}, f32[32,512]{1,0:T(8,128)S(1)}) custom-call(s32[1]{0:T(128)} %bitcast.which_ref, bf16[64,2,16,128]{3,2,1,0:T(8,128)(2,1)S(1)} %bitcast.10, bf16[16,2,16,512]{3,2,1,0:T(8,128)(2,1)S(1)} %copy-done.12, bf16[512,1024]{1,0:T(8,128)(2,1)S(1)} %copy-done.13, bf16[1024,128]{1,0:T(8,128)(2,1)S(1)} %copy-done.14), custom_call_target="tpu_custom_call" | custom-call | flops 1000000000 | bytes 3145728 | tf_op jit(solution)/shard_map/adjoint_modes/pallas_call | solution.py:498
  129.8 14.2 %all-to-all-start.3 = ((bf16[128,16,128]{2,1,0:T(8,128)(2,1)}), bf16[128,16,128]{2,1,0:T(8,128)(2,1)S(1)}, u32[]{:S(2)}, u32[]{:S(2)}) async-start(bf16[128,16,128]{2,1,0:T(8,128)(2,1)} %bitcast.5), calls=%async_computation.3 | async-start | bytes 1048576 | tf_op jit(solution)/shard_map/all_to_all | solution.py:430
  144.1 3.4 %copy-done.4 = bf16[8,16,256,128]{3,2,1,0:T(8,128)(2,1)S(1)} copy-done((bf16[8,16,256,128]{3,2,1,0:T(8,128)(2,1)S(1)}, bf16[8,16,256,128]{3,2,1,0:T(8,128)(2,1)}, u32[]{:S(2)}) %copy-start.4) | copy-done | bytes 8388632
  147.5 3.6 %point_map_back.1.mapped_ref = bf16[8,16,256,128]{3,2,1,0:T(8,128)(2,1)S(1)} custom-call(bf16[8,16,256,128]{3,2,1,0:T(8,128)(2,1)S(1)} %copy-done.4, bf16[256,256]{1,0:T(8,128)(2,1)S(1)} %mul.59.kron_ref), custom_call_target="tpu_custom_call" | custom-call | flops 2000000000 | bytes 16777216 | tf_op jit(solution)/shard_map/point_map_back/pallas_call | solution.py:507
  151.0 3.3 %copy-done.5 = bf16[8,16,256,128]{3,2,1,0:T(8,128)(2,1)} copy-done((bf16[8,16,256,128]{3,2,1,0:T(8,128)(2,1)}, bf16[8,16,256,128]{3,2,1,0:T(8,128)(2,1)S(1)}, u32[]{:S(2)}) %copy-start.5) | copy-done | bytes 8388632
  154.3 0.0 collective-permute-done.8
  154.3 0.6 slice_multiply_fusion
  154.9 1.5 collective-permute-start.1
  156.4 0.6 mul.63
  157.0 0.0 collective-permute-done.v_ref
  157.0 1.1 collective-permute-done.1.e_ref
  158.1 1.2 spectral_gradient.1
  159.3 0.0 all-to-all-done.3.in_ref
  159.3 12.0 %input_gradient.1 = bf16[1,16,8,256,128]{4,3,2,1,0:T(8,128)(2,1)} custom-call(bf16[128,16,128]{2,1,0:T(8,128)(2,1)S(1)} %all-to-all-done.3.in_ref, bf16[8,16,256,128]{3,2,1,0:T(8,128)(2,1)} %copy-done.5, bf16[256,64]{1,0:T(8,128)(2,1)S(1)} %copy-done.9, bf16[256,512]{1,0:T(8,128)(2,1)S(1)} %copy-done.8), custom_call_target="tpu_custom_call" | custom-call | flops 4000000000 | bytes 16777216 | tf_op jit(solution)/shard_map/input_gradient/pallas_call | solution.py:518
  (22 shorter events, 0.1 us)
Async XLA Ops:
  0.6 3.4 %copy-start = (bf16[1,16,8,256,128]{4,3,2,1,0:T(8,128)(2,1)S(1)}, bf16[1,16,8,256,128]{4,3,2,1,0:T(8,128)(2,1)}, u32[]{:S(2)}) copy-start(bf16[1,16,8,256,128]{4,3,2,1,0:T(8,128)(2,1)} %field_ref.3) | copy-start | bytes 25165828
  4.0 0.9 copy-start.7
  5.0 0.8 copy-start.10
  5.7 31.8 %copy-start.12 = (bf16[16,2,16,512]{3,2,1,0:T(8,128)(2,1)S(1)}, bf16[16,2,16,512]{3,2,1,0:T(8,128)(2,1)}, u32[]{:S(2)}) copy-start(bf16[16,2,16,512]{3,2,1,0:T(8,128)(2,1)} %weight_ref.3) | copy-start | bytes 1572868
  5.7 31.8 %copy-start.13 = (bf16[512,1024]{1,0:T(8,128)(2,1)S(1)}, bf16[512,1024]{1,0:T(8,128)(2,1)}, u32[]{:S(2)}) copy-start(bf16[512,1024]{1,0:T(8,128)(2,1)} %constant.20.clone.tx_ref) | copy-start | bytes 3145732
  5.7 31.8 %copy-start.14 = (bf16[1024,128]{1,0:T(8,128)(2,1)S(1)}, bf16[1024,128]{1,0:T(8,128)(2,1)}, u32[]{:S(2)}) copy-start(bf16[1024,128]{1,0:T(8,128)(2,1)} %constant.21.clone.txi_ref) | copy-start | bytes 786436
  5.7 38.2 %copy-start.15 = (bf16[16,16]{1,0:T(8,128)(2,1)S(1)}, bf16[16,16]{1,0:T(8,128)(2,1)}, u32[]{:S(2)}) copy-start(bf16[16,16]{1,0:T(8,128)(2,1)} %param.13) | copy-start | bytes 1540
  5.7 38.2 %copy-start.16 = (f32[16]{0:T(128)S(1)}, f32[16]{0:T(128)}, u32[]{:S(2)}) copy-start(f32[16]{0:T(128)} %param.14) | copy-start | bytes 196
  11.9 25.7 %all-to-all-start = ((bf16[128,16,128]{2,1,0:T(8,128)(2,1)}), bf16[128,16,128]{2,1,0:T(8,128)(2,1)S(1)}, u32[]{:S(2)}, u32[]{:S(2)}) async-start(bf16[128,16,128]{2,1,0:T(8,128)(2,1)} %field_planes.1), calls=%async_computation | async-start | bytes 1048576 | tf_op jit(solution)/shard_map/all_to_all | solution.py:430
  40.0 19.0 %all-to-all-start.1 = ((bf16[128,16,128]{2,1,0:T(8,128)(2,1)}), bf16[128,16,128]{2,1,0:T(8,128)(2,1)S(1)}, u32[]{:S(2)}, u32[]{:S(2)}) async-start(bf16[128,16,128]{2,1,0:T(8,128)(2,1)} %bitcast.2), calls=%async_computation.1 | async-start | bytes 1048576 | tf_op jit(solution)/shard_map/all_to_all | solution.py:430
  47.9 3.4 %copy-start.1 = (bf16[1,16,8,256,128]{4,3,2,1,0:T(8,128)(2,1)S(1)}, bf16[1,16,8,256,128]{4,3,2,1,0:T(8,128)(2,1)}, u32[]{:S(2)}) copy-start(bf16[1,16,8,256,128]{4,3,2,1,0:T(8,128)(2,1)} %field_ref.3) | copy-start | bytes 25165828
  51.3 7.7 %copy-start.8 = (bf16[256,512]{1,0:T(8,128)(2,1)S(1)}, bf16[256,512]{1,0:T(8,128)(2,1)}, u32[]{:S(2)}) copy-start(bf16[256,512]{1,0:T(8,128)(2,1)} %constant.19.clone.zb_ref) | copy-start | bytes 786436
  51.3 7.7 %copy-start.9 = (bf16[256,64]{1,0:T(8,128)(2,1)S(1)}, bf16[256,64]{1,0:T(8,128)(2,1)}, u32[]{:S(2)}) copy-start(bf16[256,64]{1,0:T(8,128)(2,1)} %constant.18.clone.tyt_ref) | copy-start | bytes 98308
  51.3 7.7 %copy-start.11 = (bf16[64,256]{1,0:T(8,128)(2,1)S(1)}, bf16[64,256]{1,0:T(8,128)(2,1)}, u32[]{:S(2)}) copy-start(bf16[64,256]{1,0:T(8,128)(2,1)} %constant.6.clone.ty_ref) | copy-start | bytes 98308
  55.6 3.4 %copy-start.6 = (bf16[8,16,256,128]{3,2,1,0:T(8,128)(2,1)}, bf16[8,16,256,128]{3,2,1,0:T(8,128)(2,1)S(1)}, u32[]{:S(2)}) copy-start(bf16[8,16,256,128]{3,2,1,0:T(8,128)(2,1)S(1)} %point_map.1.pre_ref) | copy-start | bytes 25165828
  84.7 42.8 %all-to-all-start.2 = ((bf16[128,16,128]{2,1,0:T(8,128)(2,1)}), bf16[128,16,128]{2,1,0:T(8,128)(2,1)S(1)}, u32[]{:S(2)}, u32[]{:S(2)}) async-start(bf16[128,16,128]{2,1,0:T(8,128)(2,1)} %get-tuple-element.12), calls=%async_computation.2 | async-start | bytes 1048576 | tf_op jit(solution)/shard_map/all_to_all | solution.py:430
  94.5 3.4 %copy-start.2 = (bf16[1,16,8,256,128]{4,3,2,1,0:T(8,128)(2,1)S(1)}, bf16[1,16,8,256,128]{4,3,2,1,0:T(8,128)(2,1)}, u32[]{:S(2)}) copy-start(bf16[1,16,8,256,128]{4,3,2,1,0:T(8,128)(2,1)} %field_ref.3) | copy-start | bytes 25165828
  97.8 3.4 %copy-start.3 = (bf16[8,16,256,128]{3,2,1,0:T(8,128)(2,1)S(1)}, bf16[8,16,256,128]{3,2,1,0:T(8,128)(2,1)}, u32[]{:S(2)}) copy-start(bf16[8,16,256,128]{3,2,1,0:T(8,128)(2,1)} %get-tuple-element.14.in_ref.dpre_ref) | copy-start | bytes 25165828
  105.9 2.2 %collective-permute-start.2 = (f32[24,128]{1,0:T(8,128)S(1)}, f32[24,128]{1,0:T(8,128)S(1)}, u32[]{:S(2)}, u32[]{:S(2)}) collective-permute-start(f32[24,128]{1,0:T(8,128)S(1)} %point_gradient.1), channel_id=1, source_target_pairs={{0,2},{2,0},{4,6},{6,4},{8,10},{10,8},{12,14},{14,12},{16,18},{18,... | collective-permute-start | bytes 36872 | tf_op jit(solution)/shard_map/ppermute | solution.py:446
  108.1 2.5 %collective-permute-start.3 = (f32[24,128]{1,0:T(8,128)S(1)}, f32[24,128]{1,0:T(8,128)S(1)}, u32[]{:S(2)}, u32[]{:S(2)}) collective-permute-start(f32[24,128]{1,0:T(8,128)S(1)} %add.21), channel_id=1, source_target_pairs={{0,4},{2,6},{4,0},{6,2},{8,12},{10,14},{12,8},{14,10},{16,20},{18,... | collective-permute-start | bytes 36872 | tf_op jit(solution)/shard_map/ppermute | solution.py:446
  110.6 4.0 %collective-permute-start.4 = (f32[24,128]{1,0:T(8,128)S(1)}, f32[24,128]{1,0:T(8,128)S(1)}, u32[]{:S(2)}, u32[]{:S(2)}) collective-permute-start(f32[24,128]{1,0:T(8,128)S(1)} %add.22), channel_id=1, source_target_pairs={{0,8},{2,10},{4,12},{6,14},{8,0},{10,2},{12,4},{14,6},{16,24},{18,... | collective-permute-start | bytes 36872 | tf_op jit(solution)/shard_map/ppermute | solution.py:446
  114.7 2.5 %collective-permute-start.5 = (f32[24,128]{1,0:T(8,128)S(1)}, f32[24,128]{1,0:T(8,128)S(1)}, u32[]{:S(2)}, u32[]{:S(2)}) collective-permute-start(f32[24,128]{1,0:T(8,128)S(1)} %add.23), channel_id=1, source_target_pairs={{0,32},{2,34},{4,36},{6,38},{8,40},{10,42},{12,44},{14,46},{16,48}... | collective-permute-start | bytes 36872 | tf_op jit(solution)/shard_map/ppermute | solution.py:446
  117.2 4.0 %collective-permute-start.6 = (f32[24,128]{1,0:T(8,128)S(1)}, f32[24,128]{1,0:T(8,128)S(1)}, u32[]{:S(2)}, u32[]{:S(2)}) collective-permute-start(f32[24,128]{1,0:T(8,128)S(1)} %add.24), channel_id=1, source_target_pairs={{0,64},{2,66},{4,68},{6,70},{8,72},{10,74},{12,76},{14,78},{16,80}... | collective-permute-start | bytes 36872 | tf_op jit(solution)/shard_map/ppermute | solution.py:446
  121.3 5.3 %collective-permute-start.7 = (f32[24,128]{1,0:T(8,128)S(1)}, f32[24,128]{1,0:T(8,128)S(1)}, u32[]{:S(2)}, u32[]{:S(2)}) collective-permute-start(f32[24,128]{1,0:T(8,128)S(1)} %add.25), channel_id=1, source_target_pairs={{0,16},{2,18},{4,20},{6,22},{8,24},{10,26},{12,28},{14,30},{16,0},... | collective-permute-start | bytes 36872 | tf_op jit(solution)/shard_map/ppermute | solution.py:446
  125.9 31.1 %collective-permute-start = (f32[512,128]{1,0:T(8,128)S(1)}, f32[512,128]{1,0:T(8,128)S(1)}, u32[]{:S(2)}, u32[]{:S(2)}) collective-permute-start(f32[512,128]{1,0:T(8,128)S(1)} %get-tuple-element.15.u_ref), channel_id=1, source_target_pairs={{0,1},{1,0},{2,3},{3,2},{4,5},{5,4},{6,7},{7,6},{8,9},{9,8},{10,11... | collective-permute-start | bytes 786440 | tf_op jit(solution)/shard_map/ppermute | solution.py:482
  126.6 27.8 %collective-permute-start.8 = (f32[24,128]{1,0:T(8,128)S(1)}, f32[24,128]{1,0:T(8,128)S(1)}, u32[]{:S(2)}, u32[]{:S(2)}) collective-permute-start(f32[24,128]{1,0:T(8,128)S(1)} %add.26), channel_id=1, source_target_pairs={{0,1},{1,0},{2,3},{3,2},{4,5},{5,4},{6,7},{7,6},{8,9},{9,8},{10,11... | collective-permute-start | bytes 36872 | tf_op jit(solution)/shard_map/ppermute | solution.py:447
  129.8 29.5 %all-to-all-start.3 = ((bf16[128,16,128]{2,1,0:T(8,128)(2,1)}), bf16[128,16,128]{2,1,0:T(8,128)(2,1)S(1)}, u32[]{:S(2)}, u32[]{:S(2)}) async-start(bf16[128,16,128]{2,1,0:T(8,128)(2,1)} %bitcast.5), calls=%async_computation.3 | async-start | bytes 1048576 | tf_op jit(solution)/shard_map/all_to_all | solution.py:430
  144.1 3.4 %copy-start.4 = (bf16[8,16,256,128]{3,2,1,0:T(8,128)(2,1)S(1)}, bf16[8,16,256,128]{3,2,1,0:T(8,128)(2,1)}, u32[]{:S(2)}) copy-start(bf16[8,16,256,128]{3,2,1,0:T(8,128)(2,1)} %get-tuple-element.14.in_ref.dpre_ref) | copy-start | bytes 25165828
  151.0 3.3 %copy-start.5 = (bf16[8,16,256,128]{3,2,1,0:T(8,128)(2,1)}, bf16[8,16,256,128]{3,2,1,0:T(8,128)(2,1)S(1)}, u32[]{:S(2)}) copy-start(bf16[8,16,256,128]{3,2,1,0:T(8,128)(2,1)S(1)} %point_map_back.1.mapped_ref) | copy-start | bytes 25165828
  154.9 3.2 %collective-permute-start.1 = (f32[32,512]{1,0:T(8,128)S(1)}, f32[32,512]{1,0:T(8,128)S(1)}, u32[]{:S(2)}, u32[]{:S(2)}) collective-permute-start(f32[32,512]{1,0:T(8,128)S(1)} %get-tuple-element.16.d_ref), channel_id=1, source_target_pairs={{0,1},{1,0},{2,3},{3,2},{4,5},{5,4},{6,7},{7,6},{8,9},{9,8},{10,11... | collective-permute-start | bytes 196616 | tf_op jit(solution)/shard_map/ppermute | solution.py:506

commit v2 on v1

v2 whole, which is shorter than its diff:
```python
import math

import jax
import jax.numpy as jnp
import numpy as np
from jax import lax
from jax.experimental import pallas as pl
from jax.experimental.pallas import tpu as pltpu
from jax.sharding import PartitionSpec as P

C = 16
X = 8
NY = 256
NZ = 128
NX = 512
MODES = 32
SLABS = 64
CELLS = NX * NY * NZ
SCALE_F = 1.0 / math.sqrt(CELLS)
SCALE_I = 1.0 / math.sqrt(MODES**3)
SCALE_P = 1.0 / math.sqrt(2 * CELLS)
SCALE_W = math.sqrt(MODES**3 / (2 * CELLS))
GELU_A = math.sqrt(2.0 / math.pi)
GK = (GELU_A * 0.044715) ** (1.0 / 3.0)
GA = GELU_A / GK
BOTH = ("slab", "batch")
F32 = jnp.float32
BF16 = jnp.bfloat16
MIB = 1 << 20
LIMIT = 48
CUT = 2


def freqs(number, length):
    index = np.arange(number)
    return np.where(index < number // 2, index, index + length - number)


def angles(length, frequencies):
    product = (np.arange(length)[:, None] * frequencies[None, :]) % length
    return product * (2.0 * math.pi / length)


def tables():
    thy = angles(NY, freqs(MODES, NY))
    thz = angles(NZ, np.arange(MODES))
    thx = angles(NX, freqs(MODES, NX))
    ty = np.concatenate([np.cos(thy).T, -np.sin(thy).T], axis=0)
    cos, sin = np.cos(thz), np.sin(thz)
    rot = np.zeros((2, NZ, 2, MODES))
    rot[0, :, 0], rot[1, :, 0] = cos, sin
    rot[1, :, 1], rot[0, :, 1] = cos, -sin
    zb = rot.reshape(2, NZ, 2, 2, 2, 8).transpose(0, 1, 3, 2, 4, 5)
    zb = np.stack([zb, zb[:, :, :, :, ::-1]], axis=2)[:, :, :, :, :, :, None, :]
    zb = np.broadcast_to(zb, (2, NZ, 2, 2, 2, 2, 4, 8)).reshape(2 * NZ, 512)
    cs = np.stack([np.cos(thx), np.sin(thx)]).reshape(2, SLABS, X, MODES)
    tx = np.zeros((2, 2, 4, MODES, SLABS, 2, X))
    txi = np.zeros((SLABS, 2, X, 2, 2, MODES))
    for half in range(2):
        tx[half, :, :, :, :, half] = cs.transpose(0, 3, 1, 2)[:, None]
        txi[:, half, :, half] = cs.transpose(1, 2, 0, 3)
    return tuple(
        np.asarray(t, np.float32).astype(BF16)
        for t in (ty, ty.T, zb, tx.reshape(512, 1024), txi.reshape(1024, 128))
    )


def dot(left, right):
    return jnp.dot(left, right, preferred_element_type=F32)


def dot_nt(left, right):
    return lax.dot_general(left, right, (((1,), (1,)), ((), ())), preferred_element_type=F32)


def build_z(zb_ref, zf_ref):
    channel = (lax.broadcasted_iota(jnp.int32, (2 * NZ, 256), 1) // 8) % 4
    for group in range(2):
        table = zb_ref[:, group * 256 : (group + 1) * 256].astype(F32)
        for c in range(4):
            row = group * 1024 + c * 256
            zf_ref[row : row + 256, :] = jnp.where(channel == c, table, 0.0).astype(BF16)


def low_lanes(rows):
    return lax.broadcasted_iota(jnp.int32, (rows, 128), 1) % 64 < 32


def z_forward(planes_ref, zf_ref, wide_ref, out_ref):
    low = low_lanes(256)
    for half in range(2):
        first, second = (
            dot(
                planes_ref[half * 256 : (half + 1) * 256, group * 1024 : (group + 1) * 1024],
                zf_ref[group * 1024 : (group + 1) * 1024, :],
            )
            for group in range(2)
        )
        for t in range(2):
            one, two = first[:, t * 128 : (t + 1) * 128], second[:, t * 128 : (t + 1) * 128]
            for j, value in enumerate((jnp.where(low, one, two), jnp.where(low, two, one))):
                for x in range(X):
                    wide_ref[pl.ds((2 * t + j) * 16 + half * 8 + x, 32, stride=64), :] = value[
                        x * 32 : (x + 1) * 32
                    ]
    out_ref[...] = wide_ref[...].astype(BF16).reshape(128, 16, 128)


def z_inverse(in_ref, zf_ref, wide_ref, gather_ref, rolled_ref):
    rows = in_ref.shape[1]
    wide_ref[...] = in_ref[...].astype(F32).reshape(128 * rows, 128)
    low = low_lanes(32)
    for half in range(2):
        for x in range(X):
            row = (half * 8 + x) * 32
            for t in range(2):
                even, odd = (
                    wide_ref[pl.ds((2 * t + j) * rows + half * 8 + x, 32, stride=4 * rows), :]
                    for j in range(2)
                )
                for group, value in enumerate((jnp.where(low, even, odd), jnp.where(low, odd, even))):
                    column = group * 256 + t * 128
                    gather_ref[row : row + 32, column : column + 128] = value.astype(BF16)
    for c in range(8):
        group = c // 4
        rolled_ref[:, c * 256 : (c + 1) * 256] = dot_nt(
            gather_ref[:, group * 256 : (group + 1) * 256], zf_ref[c * 256 : (c + 1) * 256, :]
        ).astype(BF16)


def y_forward(ty_ref, pair, planes_ref, x, op):
    result = dot(ty_ref[...], pair)
    half, first = op // 4, (op % 4) * 2
    rows = pl.ds(pl.multiple_of(half * 256 + x * 32, 32), 32)
    for j in range(2):
        for part in range(2):
            column = (first + j) * 256 + part * 128
            planes_ref[rows, column : column + 128] = result[
                part * 32 : (part + 1) * 32, j * 128 : (j + 1) * 128
            ].astype(BF16)
    return result


def y_inverse(tyt_ref, rolled_ref, x, op):
    half, first = op // 4, (op % 4) * 2
    rows = pl.ds(pl.multiple_of(half * 256 + x * 32, 32), 32)
    blocks = []
    for j in range(2):
        column = (first + j) * 256
        blocks.append(
            jnp.concatenate(
                [
                    rolled_ref[rows, column : column + 128],
                    rolled_ref[rows, column + 128 : column + 256],
                ],
                axis=0,
            )
        )
    return dot(tyt_ref[...], jnp.concatenate(blocks, axis=1))


class Planes:
    def __init__(self, hbm_ref, vmem_ref, sem, given, out=False):
        self.hbm_ref, self.vmem_ref, self.sem, self.given, self.out = hbm_ref, vmem_ref, sem, given, out

    def copy(self, x, channels):
        far = self.hbm_ref.at[0, channels, x] if self.given else self.hbm_ref.at[x, channels]
        near = self.vmem_ref.at[x, channels]
        source, target = (near, far) if self.out else (far, near)
        return pltpu.make_async_copy(source, target, self.sem.at[x])

    def start(self, x):
        for c in range(0, C, CUT):
            self.copy(x, pl.ds(c, CUT)).start()

    def wait(self, x):
        self.copy(x, pl.ds(0, C)).wait()


def field_kernel(
    field_hbm, ty_hbm, zb_hbm, out_ref,
    zf_ref, planes_ref, wide_ref, field_ref, ty_ref, zb_ref, sem, ty_sem, zb_sem,
):
    load = Planes(field_hbm, field_ref, sem, True)
    load_ty = pltpu.make_async_copy(ty_hbm, ty_ref, ty_sem)
    load_zb = pltpu.make_async_copy(zb_hbm, zb_ref, zb_sem)
    load_ty.start()
    load.start(0)
    load_zb.start()
    for x in range(1, X):
        load.start(x)
    load_ty.wait()
    load_zb.wait()
    build_z(zb_ref, zf_ref)

    def step(x, _):
        load.wait(x)
        for op in range(8):
            pair = jnp.concatenate([field_ref[x, 2 * op], field_ref[x, 2 * op + 1]], axis=1)
            y_forward(ty_ref, pair, planes_ref, x, op)
        return 0

    lax.fori_loop(0, X, step, 0)
    z_forward(planes_ref, zf_ref, wide_ref, out_ref)


def y_blocks(ref, x):
    return jnp.concatenate(
        [ref[x, :, b * 16 : (b + 1) * 16, :].reshape(256, 128) for b in range(16)], axis=1
    )


def owner_rows():
    group = lax.broadcasted_iota(jnp.int32, (256, 16), 0) // 16
    return jnp.where(group == lax.broadcasted_iota(jnp.int32, (256, 16), 1), 1.0, 0.0)


def same_row(value):
    row = lax.broadcasted_iota(jnp.int32, (256, 256), 0) % 16
    column = lax.broadcasted_iota(jnp.int32, (256, 256), 1) % 16
    return jnp.where(row == column, value, 0.0)


def map_planes(scale, in_hbm, map_rows, bias, out_hbm, in_ref, out_ref, in_sem, out_sem):
    load = Planes(in_hbm, in_ref, in_sem, len(in_hbm.shape) == 5)
    store = Planes(out_hbm, out_ref, out_sem, False, True)
    for x in range(X):
        load.start(x)
    kron = same_row(dot_nt(map_rows.astype(BF16), owner_rows().astype(BF16))).astype(BF16)

    def step(x, _):
        load.wait(x)
        for b in range(8):
            pair = jnp.concatenate(
                [in_ref[x, :, y : y + 16, :].reshape(256, 128) for y in (b * 32, b * 32 + 16)],
                axis=1,
            )
            result = dot(kron, pair)
            if bias is not None:
                result = result + bias
            result = (result * scale).astype(BF16)
            for j in range(2):
                y = b * 32 + j * 16
                out_ref[x, :, y : y + 16, :] = result[:, j * 128 : (j + 1) * 128].reshape(C, 16, 128)
        store.start(x)
        return 0

    lax.fori_loop(0, X, step, 0)
    for x in range(X):
        store.wait(x)


def pre_kernel(in_hbm, weight_ref, bias_ref, out_hbm, in_ref, out_ref, in_sem, out_sem):
    map_rows = dot_nt(owner_rows().astype(BF16), weight_ref[...])
    bias = jnp.sum(owner_rows() * bias_ref[...], axis=1, keepdims=True)
    map_planes(GK, in_hbm, map_rows, bias, out_hbm, in_ref, out_ref, in_sem, out_sem)


def back_kernel(in_hbm, weight_ref, out_hbm, in_ref, out_ref, in_sem, out_sem):
    map_rows = dot(owner_rows().astype(BF16), weight_ref[...])
    map_planes(0.5, in_hbm, map_rows, None, out_hbm, in_ref, out_ref, in_sem, out_sem)


def slope_of(h):
    one, add = BF16(1.0), BF16(GA)
    square = h * h
    t = jnp.tanh(h * (square + add))
    slope = h * (square * BF16(3.0) + add)
    return (one + t) * (one + (one - t) * slope)


def signal_kernel(
    in_ref, pre_hbm, cot_hbm, ty_ref, tyt_ref, zb_ref,
    dpre_hbm, out_ref, bias_ref,
    zf_ref, planes_ref, wide_ref, gather_ref, rolled_ref, pre_ref, cot_ref,
    pre_sem, cot_sem, out_sem,
):
    load_pre = Planes(pre_hbm, pre_ref, pre_sem, False)
    load_cot = Planes(cot_hbm, cot_ref, cot_sem, True)
    store = Planes(dpre_hbm, cot_ref, out_sem, False, True)
    for x in range(X):
        load_pre.start(x)
        load_cot.start(x)
    build_z(zb_ref, zf_ref)
    z_inverse(in_ref, zf_ref, wide_ref, gather_ref, rolled_ref)
    bias_ref[...] = jnp.zeros_like(bias_ref)

    def step(x, _):
        load_pre.wait(x)
        load_cot.wait(x)
        for op in range(8):
            back = y_inverse(tyt_ref, rolled_ref, x, op)
            for j in range(2):
                o = 2 * op + j
                h = back[:, j * 128 : (j + 1) * 128].astype(BF16) + pre_ref[x, o]
                cot_ref[x, o] = slope_of(h) * cot_ref[x, o]
        store.start(x)
        for op in range(8):
            pair = jnp.concatenate([cot_ref[x, 2 * op], cot_ref[x, 2 * op + 1]], axis=1)
            result = y_forward(ty_ref, pair, planes_ref, x, op)
            bias_ref[op : op + 1, :] += result[0:1, :]
        return 0

    lax.fori_loop(0, X, step, 0)
    z_forward(planes_ref, zf_ref, wide_ref, out_ref)
    for x in range(X):
        store.wait(x)


def final_kernel(
    in_ref, mapped_hbm, tyt_ref, zb_ref, out_hbm, point_ref, bias_ref,
    zf_ref, wide_ref, gather_ref, rolled_ref, mapped_ref, out_ref, in_sem, out_sem,
):
    load = Planes(mapped_hbm, mapped_ref, in_sem, False)
    store = Planes(out_hbm, out_ref, out_sem, True, True)
    for x in range(X):
        load.start(x)
    build_z(zb_ref, zf_ref)
    z_inverse(in_ref, zf_ref, wide_ref, gather_ref, rolled_ref)

    def step(x, _):
        load.wait(x)
        for op in range(8):
            back = y_inverse(tyt_ref, rolled_ref, x, op)
            for j in range(2):
                o = 2 * op + j
                mapped = mapped_ref[x, o].astype(F32)
                out_ref[x, o] = (back[:, j * 128 : (j + 1) * 128] + mapped).astype(BF16)
        store.start(x)
        return 0

    lax.fori_loop(0, X, step, 0)
    total = jnp.sum(wide_ref[...].reshape(128, 24, 128)[:, 16:24, :], axis=0) * (0.5 * SCALE_P)
    lane = lax.broadcasted_iota(jnp.int32, (16, 128), 1)
    row = lax.broadcasted_iota(jnp.int32, (16, 128), 0)
    point = jnp.where(row < 8, total[0:1] + total[2:3], total[1:2] + total[3:4])
    point = jnp.where(lane // 16 == row % 8, point, 0.0)
    bias = jnp.where(lane < 32, total[4:5], 0.0)
    fold = lax.broadcasted_iota(jnp.int32, (128, 16), 0) % 16
    fold = jnp.where(fold == lax.broadcasted_iota(jnp.int32, (128, 16), 1), 1.0, 0.0)
    exact = lax.Precision.HIGHEST
    point_ref[...] = jnp.dot(point, fold, preferred_element_type=F32, precision=exact)
    bias_ref[...] = jnp.dot(bias, fold, preferred_element_type=F32, precision=exact)[0:1]
    for x in range(X):
        store.wait(x)


def swapped(which, w):
    return which + w * (1 - 2 * which)


def x_forward(which, in_ref, tx_ref, scale, modes_ref):
    data = jnp.concatenate([in_ref[:, b].reshape(1024, 128) for b in range(2)], axis=1)
    raw = dot(tx_ref[...], data)
    lane = lax.broadcasted_iota(jnp.int32, (128, 128), 1)
    sign = jnp.where(lane < 64, scale, -scale)
    for half in range(2):
        for b in range(2):
            cosine = raw[half * 256 : half * 256 + 128, b * 128 : (b + 1) * 128]
            sine = raw[half * 256 + 128 : half * 256 + 256, b * 128 : (b + 1) * 128]
            modes = cosine * scale + pltpu.roll(sine, 64, 1) * sign
            turned = modes.T
            for s in range(2):
                for w in range(2):
                    row = (half * 2 + b) * 128 + s * 64 + swapped(which, w) * 32
                    place = s * 64 + w * 32
                    modes_ref[pl.ds(pl.multiple_of(row, 32), 32), :] = turned[place : place + 32]


def x_inverse(mixed, txi_ref, out_ref, extra):
    lane = lax.broadcasted_iota(jnp.int32, (32, 128), 1)
    rows = []
    for half in range(2):
        turned = [mixed(half, b).T[:32] for b in range(2)]
        rows.append(jnp.concatenate(turned, axis=1))
        rows.append(
            jnp.concatenate(
                [jnp.where(lane < 64, -1.0, 1.0) * pltpu.roll(g, 64, 1) for g in turned], axis=1
            )
        )
    result = dot(txi_ref[...], jnp.concatenate(rows, axis=0).astype(BF16))
    for b in range(2):
        block = result[:, b * 128 : (b + 1) * 128].reshape(SLABS, 16, 128)
        if extra is not None:
            block = jnp.concatenate(
                [block, jnp.broadcast_to(extra[None], (SLABS, 8, 128))], axis=1
            )
        out_ref[:, b] = block.astype(BF16)


def mix_kernel(which_ref, in_ref, weight_ref, tx_ref, txi_ref, out_ref, modes_ref, mixed_ref):
    which = which_ref[0]
    x_forward(which, in_ref, tx_ref, SCALE_F, modes_ref)
    first = which * 8
    for p in range(8):
        real = weight_ref[first + p, 0].astype(F32)
        imag = weight_ref[first + p, 1].astype(F32)
        for b in range(2):
            u = [
                [modes_ref[pl.ds((half * 2 + b) * 128 + s * 64 + p, 8, stride=8), :] for s in range(2)]
                for half in range(2)
            ]
            for q in range(4):
                total = [0.0, 0.0]
                for half in range(2):
                    w0 = real[half * 8 : half * 8 + 8, q * 128 : (q + 1) * 128]
                    w1 = imag[half * 8 : half * 8 + 8, q * 128 : (q + 1) * 128]
                    u0, u1 = u[half]
                    total[0] = total[0] + (u0 * w0 - u1 * w1)
                    total[1] = total[1] + (u0 * w1 + u1 * w0)
                for s in range(2):
                    row = (b * 2 + s) * 8 + p
                    mixed_ref[row : row + 1, q * 128 : (q + 1) * 128] = jnp.sum(
                        total[s], axis=0, keepdims=True
                    ) * (SCALE_I * GK)

    def mixed(half, b):
        pieces = []
        for s in range(2):
            row = (b * 2 + s) * 8
            for w in range(2):
                column = pl.multiple_of((half * 2 + swapped(which, w)) * 128, 128)
                piece = mixed_ref[row : row + 8, pl.ds(column, 128)]
                for r in range(4):
                    pieces.append(pltpu.roll(piece, 128 - 32 * r, 1) if r else piece)
        return jnp.concatenate(pieces, axis=0)

    x_inverse(mixed, txi_ref, out_ref, None)


def adjoint_kernel(
    which_ref, in_ref, weight_ref, tx_ref, txi_ref, extra_ref,
    out_ref, rows_ref, modes_ref, mixed_ref,
):
    which = which_ref[0]
    x_forward(which, in_ref, tx_ref, 0.5 * SCALE_I, modes_ref)
    group = lax.broadcasted_iota(jnp.int32, (8, 128), 1) // 32
    for b in range(2):
        for s in range(2):
            for q in range(4):
                half, c = q // 2, (q % 2) * 4
                row = (half * 2 + b) * 128 + s * 64 + c * 8
                value = modes_ref[row : row + 8, :]
                for r in range(1, 4):
                    value = jnp.where(group == r, modes_ref[row + 8 * r : row + 8 * r + 8, :], value)
                row = (b * 2 + s) * 8
                rows_ref[row : row + 8, q * 128 : (q + 1) * 128] = value
    first = which * 8
    for p in range(8):
        real = weight_ref[first + p, 0].astype(F32)
        imag = weight_ref[first + p, 1].astype(F32)
        for b in range(2):
            d0 = rows_ref[b * 16 + p : b * 16 + p + 1, :]
            d1 = rows_ref[b * 16 + 8 + p : b * 16 + 8 + p + 1, :]
            total0 = real * d0 + imag * d1
            total1 = real * d1 - imag * d0
            for s, total in enumerate((total0, total1)):
                folded = sum(total[:, q * 128 : (q + 1) * 128] for q in range(4))
                folded = folded + pltpu.roll(folded, 64, 1)
                folded = folded + pltpu.roll(folded, 32, 1)
                for half in range(2):
                    mixed_ref[pl.ds((half * 2 + b) * 128 + s * 64 + p, 8, stride=8), :] = (
                        folded[half * 8 : half * 8 + 8] * SCALE_F
                    )

    def mixed(half, b):
        pieces = []
        for s in range(2):
            for w in range(2):
                row = (half * 2 + b) * 128 + s * 64 + swapped(which, w) * 32
                pieces.append(mixed_ref[pl.ds(pl.multiple_of(row, 32), 32), :])
        return jnp.concatenate(pieces, axis=0)

    x_inverse(mixed, txi_ref, out_ref, extra_ref[...])


def spec_kernel(which_ref, u_ref, v_bf_ref, d_ref, e_bf_ref, out_ref, v_ref, e_ref):
    v_ref[...] = v_bf_ref[...].astype(F32)
    e_ref[...] = e_bf_ref[...].astype(F32)
    mine = which_ref[0] * 8
    other = 8 - mine
    for start, modes_ref, rows_ref in ((mine, u_ref, d_ref), (other, v_ref, e_ref)):
        for p in range(8):
            for half in range(2):
                u = [
                    [
                        modes_ref[pl.ds((half * 2 + b) * 128 + s * 64 + p, 8, stride=8), :] * SCALE_W
                        for s in range(2)
                    ]
                    for b in range(2)
                ]
                for q in range(4):
                    real = imag = 0.0
                    for b in range(2):
                        d0 = rows_ref[b * 16 + p : b * 16 + p + 1, q * 128 : (q + 1) * 128]
                        d1 = rows_ref[b * 16 + 8 + p : b * 16 + 9 + p, q * 128 : (q + 1) * 128]
                        real = real + (u[b][0] * d0 + u[b][1] * d1)
                        imag = imag + (u[b][0] * d1 - u[b][1] * d0)
                    lanes = slice(q * 128, (q + 1) * 128)
                    out_ref[start + p, 0, half * 8 : half * 8 + 8, lanes] = real
                    out_ref[start + p, 1, half * 8 : half * 8 + 8, lanes] = imag


def point_kernel(
    field_hbm, dpre_hbm, bias_ref, out_ref, acc_ref, field_ref, dpre_ref, field_sem, dpre_sem
):
    load_field = Planes(field_hbm, field_ref, field_sem, True)
    load_dpre = Planes(dpre_hbm, dpre_ref, dpre_sem, False)
    for x in range(X):
        load_field.start(x)
        load_dpre.start(x)
    acc_ref[...] = jnp.zeros_like(acc_ref)

    def step(x, _):
        load_field.wait(x)
        load_dpre.wait(x)
        acc_ref[...] += dot_nt(y_blocks(field_ref, x), y_blocks(dpre_ref, x))
        return 0

    lax.fori_loop(0, X, step, 0)
    kept = same_row(acc_ref[...])
    rows = jnp.concatenate(
        [jnp.sum(kept[i * 16 : (i + 1) * 16], axis=0, keepdims=True) for i in range(16)], axis=0
    )
    owner = lax.broadcasted_iota(jnp.int32, (256, 128), 0) // 16
    column = lax.broadcasted_iota(jnp.int32, (256, 128), 1) % 16
    point = jnp.dot(
        rows,
        jnp.where(owner == column, 1.0, 0.0),
        preferred_element_type=F32,
        precision=lax.Precision.HIGHEST,
    )
    lane = lax.broadcasted_iota(jnp.int32, (8, 128), 1)
    row = lax.broadcasted_iota(jnp.int32, (8, 128), 0)
    first, second = (
        jnp.sum(jnp.where(lane // 16 == row, point[h * 8 : h * 8 + 8], 0.0), axis=0, keepdims=True)
        for h in range(2)
    )
    even = jnp.sum(bias_ref[:, 0:128], axis=1, keepdims=True)
    odd = jnp.sum(bias_ref[:, 128:256], axis=1, keepdims=True)
    bias = jnp.where(lane == 2 * row, even, jnp.where(lane == 2 * row + 1, odd, 0.0))
    bias = jnp.sum(bias, axis=0, keepdims=True)
    value = jnp.where(
        (row == 0) | (row == 2), first, jnp.where((row == 1) | (row == 3), second, 0.0)
    )
    value = jnp.where(row == 4, bias, value)
    high = value.astype(BF16).astype(F32)
    low = value - high
    packed = jnp.where(row < 2, high, jnp.where(row < 4, low, 0.0))
    packed = jnp.where((row == 4) & (lane < 16), high, packed)
    out_ref[...] = jnp.where((row == 4) & (lane >= 16), pltpu.roll(low, 16, 1), packed)


SMEM = pl.BlockSpec(memory_space=pltpu.SMEM)
VMEM = pl.BlockSpec(memory_space=pltpu.VMEM)
HBM = pl.BlockSpec(memory_space=pltpu.HBM)
BUFFER = (128, 16, 128)
PLANES = (X, C, NY, NZ)
GIVEN = (1, C, X, NY, NZ)


def struct(shape, dtype):
    return jax.ShapeDtypeStruct(shape, dtype)


def call(kernel, out_shape, in_specs, out_specs, scratch, flops, moved, limit, name):
    return pl.pallas_call(
        kernel,
        out_shape=out_shape,
        in_specs=in_specs,
        out_specs=out_specs,
        scratch_shapes=scratch,
        compiler_params=pltpu.CompilerParams(vmem_limit_bytes=limit * MIB),
        cost_estimate=pl.CostEstimate(flops=flops, bytes_accessed=moved, transcendentals=0),
        name=name,
    )


def exchange(buffer):
    return lax.all_to_all(buffer, BOTH, 0, 0, tiled=True)


def grouped(buffer):
    return buffer.reshape((SLABS, 2) + buffer.shape[1:])


def flat(buffer):
    return buffer.reshape((128,) + buffer.shape[2:])


def body(field, cotangent, spectral_weight, point_weight, point_bias):
    ty, tyt, zb, tx, txi = (jnp.asarray(t) for t in tables())
    which = lax.axis_index("batch").astype(jnp.int32).reshape(1)
    zf = pltpu.VMEM((2048, 256), BF16)
    planes = pltpu.VMEM((512, 2048), BF16)
    wide = pltpu.VMEM((2048, 128), F32)
    gather = pltpu.VMEM((512, 512), BF16)
    held = pltpu.VMEM(PLANES, BF16)
    sems = pltpu.SemaphoreType.DMA((X,))
    big = 8 * MIB
    swap = [(0, 1), (1, 0)]

    sent = call(
        field_kernel, struct(BUFFER, BF16), [HBM, HBM, HBM], VMEM,
        [zf, planes, wide, held, pltpu.VMEM((64, NY), BF16), pltpu.VMEM((256, 512), BF16), sems,
         pltpu.SemaphoreType.DMA, pltpu.SemaphoreType.DMA], 2 * 10**9, big, 60, "field_planes",
    )(field, ty, zb)
    got = exchange(sent)
    pre = call(
        pre_kernel, struct(PLANES, BF16), [HBM, VMEM, VMEM], HBM,
        [held, held, sems, sems], 2 * 10**9, 2 * big, LIMIT, "point_map",
    )(field, point_weight, point_bias.reshape(1, C))
    got, pre = lax.optimization_barrier((got, pre))
    back, modes_u = call(
        mix_kernel, (struct((SLABS, 2, 16, 128), BF16), struct((512, 128), F32)),
        [SMEM] + [VMEM] * 4, (VMEM, VMEM),
        [pltpu.VMEM((32, 512), F32)], 10**9, 3 * MIB, 32, "mix_modes",
    )(which, grouped(got), spectral_weight, tx, txi)
    got = exchange(flat(back))
    other_u = lax.ppermute(modes_u.astype(BF16), "batch", swap)
    got, other_u = lax.optimization_barrier((got, other_u))
    dpre, sent, bias_rows = call(
        signal_kernel,
        (struct(PLANES, BF16), struct(BUFFER, BF16), struct((8, 256), F32)),
        [VMEM, HBM, HBM, VMEM, VMEM, VMEM], (HBM, VMEM, VMEM),
        [zf, planes, wide, gather, planes, held, held, sems, sems, sems],
        6 * 10**9, 3 * big, LIMIT, "signal",
    )(got, pre, cotangent, ty, tyt, zb)
    got = exchange(sent)
    extra = call(
        point_kernel, struct((8, 128), F32), [HBM, HBM, VMEM], VMEM,
        [pltpu.VMEM((256, 256), F32), held, held, sems, sems],
        2 * 10**9, 2 * big, LIMIT, "point_gradient",
    )(field, dpre, bias_rows)
    back, rows_d = call(
        adjoint_kernel, (struct((SLABS, 2, 24, 128), BF16), struct((32, 512), F32)),
        [SMEM] + [VMEM] * 5, (VMEM, VMEM),
        [pltpu.VMEM((512, 128), F32), pltpu.VMEM((512, 128), F32)],
        10**9, 3 * MIB, 32, "adjoint_modes",
    )(which, grouped(got), spectral_weight, tx, txi, extra)
    dpre, rows_d = lax.optimization_barrier((dpre, rows_d))
    got = exchange(flat(back))
    other_d = lax.ppermute(rows_d.astype(BF16), "batch", swap)
    mapped = call(
        back_kernel, struct(PLANES, BF16), [HBM, VMEM], HBM,
        [held, held, sems, sems], 2 * 10**9, 2 * big, LIMIT, "point_map_back",
    )(dpre, point_weight)
    grad_spec = call(
        spec_kernel, struct((16, 2, C, 512), F32), [SMEM] + [VMEM] * 4, VMEM,
        [pltpu.VMEM((512, 128), F32), pltpu.VMEM((32, 512), F32)],
        10**7, 2 * MIB, 32, "spectral_gradient",
    )(which, modes_u, other_u, rows_d, other_d)
    input_grad, grad_point, grad_bias = call(
        final_kernel, (struct(GIVEN, BF16), struct((C, C), F32), struct((1, C), F32)),
        [VMEM, HBM, VMEM, VMEM], (HBM, VMEM, VMEM),
        [zf, pltpu.VMEM((3072, 128), F32), gather, planes, held, held, sems, sems],
        4 * 10**9, 2 * big, LIMIT, "input_gradient",
    )(got, mapped, tyt, zb)
    return input_grad, grad_spec, grad_point, grad_bias.reshape(C)


def solution(mesh):
    planes = P("batch", None, "slab", None, None)
    return jax.shard_map(
        body,
        mesh=mesh,
        in_specs=(planes, planes, P("slab", None, None, None), P(), P()),
        out_specs=(planes, P("slab", None, None, None), P(), P()),
        check_vma=False,
    )
```

time: 173 us -> 120 us (0.69)
  local copies, waits for them, and re-layouts: 30.6 us -> 0.05 us
  starting transfers between devices: 51.2 us -> 28.6 us
  waiting for transfers between devices: 24.2 us -> 33.8 us
  Pallas kernels: 62.4 us -> 56 us
  other arithmetic: 2.16 us -> 0.02 us
    unnamed x34 -> x16, local copies, waits for them, and re-layouts: 25.3 us -> 0.05 us
    all_to_all x4, starting transfers between devices: 39.4 us -> 25.3 us  [exchange(): return lax.all_to_all(buffer, BOTH, 0, 0, tiled=True)]
    pallas_call x1, Pallas kernels: 25.6 us -> 12.1 us  [body(): call(signal_kernel, (struct(PLANES, BF16), struct(BUFFER, BF16), struct((...]
    all_to_all x4, waiting for transfers between devices: 14.2 us -> 26.2 us  [exchange(): return lax.all_to_all(buffer, BOTH, 0, 0, tiled=True)]
    ppermute x9 -> x2, starting transfers between devices: 11.8 us -> 3.35 us  [the longest x1 1.77 us: body(): other_d = lax.ppermute(rows_d.astype(BF16), 'batch', swap)]
    pallas_call x8, Pallas kernels: 36.8 us -> 43.9 us  [the longest x1 8.58 us: body(): call(final_kernel, (struct(GIVEN, BF16), struct((C, C), F32), struct((1,...]
    mul x3 -> x0, local copies, waits for them, and re-layouts: 5.02 us -> none  [the longest x1 2.21 us: body(): kron = jnp.kron(point_weight.T, eye)]
    ppermute x9 -> x2, waiting for transfers between devices: 10 us -> 7.63 us  [the longest x1 7.62 us: body(): other_u = lax.ppermute(modes_u.astype(BF16), 'batch', swap)]
  transfers between devices with their start and end apart: 13 -> 6, of which waited for: 7 -> 5; matrix products, arithmetic and copies ran while one was open for 4% -> 0% of each run, Pallas kernels for 9% -> 18%
where the time goes in v2:
time: 120 us; the launch traced here: 119 us
  Pallas kernels  56 us (47%)
  waiting for transfers between devices  33.8 us (28%)
  starting transfers between devices  28.6 us (24%)
    all_to_all x4, waiting for transfers between devices, exchange(): return lax.all_to_all(buffer, BOTH, 0, 0, tiled=True)  26.2 us
    all_to_all x4, starting transfers between devices, exchange(): return lax.all_to_all(buffer, BOTH, 0, 0, tiled=True)  25.3 us
    pallas_call x1, Pallas kernels, body(): call(signal_kernel, (struct(PLANES, BF16), struct(BUFFER, BF16), struct((...  12.1 us
    pallas_call x1, Pallas kernels, body(): call(final_kernel, (struct(GIVEN, BF16), struct((C, C), F32), struct((1,...  8.58 us
    pallas_call x1, Pallas kernels, body(): call(field_kernel, struct(BUFFER, BF16), [HBM, HBM, HBM], VMEM, [zf, plan...  8.31 us
    ppermute x1, waiting for transfers between devices, body(): other_u = lax.ppermute(modes_u.astype(BF16), 'batch', swap)  7.62 us
    pallas_call x1, Pallas kernels, body(): call(pre_kernel, struct(PLANES, BF16), [HBM, VMEM, VMEM], HBM, [held, hel...  7.11 us
    pallas_call x1, Pallas kernels, body(): call(back_kernel, struct(PLANES, BF16), [HBM, VMEM], HBM, [held, held, se...  6.98 us
  transfers between devices with their start and end apart: 6, of which 5 were waited for; matrix products, arithmetic and copies ran while one was open for 0% of the time, Pallas kernels for 18%

profile of v2, /device:TPU:1, one launch (start us, length us, event | category | flops | bytes accessed | tf_op | source)
XLA Modules:
  0.0 119.5 jit_solution(13528297856180539064)
XLA Ops:
  0.6 0.0 copy-start.2
  0.6 0.0 copy-start.3
  0.7 8.3 %field_planes.1 = bf16[128,16,128]{2,1,0:T(8,128)(2,1)} custom-call(bf16[1,16,8,256,128]{4,3,2,1,0:T(8,128)(2,1)} %field_hbm.3, bf16[64,256]{1,0:T(8,128)(2,1)} %constant.14.clone.ty_hbm.ty_ref, bf16[256,512]{1,0:T(8,128)(2,1)} %constant.16.clone.zb_hbm.zb_ref), custom_call_target="tpu_custom_call" | custom-call | flops 2000000000 | bytes 8388608 | tf_op jit(solution)/shard_map/field_planes/pallas_call | solution.py:603
  9.0 11.5 %all-to-all-start = ((bf16[128,16,128]{2,1,0:T(8,128)(2,1)}), bf16[128,16,128]{2,1,0:T(8,128)(2,1)S(1)}, u32[]{:S(2)}, u32[]{:S(2)}) async-start(bf16[128,16,128]{2,1,0:T(8,128)(2,1)} %field_planes.1), calls=%async_computation | async-start | bytes 1048576 | tf_op jit(solution)/shard_map/all_to_all | solution.py:580
  20.5 0.0 copy-done.2
  20.5 0.0 copy-done.3
  20.5 0.0 copy-start.4
  20.5 0.0 copy-start.5
  20.5 0.0 copy-start.6
  20.5 0.0 copy-start
  20.6 0.0 copy-start.1
  20.6 0.0 copy-start.7
  20.6 7.1 %point_map.1.pre_hbm = bf16[8,16,256,128]{3,2,1,0:T(8,128)(2,1)} custom-call(bf16[1,16,8,256,128]{4,3,2,1,0:T(8,128)(2,1)} %field_hbm.3, bf16[16,16]{1,0:T(8,128)(2,1)S(1)} %copy-done.2, f32[1,16]{1,0:T(1,128)S(1)} %bitcast.9), custom_call_target="tpu_custom_call" | custom-call | flops 2000000000 | bytes 16777216 | tf_op jit(solution)/shard_map/point_map/pallas_call | solution.py:609
  27.7 6.9 %all-to-all-done = bf16[128,16,128]{2,1,0:T(8,128)(2,1)S(1)} async-done(((bf16[128,16,128]{2,1,0:T(8,128)(2,1)}), bf16[128,16,128]{2,1,0:T(8,128)(2,1)S(1)}, u32[]{:S(2)}, u32[]{:S(2)}) %all-to-all-start) | async-done | bytes 524320 | tf_op jit(solution)/shard_map/all_to_all | solution.py:580
  34.6 0.0 copy-done.4
  34.6 0.0 copy-done.5
  34.6 0.0 copy-done.6
  34.7 2.4 %mix_modes.1 = (bf16[64,2,16,128]{3,2,1,0:T(8,128)(2,1)}, f32[512,128]{1,0:T(8,128)S(1)}) custom-call(s32[1]{0:T(128)} %bitcast.which_ref, bf16[64,2,16,128]{3,2,1,0:T(8,128)(2,1)S(1)} %bitcast.7, bf16[16,2,16,512]{3,2,1,0:T(8,128)(2,1)S(1)} %copy-done.4, bf16[512,1024]{1,0:T(8,128)(2,1)S(1)} %copy-done.5, bf16[1024,128]{1,0:T(8,128)(2,1)S(1)} %copy-done.6), custom_call_target="tpu_custom_call" | custom-call | flops 1000000000 | bytes 3145728 | tf_op jit(solution)/shard_map/mix_modes/pallas_call | solution.py:614
  37.1 3.9 %all-to-all-start.1 = ((bf16[128,16,128]{2,1,0:T(8,128)(2,1)}), bf16[128,16,128]{2,1,0:T(8,128)(2,1)S(1)}, u32[]{:S(2)}, u32[]{:S(2)}) async-start(bf16[128,16,128]{2,1,0:T(8,128)(2,1)} %bitcast.3), calls=%async_computation.1 | async-start | bytes 1048576 | tf_op jit(solution)/shard_map/all_to_all | solution.py:580
  41.0 1.6 %collective-permute-start = (bf16[512,128]{1,0:T(8,128)(2,1)S(1)}, bf16[512,128]{1,0:T(8,128)(2,1)S(1)}, u32[]{:S(2)}, u32[]{:S(2)}) collective-permute-start(bf16[512,128]{1,0:T(8,128)(2,1)S(1)} %convert_element_type.6), channel_id=1, source_target_pairs={{0,1},{1,0},{2,3},{3,2},{4,5},{5,4},{6,7},{7,6},{8,9},{9,8},{10,11... | collective-permute-start | bytes 393224 | tf_op jit(solution)/shard_map/ppermute | solution.py:620
  42.6 7.6 %collective-permute-done.v_bf_ref = bf16[512,128]{1,0:T(8,128)(2,1)S(1)} collective-permute-done((bf16[512,128]{1,0:T(8,128)(2,1)S(1)}, bf16[512,128]{1,0:T(8,128)(2,1)S(1)}, u32[]{:S(2)}, u32[]{:S(2)}) %collective-permute-start) | collective-permute-done | bytes 131104 | tf_op jit(solution)/shard_map/ppermute | solution.py:620
  50.2 4.9 %all-to-all-done.1.in_ref = bf16[128,16,128]{2,1,0:T(8,128)(2,1)S(1)} async-done(((bf16[128,16,128]{2,1,0:T(8,128)(2,1)}), bf16[128,16,128]{2,1,0:T(8,128)(2,1)S(1)}, u32[]{:S(2)}, u32[]{:S(2)}) %all-to-all-start.1) | async-done | bytes 524320 | tf_op jit(solution)/shard_map/all_to_all | solution.py:580
  55.1 0.0 copy-done
  55.1 0.0 copy-done.1
  55.1 0.0 copy-done.7
  55.1 12.1 %signal.1 = (bf16[8,16,256,128]{3,2,1,0:T(8,128)(2,1)}, bf16[128,16,128]{2,1,0:T(8,128)(2,1)}, f32[8,256]{1,0:T(8,128)S(1)}) custom-call(bf16[128,16,128]{2,1,0:T(8,128)(2,1)S(1)} %all-to-all-done.1.in_ref, bf16[8,16,256,128]{3,2,1,0:T(8,128)(2,1)} %point_map.1.pre_hbm, bf16[1,16,8,256,128]{4,3,2,1,0:T(8,128)(2,1)} %cot_hbm.1, ...), custom_call_target="tpu_custom_call" | custom-call | flops 6000000000 | bytes 25165824 | tf_op jit(solution)/shard_map/signal/pallas_call | solution.py:622
  67.2 6.0 %all-to-all-start.2 = ((bf16[128,16,128]{2,1,0:T(8,128)(2,1)}), bf16[128,16,128]{2,1,0:T(8,128)(2,1)S(1)}, u32[]{:S(2)}, u32[]{:S(2)}) async-start(bf16[128,16,128]{2,1,0:T(8,128)(2,1)} %get-tuple-element.25), calls=%async_computation.2 | async-start | bytes 1048576 | tf_op jit(solution)/shard_map/all_to_all | solution.py:580
  73.2 6.8 %point_gradient.1.extra_ref = f32[8,128]{1,0:T(8,128)S(1)} custom-call(bf16[1,16,8,256,128]{4,3,2,1,0:T(8,128)(2,1)} %field_hbm.3, bf16[8,16,256,128]{3,2,1,0:T(8,128)(2,1)} %get-tuple-element.30.dpre_hbm.in_hbm, f32[8,256]{1,0:T(8,128)S(1)} %get-tuple-element.27.bias_ref), custom_call_target="tpu_custom_call" | custom-call | flops 2000000000 | bytes 16777216 | tf_op jit(solution)/shard_map/point_gradient/pallas_call | solution.py:630
  80.0 7.4 %all-to-all-done.2 = bf16[128,16,128]{2,1,0:T(8,128)(2,1)S(1)} async-done(((bf16[128,16,128]{2,1,0:T(8,128)(2,1)}), bf16[128,16,128]{2,1,0:T(8,128)(2,1)S(1)}, u32[]{:S(2)}, u32[]{:S(2)}) %all-to-all-start.2) | async-done | bytes 524320 | tf_op jit(solution)/shard_map/all_to_all | solution.py:580
  87.4 2.5 %adjoint_modes.1 = (bf16[64,2,24,128]{3,2,1,0:T(8,128)(2,1)}, f32[32,512]{1,0:T(8,128)S(1)}) custom-call(s32[1]{0:T(128)} %bitcast.which_ref, bf16[64,2,16,128]{3,2,1,0:T(8,128)(2,1)S(1)} %bitcast.8, bf16[16,2,16,512]{3,2,1,0:T(8,128)(2,1)S(1)} %copy-done.4, bf16[512,1024]{1,0:T(8,128)(2,1)S(1)} %copy-done.5, bf16[1024,128]{1,0:T(8,128)(2,1)S(1)} %copy-done.6, ...), custom_call_target="tpu_custom_call" | custom-call | flops 1000000000 | bytes 3145728 | tf_op jit(solution)/shard_map/adjoint_modes/pallas_call | solution.py:635
  89.9 3.9 %all-to-all-start.3 = ((bf16[128,24,128]{2,1,0:T(8,128)(2,1)}), bf16[128,24,128]{2,1,0:T(8,128)(2,1)S(1)}, u32[]{:S(2)}, u32[]{:S(2)}) async-start(bf16[128,24,128]{2,1,0:T(8,128)(2,1)} %bitcast.5), calls=%async_computation.3 | async-start | bytes 1572864 | tf_op jit(solution)/shard_map/all_to_all | solution.py:580
  93.8 1.8 %collective-permute-start.1 = (bf16[32,512]{1,0:T(8,128)(2,1)S(1)}, bf16[32,512]{1,0:T(8,128)(2,1)S(1)}, u32[]{:S(2)}, u32[]{:S(2)}) collective-permute-start(bf16[32,512]{1,0:T(8,128)(2,1)S(1)} %convert_element_type.7), channel_id=1, source_target_pairs={{0,1},{1,0},{2,3},{3,2},{4,5},{5,4},{6,7},{7,6},{8,9},{9,8},{10,11... | collective-permute-start | bytes 98312 | tf_op jit(solution)/shard_map/ppermute | solution.py:643
  95.5 7.0 %point_map_back.1.mapped_hbm = bf16[8,16,256,128]{3,2,1,0:T(8,128)(2,1)} custom-call(bf16[8,16,256,128]{3,2,1,0:T(8,128)(2,1)} %get-tuple-element.30.dpre_hbm.in_hbm, bf16[16,16]{1,0:T(8,128)(2,1)S(1)} %copy-done.2), custom_call_target="tpu_custom_call" | custom-call | flops 2000000000 | bytes 16777216 | tf_op jit(solution)/shard_map/point_map_back/pallas_call | solution.py:644
  102.5 0.0 collective-permute-done.1.e_bf_ref
  102.5 1.3 %spectral_gradient.1 = f32[16,2,16,512]{3,2,1,0:T(8,128)} custom-call(s32[1]{0:T(128)} %bitcast.which_ref, f32[512,128]{1,0:T(8,128)S(1)} %get-tuple-element.22.u_ref, bf16[512,128]{1,0:T(8,128)(2,1)S(1)} %collective-permute-done.v_bf_ref, f32[32,512]{1,0:T(8,128)S(1)} %get-tuple-element.33.d_ref, bf16[32,512]{1,0:T(8,128)(2,1)S(1)} %collective-permute-done.1.e_bf_ref), custom_call_target="tpu_custom_call" | custom-call | flops 10000000 | bytes 2097152 | tf_op jit(solution)/shard_map/spectral_gradient/pallas_call | solution.py:648
  103.8 6.9 %all-to-all-done.3.in_ref = bf16[128,24,128]{2,1,0:T(8,128)(2,1)S(1)} async-done(((bf16[128,24,128]{2,1,0:T(8,128)(2,1)}), bf16[128,24,128]{2,1,0:T(8,128)(2,1)S(1)}, u32[]{:S(2)}, u32[]{:S(2)}) %all-to-all-start.3) | async-done | bytes 786464 | tf_op jit(solution)/shard_map/all_to_all | solution.py:580
  110.7 8.6 %input_gradient.1 = (bf16[1,16,8,256,128]{4,3,2,1,0:T(8,128)(2,1)}, f32[16,16]{1,0:T(8,128)}, f32[1,16]{1,0:T(1,128)}) custom-call(bf16[128,24,128]{2,1,0:T(8,128)(2,1)S(1)} %all-to-all-done.3.in_ref, bf16[8,16,256,128]{3,2,1,0:T(8,128)(2,1)} %point_map_back.1.mapped_hbm, bf16[256,64]{1,0:T(8,128)(2,1)S(1)} %copy-done.7, bf16[256,512]{1,0:T(8,128)(2,1)S(1)} %copy-done), custom_call_target="tpu_custom_call" | custom-call | flops 4000000000 | bytes 16777216 | tf_op jit(solution)/shard_map/input_gradient/pallas_call | solution.py:653
  (2 shorter events, 0.0 us)
Async XLA Ops:
  0.6 19.9 %copy-start.2 = (bf16[16,16]{1,0:T(8,128)(2,1)S(1)}, bf16[16,16]{1,0:T(8,128)(2,1)}, u32[]{:S(2)}) copy-start(bf16[16,16]{1,0:T(8,128)(2,1)} %weight_ref.7) | copy-start | bytes 1540
  0.6 19.9 %copy-start.3 = (f32[16]{0:T(128)S(1)}, f32[16]{0:T(128)}, u32[]{:S(2)}) copy-start(f32[16]{0:T(128)} %param.14) | copy-start | bytes 196
  9.0 25.7 %all-to-all-start = ((bf16[128,16,128]{2,1,0:T(8,128)(2,1)}), bf16[128,16,128]{2,1,0:T(8,128)(2,1)S(1)}, u32[]{:S(2)}, u32[]{:S(2)}) async-start(bf16[128,16,128]{2,1,0:T(8,128)(2,1)} %field_planes.1), calls=%async_computation | async-start | bytes 1048576 | tf_op jit(solution)/shard_map/all_to_all | solution.py:580
  20.5 14.1 %copy-start.4 = (bf16[16,2,16,512]{3,2,1,0:T(8,128)(2,1)S(1)}, bf16[16,2,16,512]{3,2,1,0:T(8,128)(2,1)}, u32[]{:S(2)}) copy-start(bf16[16,2,16,512]{3,2,1,0:T(8,128)(2,1)} %weight_ref.6) | copy-start | bytes 1572868
  20.5 14.1 %copy-start.5 = (bf16[512,1024]{1,0:T(8,128)(2,1)S(1)}, bf16[512,1024]{1,0:T(8,128)(2,1)}, u32[]{:S(2)}) copy-start(bf16[512,1024]{1,0:T(8,128)(2,1)} %constant.17.clone.tx_ref) | copy-start | bytes 3145732
  20.5 14.1 %copy-start.6 = (bf16[1024,128]{1,0:T(8,128)(2,1)S(1)}, bf16[1024,128]{1,0:T(8,128)(2,1)}, u32[]{:S(2)}) copy-start(bf16[1024,128]{1,0:T(8,128)(2,1)} %constant.18.clone.txi_ref) | copy-start | bytes 786436
  20.5 34.6 %copy-start = (bf16[256,512]{1,0:T(8,128)(2,1)S(1)}, bf16[256,512]{1,0:T(8,128)(2,1)}, u32[]{:S(2)}) copy-start(bf16[256,512]{1,0:T(8,128)(2,1)} %constant.16.clone.zb_hbm.zb_ref) | copy-start | bytes 786436
  20.6 34.6 %copy-start.1 = (bf16[64,256]{1,0:T(8,128)(2,1)S(1)}, bf16[64,256]{1,0:T(8,128)(2,1)}, u32[]{:S(2)}) copy-start(bf16[64,256]{1,0:T(8,128)(2,1)} %constant.14.clone.ty_hbm.ty_ref) | copy-start | bytes 98308
  20.6 34.6 %copy-start.7 = (bf16[256,64]{1,0:T(8,128)(2,1)S(1)}, bf16[256,64]{1,0:T(8,128)(2,1)}, u32[]{:S(2)}) copy-start(bf16[256,64]{1,0:T(8,128)(2,1)} %constant.15.clone.tyt_ref) | copy-start | bytes 98308
  37.1 18.1 %all-to-all-start.1 = ((bf16[128,16,128]{2,1,0:T(8,128)(2,1)}), bf16[128,16,128]{2,1,0:T(8,128)(2,1)S(1)}, u32[]{:S(2)}, u32[]{:S(2)}) async-start(bf16[128,16,128]{2,1,0:T(8,128)(2,1)} %bitcast.3), calls=%async_computation.1 | async-start | bytes 1048576 | tf_op jit(solution)/shard_map/all_to_all | solution.py:580
  41.0 9.2 %collective-permute-start = (bf16[512,128]{1,0:T(8,128)(2,1)S(1)}, bf16[512,128]{1,0:T(8,128)(2,1)S(1)}, u32[]{:S(2)}, u32[]{:S(2)}) collective-permute-start(bf16[512,128]{1,0:T(8,128)(2,1)S(1)} %convert_element_type.6), channel_id=1, source_target_pairs={{0,1},{1,0},{2,3},{3,2},{4,5},{5,4},{6,7},{7,6},{8,9},{9,8},{10,11... | collective-permute-start | bytes 393224 | tf_op jit(solution)/shard_map/ppermute | solution.py:620
  67.2 20.1 %all-to-all-start.2 = ((bf16[128,16,128]{2,1,0:T(8,128)(2,1)}), bf16[128,16,128]{2,1,0:T(8,128)(2,1)S(1)}, u32[]{:S(2)}, u32[]{:S(2)}) async-start(bf16[128,16,128]{2,1,0:T(8,128)(2,1)} %get-tuple-element.25), calls=%async_computation.2 | async-start | bytes 1048576 | tf_op jit(solution)/shard_map/all_to_all | solution.py:580
  89.9 20.9 %all-to-all-start.3 = ((bf16[128,24,128]{2,1,0:T(8,128)(2,1)}), bf16[128,24,128]{2,1,0:T(8,128)(2,1)S(1)}, u32[]{:S(2)}, u32[]{:S(2)}) async-start(bf16[128,24,128]{2,1,0:T(8,128)(2,1)} %bitcast.5), calls=%async_computation.3 | async-start | bytes 1572864 | tf_op jit(solution)/shard_map/all_to_all | solution.py:580
  93.8 8.8 %collective-permute-start.1 = (bf16[32,512]{1,0:T(8,128)(2,1)S(1)}, bf16[32,512]{1,0:T(8,128)(2,1)S(1)}, u32[]{:S(2)}, u32[]{:S(2)}) collective-permute-start(bf16[32,512]{1,0:T(8,128)(2,1)S(1)} %convert_element_type.7), channel_id=1, source_target_pairs={{0,1},{1,0},{2,3},{3,2},{4,5},{5,4},{6,7},{7,6},{8,9},{9,8},{10,11... | collective-permute-start | bytes 98312 | tf_op jit(solution)/shard_map/ppermute | solution.py:643

commit v3 on v2

--- a/solution.py
+++ b/solution.py
@@ -28,7 +28,9 @@
 BF16 = jnp.bfloat16
 MIB = 1 << 20
 LIMIT = 48
-CUT = 2
+CUT = 4
+AHEAD = 4
+PARTS = 8
 
 
 def freqs(number, length):
@@ -73,6 +75,17 @@
     return lax.dot_general(left, right, (((1,), (1,)), ((), ())), preferred_element_type=F32)
 
 
+def send_part(stage_ref, out_hbm, sem, i):
+    count = out_hbm.shape[0] // PARTS
+    part = pl.ds(i * count, count)
+    return pltpu.make_async_copy(stage_ref.at[part], out_hbm.at[part], sem.at[i])
+
+
+def finish(stage_ref, out_hbm, sem):
+    for i in range(PARTS):
+        send_part(stage_ref, out_hbm, sem, i).wait()
+
+
 def build_z(zb_ref, zf_ref):
     channel = (lax.broadcasted_iota(jnp.int32, (2 * NZ, 256), 1) // 8) % 4
     for group in range(2):
@@ -86,7 +99,7 @@
     return lax.broadcasted_iota(jnp.int32, (rows, 128), 1) % 64 < 32
 
 
-def z_forward(planes_ref, zf_ref, wide_ref, out_ref):
+def z_forward(planes_ref, zf_ref, wide_ref, stage_ref, out_hbm, sem):
     low = low_lanes(256)
     for half in range(2):
         first, second = (
@@ -103,7 +116,12 @@
                     wide_ref[pl.ds((2 * t + j) * 16 + half * 8 + x, 32, stride=64), :] = value[
                         x * 32 : (x + 1) * 32
                     ]
-    out_ref[...] = wide_ref[...].astype(BF16).reshape(128, 16, 128)
+    for i in range(PARTS):
+        rows = 128 // PARTS
+        stage_ref[i * rows : (i + 1) * rows] = (
+            wide_ref[i * rows * 16 : (i + 1) * rows * 16, :].astype(BF16).reshape(rows, 16, 128)
+        )
+        send_part(stage_ref, out_hbm, sem, i).start()
 
 
 def z_inverse(in_ref, zf_ref, wide_ref, gather_ref, rolled_ref):
@@ -131,7 +149,8 @@
 def y_forward(ty_ref, pair, planes_ref, x, op):
     result = dot(ty_ref[...], pair)
     half, first = op // 4, (op % 4) * 2
-    rows = pl.ds(pl.multiple_of(half * 256 + x * 32, 32), 32)
+    row = half * 256 + x * 32
+    rows = pl.ds(row if isinstance(x, int) else pl.multiple_of(row, 32), 32)
     for j in range(2):
         for part in range(2):
             column = (first + j) * 256 + part * 128
@@ -178,8 +197,8 @@
 
 
 def field_kernel(
-    field_hbm, ty_hbm, zb_hbm, out_ref,
-    zf_ref, planes_ref, wide_ref, field_ref, ty_ref, zb_ref, sem, ty_sem, zb_sem,
+    field_hbm, ty_hbm, zb_hbm, out_hbm,
+    zf_ref, planes_ref, wide_ref, field_ref, ty_ref, zb_ref, stage_ref, sem, ty_sem, zb_sem, sent_sem,
 ):
     load = Planes(field_hbm, field_ref, sem, True)
     load_ty = pltpu.make_async_copy(ty_hbm, ty_ref, ty_sem)
@@ -187,21 +206,20 @@
     load_ty.start()
     load.start(0)
     load_zb.start()
-    for x in range(1, X):
+    for x in range(1, AHEAD):
         load.start(x)
     load_ty.wait()
     load_zb.wait()
     build_z(zb_ref, zf_ref)
-
-    def step(x, _):
+    for x in range(X):
+        if x + AHEAD < X:
+            load.start(x + AHEAD)
         load.wait(x)
         for op in range(8):
             pair = jnp.concatenate([field_ref[x, 2 * op], field_ref[x, 2 * op + 1]], axis=1)
             y_forward(ty_ref, pair, planes_ref, x, op)
-        return 0
-
-    lax.fori_loop(0, X, step, 0)
-    z_forward(planes_ref, zf_ref, wide_ref, out_ref)
+    z_forward(planes_ref, zf_ref, wide_ref, stage_ref, out_hbm, sent_sem)
+    finish(stage_ref, out_hbm, sent_sem)
 
 
 def y_blocks(ref, x):
@@ -271,9 +289,9 @@
 
 def signal_kernel(
     in_ref, pre_hbm, cot_hbm, ty_ref, tyt_ref, zb_ref,
-    dpre_hbm, out_ref, bias_ref,
-    zf_ref, planes_ref, wide_ref, gather_ref, rolled_ref, pre_ref, cot_ref,
-    pre_sem, cot_sem, out_sem,
+    dpre_hbm, out_hbm, bias_ref,
+    zf_ref, planes_ref, wide_ref, gather_ref, rolled_ref, pre_ref, cot_ref, stage_ref,
+    pre_sem, cot_sem, out_sem, sent_sem,
 ):
     load_pre = Planes(pre_hbm, pre_ref, pre_sem, False)
     load_cot = Planes(cot_hbm, cot_ref, cot_sem, True)
@@ -302,9 +320,10 @@
         return 0
 
     lax.fori_loop(0, X, step, 0)
-    z_forward(planes_ref, zf_ref, wide_ref, out_ref)
+    z_forward(planes_ref, zf_ref, wide_ref, stage_ref, out_hbm, sent_sem)
     for x in range(X):
         store.wait(x)
+    finish(stage_ref, out_hbm, sent_sem)
 
 
 def final_kernel(
@@ -367,7 +386,7 @@
                     modes_ref[pl.ds(pl.multiple_of(row, 32), 32), :] = turned[place : place + 32]
 
 
-def x_inverse(mixed, txi_ref, out_ref, extra):
+def x_inverse(mixed, txi_ref, stage_ref, extra, send):
     lane = lax.broadcasted_iota(jnp.int32, (32, 128), 1)
     rows = []
     for half in range(2):
@@ -378,14 +397,21 @@
                 [jnp.where(lane < 64, -1.0, 1.0) * pltpu.roll(g, 64, 1) for g in turned], axis=1
             )
         )
-    result = dot(txi_ref[...], jnp.concatenate(rows, axis=0).astype(BF16))
-    for b in range(2):
-        block = result[:, b * 128 : (b + 1) * 128].reshape(SLABS, 16, 128)
-        if extra is not None:
-            block = jnp.concatenate(
-                [block, jnp.broadcast_to(extra[None], (SLABS, 8, 128))], axis=1
-            )
-        out_ref[:, b] = block.astype(BF16)
+    right = jnp.concatenate(rows, axis=0).astype(BF16)
+    parts = 1 if send is None else PARTS
+    count = SLABS // parts
+    for i in range(parts):
+        result = dot(txi_ref[i * count * 16 : (i + 1) * count * 16, :], right)
+        if extra is None:
+            result = result.astype(BF16)
+        for b in range(2):
+            block = result[:, b * 128 : (b + 1) * 128].reshape(count, 16, 128)
+            if extra is not None:
+                more = jnp.broadcast_to(extra[None], (count, 8, 128))
+                block = jnp.concatenate([block, more], axis=1).astype(BF16)
+            stage_ref[i * count : (i + 1) * count, b] = block
+        if send is not None:
+            send_part(stage_ref, *send, i).start()
 
 
 def mix_kernel(which_ref, in_ref, weight_ref, tx_ref, txi_ref, out_ref, modes_ref, mixed_ref):
@@ -425,12 +451,12 @@
                     pieces.append(pltpu.roll(piece, 128 - 32 * r, 1) if r else piece)
         return jnp.concatenate(pieces, axis=0)
 
-    x_inverse(mixed, txi_ref, out_ref, None)
+    x_inverse(mixed, txi_ref, out_ref, None, None)
 
 
 def adjoint_kernel(
     which_ref, in_ref, weight_ref, tx_ref, txi_ref, extra_ref,
-    out_ref, rows_ref, modes_ref, mixed_ref,
+    out_hbm, rows_ref, short_ref, modes_ref, mixed_ref, stage_ref, sent_sem,
 ):
     which = which_ref[0]
     x_forward(which, in_ref, tx_ref, 0.5 * SCALE_I, modes_ref)
@@ -471,11 +497,18 @@
                 pieces.append(mixed_ref[pl.ds(pl.multiple_of(row, 32), 32), :])
         return jnp.concatenate(pieces, axis=0)
 
-    x_inverse(mixed, txi_ref, out_ref, extra_ref[...])
+    x_inverse(mixed, txi_ref, stage_ref, extra_ref[...], (out_hbm, sent_sem))
+    short_ref[...] = rows_ref[...].astype(BF16)
+    finish(stage_ref, out_hbm, sent_sem)
 
 
 def spec_kernel(which_ref, u_ref, v_bf_ref, d_ref, e_bf_ref, out_ref, v_ref, e_ref):
-    v_ref[...] = v_bf_ref[...].astype(F32)
+    group = lax.broadcasted_iota(jnp.int32, (128, 128), 1) // 32
+    short = v_bf_ref[...].astype(F32)
+    for i in range(4):
+        part = jnp.where(group == i, short, 0.0)
+        part = part + pltpu.roll(part, 32, 1)
+        v_ref[i * 128 : (i + 1) * 128, :] = part + pltpu.roll(part, 64, 1)
     e_ref[...] = e_bf_ref[...].astype(F32)
     mine = which_ref[0] * 8
     other = 8 - mine
@@ -502,13 +535,19 @@
 
 
 def point_kernel(
-    field_hbm, dpre_hbm, bias_ref, out_ref, acc_ref, field_ref, dpre_ref, field_sem, dpre_sem
+    field_hbm, dpre_hbm, bias_ref, modes_ref, out_ref, short_ref,
+    acc_ref, field_ref, dpre_ref, field_sem, dpre_sem,
 ):
     load_field = Planes(field_hbm, field_ref, field_sem, True)
     load_dpre = Planes(dpre_hbm, dpre_ref, dpre_sem, False)
     for x in range(X):
         load_field.start(x)
         load_dpre.start(x)
+    group = lax.broadcasted_iota(jnp.int32, (128, 128), 1) // 32
+    short = modes_ref[0:128, :]
+    for i in range(1, 4):
+        short = jnp.where(group == i, modes_ref[i * 128 : (i + 1) * 128, :], short)
+    short_ref[...] = short.astype(BF16)
     acc_ref[...] = jnp.zeros_like(acc_ref)
 
     def step(x, _):
@@ -596,14 +635,15 @@
     wide = pltpu.VMEM((2048, 128), F32)
     gather = pltpu.VMEM((512, 512), BF16)
     held = pltpu.VMEM(PLANES, BF16)
+    stage = pltpu.VMEM(BUFFER, BF16)
     sems = pltpu.SemaphoreType.DMA((X,))
     big = 8 * MIB
     swap = [(0, 1), (1, 0)]
 
     sent = call(
-        field_kernel, struct(BUFFER, BF16), [HBM, HBM, HBM], VMEM,
-        [zf, planes, wide, held, pltpu.VMEM((64, NY), BF16), pltpu.VMEM((256, 512), BF16), sems,
-         pltpu.SemaphoreType.DMA, pltpu.SemaphoreType.DMA], 2 * 10**9, big, 60, "field_planes",
+        field_kernel, struct(BUFFER, BF16), [HBM, HBM, HBM], HBM,
+        [zf, planes, wide, held, pltpu.VMEM((64, NY), BF16), pltpu.VMEM((256, 512), BF16), stage,
+         sems, pltpu.SemaphoreType.DMA, pltpu.SemaphoreType.DMA, sems], 2 * 10**9, big, 60, "field_planes",
     )(field, ty, zb)
     got = exchange(sent)
     pre = call(
@@ -612,35 +652,39 @@
     )(field, point_weight, point_bias.reshape(1, C))
     got, pre = lax.optimization_barrier((got, pre))
     back, modes_u = call(
-        mix_kernel, (struct((SLABS, 2, 16, 128), BF16), struct((512, 128), F32)),
+        mix_kernel,
+        (struct((SLABS, 2, 16, 128), BF16), struct((512, 128), F32)),
         [SMEM] + [VMEM] * 4, (VMEM, VMEM),
-        [pltpu.VMEM((32, 512), F32)], 10**9, 3 * MIB, 32, "mix_modes",
+        [pltpu.VMEM((32, 512), F32)],
+        10**9, 3 * MIB, 32, "mix_modes",
     )(which, grouped(got), spectral_weight, tx, txi)
     got = exchange(flat(back))
-    other_u = lax.ppermute(modes_u.astype(BF16), "batch", swap)
-    got, other_u = lax.optimization_barrier((got, other_u))
     dpre, sent, bias_rows = call(
         signal_kernel,
         (struct(PLANES, BF16), struct(BUFFER, BF16), struct((8, 256), F32)),
-        [VMEM, HBM, HBM, VMEM, VMEM, VMEM], (HBM, VMEM, VMEM),
-        [zf, planes, wide, gather, planes, held, held, sems, sems, sems],
+        [VMEM, HBM, HBM, VMEM, VMEM, VMEM], (HBM, HBM, VMEM),
+        [zf, planes, wide, gather, planes, held, held, stage, sems, sems, sems, sems],
         6 * 10**9, 3 * big, LIMIT, "signal",
     )(got, pre, cotangent, ty, tyt, zb)
     got = exchange(sent)
-    extra = call(
-        point_kernel, struct((8, 128), F32), [HBM, HBM, VMEM], VMEM,
+    extra, short_u = call(
+        point_kernel, (struct((8, 128), F32), struct((128, 128), BF16)),
+        [HBM, HBM, VMEM, VMEM], (VMEM, VMEM),
         [pltpu.VMEM((256, 256), F32), held, held, sems, sems],
         2 * 10**9, 2 * big, LIMIT, "point_gradient",
-    )(field, dpre, bias_rows)
-    back, rows_d = call(
-        adjoint_kernel, (struct((SLABS, 2, 24, 128), BF16), struct((32, 512), F32)),
-        [SMEM] + [VMEM] * 5, (VMEM, VMEM),
-        [pltpu.VMEM((512, 128), F32), pltpu.VMEM((512, 128), F32)],
+    )(field, dpre, bias_rows, modes_u)
+    back, rows_d, short_d = call(
+        adjoint_kernel,
+        (struct((SLABS, 2, 24, 128), BF16), struct((32, 512), F32), struct((32, 512), BF16)),
+        [SMEM] + [VMEM] * 5, (HBM, VMEM, VMEM),
+        [pltpu.VMEM((512, 128), F32), pltpu.VMEM((512, 128), F32),
+         pltpu.VMEM((SLABS, 2, 24, 128), BF16), sems],
         10**9, 3 * MIB, 32, "adjoint_modes",
     )(which, grouped(got), spectral_weight, tx, txi, extra)
-    dpre, rows_d = lax.optimization_barrier((dpre, rows_d))
+    dpre, short_d, short_u = lax.optimization_barrier((dpre, short_d, short_u))
     got = exchange(flat(back))
-    other_d = lax.ppermute(rows_d.astype(BF16), "batch", swap)
+    other_u = lax.ppermute(short_u, "batch", swap)
+    other_d = lax.ppermute(short_d, "batch", swap)
     mapped = call(
         back_kernel, struct(PLANES, BF16), [HBM, VMEM], HBM,
         [held, held, sems, sems], 2 * 10**9, 2 * big, LIMIT, "point_map_back",

time: 120 us -> 115 us (0.958)
  blocking collectives: 0 us -> 17.9 us
  waiting for transfers between devices: 33.8 us -> 21.3 us
  starting transfers between devices: 28.6 us -> 21.1 us
  Pallas kernels: 56 us -> 53.5 us
    all_to_all x0 -> x1, blocking collectives: none -> 17.9 us  [exchange(): return lax.all_to_all(buffer, BOTH, 0, 0, tiled=True)]
    ppermute x2, waiting for transfers between devices: 7.63 us -> 0.01 us  [the longest x1 0.01 us: body(): other_u = lax.ppermute(short_u, 'batch', swap)]
    all_to_all x4 -> x3, starting transfers between devices: 25.3 us -> 19.3 us  [exchange(): return lax.all_to_all(buffer, BOTH, 0, 0, tiled=True)]
    all_to_all x4 -> x3, waiting for transfers between devices: 26.2 us -> 21.3 us  [exchange(): return lax.all_to_all(buffer, BOTH, 0, 0, tiled=True)]
    ppermute x2, starting transfers between devices: 3.35 us -> 1.82 us  [the longest x1 1.73 us: body(): other_u = lax.ppermute(short_u, 'batch', swap)]
    pallas_call x2, Pallas kernels: 15.1 us -> 13.6 us  [the longest x1 6.89 us: body(): call(field_kernel, struct(BUFFER, BF16), [HBM, HBM, HBM], HBM, [zf, plane...]
  transfers between devices with their start and end apart: 6 -> 5, of which waited for: 5 -> 3; matrix products, arithmetic and copies ran while one was open for 0% -> 0% of each run, Pallas kernels for 18% -> 19%
where the time goes in v3:
time: 115 us
  Pallas kernels  53.5 us (47%)
  waiting for transfers between devices  21.3 us (19%)
  starting transfers between devices  21.1 us (18%)
  blocking collectives  17.9 us (16%)
    all_to_all x3, waiting for transfers between devices, exchange(): return lax.all_to_all(buffer, BOTH, 0, 0, tiled=True)  21.3 us
    all_to_all x3, starting transfers between devices, exchange(): return lax.all_to_all(buffer, BOTH, 0, 0, tiled=True)  19.3 us
    all_to_all x1, blocking collectives, exchange(): return lax.all_to_all(buffer, BOTH, 0, 0, tiled=True)  17.9 us
    pallas_call x1, Pallas kernels, body(): call(signal_kernel, (struct(PLANES, BF16), struct(BUFFER, BF16), struct((...  12 us
    pallas_call x1, Pallas kernels, body(): call(final_kernel, (struct(GIVEN, BF16), struct((C, C), F32), struct((1,...  8.55 us
    pallas_call x1, Pallas kernels, body(): call(pre_kernel, struct(PLANES, BF16), [HBM, VMEM, VMEM], HBM, [held, hel...  7.05 us
    pallas_call x1, Pallas kernels, body(): call(back_kernel, struct(PLANES, BF16), [HBM, VMEM], HBM, [held, held, se...  6.92 us
    pallas_call x1, Pallas kernels, body(): call(field_kernel, struct(BUFFER, BF16), [HBM, HBM, HBM], HBM, [zf, plane...  6.89 us
  transfers between devices with their start and end apart: 5, of which 3 were waited for; matrix products, arithmetic and copies ran while one was open for 0% of the time, Pallas kernels for 19%

profile of v3, /device:TPU:1, one launch (start us, length us, event | category | flops | bytes accessed | tf_op | source)
XLA Modules:
  0.0 114.8 jit_solution(11284424453173423627)
XLA Ops:
  0.6 0.0 copy-start.2
  0.6 0.0 copy-start.3
  0.7 6.9 %field_planes.1 = bf16[128,16,128]{2,1,0:T(8,128)(2,1)} custom-call(bf16[1,16,8,256,128]{4,3,2,1,0:T(8,128)(2,1)} %field_hbm.3, bf16[64,256]{1,0:T(8,128)(2,1)} %constant.14.clone.ty_hbm.ty_ref, bf16[256,512]{1,0:T(8,128)(2,1)} %constant.16.clone.zb_hbm.zb_ref), custom_call_target="tpu_custom_call" | custom-call | flops 2000000000 | bytes 8388608 | tf_op jit(solution)/shard_map/field_planes/pallas_call | solution.py:643
  7.6 11.5 %all-to-all-start = ((bf16[128,16,128]{2,1,0:T(8,128)(2,1)}), bf16[128,16,128]{2,1,0:T(8,128)(2,1)S(1)}, u32[]{:S(2)}, u32[]{:S(2)}) async-start(bf16[128,16,128]{2,1,0:T(8,128)(2,1)} %field_planes.1), calls=%async_computation | async-start | bytes 1048576 | tf_op jit(solution)/shard_map/all_to_all | solution.py:619
  19.1 0.0 copy-done.2
  19.1 0.0 copy-done.3
  19.1 0.0 copy-start.4
  19.1 0.0 copy-start.5
  19.1 0.0 copy-start.6
  19.1 0.0 copy-start
  19.1 0.0 copy-start.1
  19.2 0.0 copy-start.7
  19.2 7.0 %point_map.1.pre_hbm = bf16[8,16,256,128]{3,2,1,0:T(8,128)(2,1)} custom-call(bf16[1,16,8,256,128]{4,3,2,1,0:T(8,128)(2,1)} %field_hbm.3, bf16[16,16]{1,0:T(8,128)(2,1)S(1)} %copy-done.2, f32[1,16]{1,0:T(1,128)S(1)} %bitcast.10), custom_call_target="tpu_custom_call" | custom-call | flops 2000000000 | bytes 16777216 | tf_op jit(solution)/shard_map/point_map/pallas_call | solution.py:649
  26.2 7.0 %all-to-all-done = bf16[128,16,128]{2,1,0:T(8,128)(2,1)S(1)} async-done(((bf16[128,16,128]{2,1,0:T(8,128)(2,1)}), bf16[128,16,128]{2,1,0:T(8,128)(2,1)S(1)}, u32[]{:S(2)}, u32[]{:S(2)}) %all-to-all-start) | async-done | bytes 524320 | tf_op jit(solution)/shard_map/all_to_all | solution.py:619
  33.2 0.0 copy-done.4
  33.2 0.0 copy-done.5
  33.2 0.0 copy-done.6
  33.2 1.6 %mix_modes.1 = (bf16[64,2,16,128]{3,2,1,0:T(8,128)(2,1)S(1)}, f32[512,128]{1,0:T(8,128)S(1)}) custom-call(s32[1]{0:T(128)} %bitcast.which_ref, bf16[64,2,16,128]{3,2,1,0:T(8,128)(2,1)S(1)} %bitcast.8, bf16[16,2,16,512]{3,2,1,0:T(8,128)(2,1)S(1)} %copy-done.4, bf16[512,1024]{1,0:T(8,128)(2,1)S(1)} %copy-done.5, bf16[1024,128]{1,0:T(8,128)(2,1)S(1)} %copy-done.6), custom_call_target="tpu_custom_call" | custom-call | flops 1000000000 | bytes 3145728 | tf_op jit(solution)/shard_map/mix_modes/pallas_call | solution.py:654
  34.9 17.9 %all_to_all.20.in_ref = bf16[128,16,128]{2,1,0:T(8,128)(2,1)S(1)} all-to-all(bf16[128,16,128]{2,1,0:T(8,128)(2,1)S(1)} %bitcast.9), channel_id=1, replica_groups=mesh['slab'=64,'batch'=2] {'slab','batch'}, dimensions={0} | all-to-all | bytes 1048576 | tf_op jit(solution)/shard_map/all_to_all | solution.py:619
  52.7 0.0 copy-done
  52.7 0.0 copy-done.1
  52.7 0.0 copy-done.7
  52.7 12.0 %signal.1 = (bf16[8,16,256,128]{3,2,1,0:T(8,128)(2,1)}, bf16[128,16,128]{2,1,0:T(8,128)(2,1)}, f32[8,256]{1,0:T(8,128)S(1)}) custom-call(bf16[128,16,128]{2,1,0:T(8,128)(2,1)S(1)} %all_to_all.20.in_ref, bf16[8,16,256,128]{3,2,1,0:T(8,128)(2,1)} %point_map.1.pre_hbm, bf16[1,16,8,256,128]{4,3,2,1,0:T(8,128)(2,1)} %cot_hbm.1, bf16[64,256]{1,0:T(8,128)(2,1)S(1)} %copy-done.1, ...), custom_call_target="tpu_custom_call" | custom-call | flops 6000000000 | bytes 25165824 | tf_op jit(solution)/shard_map/signal/pallas_call | solution.py:662
  64.7 3.9 %all-to-all-start.2 = ((bf16[128,16,128]{2,1,0:T(8,128)(2,1)}), bf16[128,16,128]{2,1,0:T(8,128)(2,1)S(1)}, u32[]{:S(2)}, u32[]{:S(2)}) async-start(bf16[128,16,128]{2,1,0:T(8,128)(2,1)} %get-tuple-element.25), calls=%async_computation.2 | async-start | bytes 1048576 | tf_op jit(solution)/shard_map/all_to_all | solution.py:619
  68.6 6.7 %point_gradient.1 = (f32[8,128]{1,0:T(8,128)S(1)}, bf16[128,128]{1,0:T(8,128)(2,1)S(1)}) custom-call(bf16[1,16,8,256,128]{4,3,2,1,0:T(8,128)(2,1)} %field_hbm.3, bf16[8,16,256,128]{3,2,1,0:T(8,128)(2,1)} %get-tuple-element.33.dpre_hbm.in_hbm, f32[8,256]{1,0:T(8,128)S(1)} %get-tuple-element.27.bias_ref, f32[512,128]{1,0:T(8,128)S(1)} %get-tuple-element.28.modes_ref.u_ref), custom_call_target="tpu_custom_call" | custom-call | flops 2000000000 | bytes 16777216 | tf_op jit(solution)/shard_map/point_gradient/pallas_call | solution.py:670
  75.3 7.5 %all-to-all-done.2 = bf16[128,16,128]{2,1,0:T(8,128)(2,1)S(1)} async-done(((bf16[128,16,128]{2,1,0:T(8,128)(2,1)}), bf16[128,16,128]{2,1,0:T(8,128)(2,1)S(1)}, u32[]{:S(2)}, u32[]{:S(2)}) %all-to-all-start.2) | async-done | bytes 524320 | tf_op jit(solution)/shard_map/all_to_all | solution.py:619
  82.8 2.3 %adjoint_modes.1 = (bf16[64,2,24,128]{3,2,1,0:T(8,128)(2,1)}, f32[32,512]{1,0:T(8,128)S(1)}, bf16[32,512]{1,0:T(8,128)(2,1)S(1)}) custom-call(s32[1]{0:T(128)} %bitcast.which_ref, bf16[64,2,16,128]{3,2,1,0:T(8,128)(2,1)S(1)} %bitcast.7, bf16[16,2,16,512]{3,2,1,0:T(8,128)(2,1)S(1)} %copy-done.4, bf16[512,1024]{1,0:T(8,128)(2,1)S(1)} %copy-done.5, ...), custom_call_target="tpu_custom_call" | custom-call | flops 1000000000 | bytes 3145728 | tf_op jit(solution)/shard_map/adjoint_modes/pallas_call | solution.py:676
  85.1 3.9 %all-to-all-start.3 = ((bf16[128,24,128]{2,1,0:T(8,128)(2,1)}), bf16[128,24,128]{2,1,0:T(8,128)(2,1)S(1)}, u32[]{:S(2)}, u32[]{:S(2)}) async-start(bf16[128,24,128]{2,1,0:T(8,128)(2,1)} %bitcast.5), calls=%async_computation.3 | async-start | bytes 1572864 | tf_op jit(solution)/shard_map/all_to_all | solution.py:619
  89.0 1.7 %collective-permute-start = (bf16[128,128]{1,0:T(8,128)(2,1)S(1)}, bf16[128,128]{1,0:T(8,128)(2,1)S(1)}, u32[]{:S(2)}, u32[]{:S(2)}) collective-permute-start(bf16[128,128]{1,0:T(8,128)(2,1)S(1)} %get-tuple-element.35), channel_id=1, source_target_pairs={{0,1},{1,0},{2,3},{3,2},{4,5},{5,4},{6,7},{7,6},{8,9},{9,8},{10,11... | collective-permute-start | bytes 98312 | tf_op jit(solution)/shard_map/ppermute | solution.py:686
  90.8 0.1 collective-permute-start.1
  90.8 6.9 %point_map_back.1.mapped_hbm = bf16[8,16,256,128]{3,2,1,0:T(8,128)(2,1)} custom-call(bf16[8,16,256,128]{3,2,1,0:T(8,128)(2,1)} %get-tuple-element.33.dpre_hbm.in_hbm, bf16[16,16]{1,0:T(8,128)(2,1)S(1)} %copy-done.2), custom_call_target="tpu_custom_call" | custom-call | flops 2000000000 | bytes 16777216 | tf_op jit(solution)/shard_map/point_map_back/pallas_call | solution.py:688
  97.8 0.0 collective-permute-done.v_bf_ref
  97.8 0.0 collective-permute-done.1.e_bf_ref
  97.8 1.5 %spectral_gradient.1 = f32[16,2,16,512]{3,2,1,0:T(8,128)} custom-call(s32[1]{0:T(128)} %bitcast.which_ref, f32[512,128]{1,0:T(8,128)S(1)} %get-tuple-element.28.modes_ref.u_ref, bf16[128,128]{1,0:T(8,128)(2,1)S(1)} %collective-permute-done.v_bf_ref, f32[32,512]{1,0:T(8,128)S(1)} %get-tuple-element.36.d_ref, bf16[32,512]{1,0:T(8,128)(2,1)S(1)} %collective-permute-done.1.e_bf_ref), custom_call_target="tpu_custom_call" | custom-call | flops 10000000 | bytes 2097152 | tf_op jit(solution)/shard_map/spectral_gradient/pallas_call | solution.py:692
  99.3 6.8 %all-to-all-done.3.in_ref = bf16[128,24,128]{2,1,0:T(8,128)(2,1)S(1)} async-done(((bf16[128,24,128]{2,1,0:T(8,128)(2,1)}), bf16[128,24,128]{2,1,0:T(8,128)(2,1)S(1)}, u32[]{:S(2)}, u32[]{:S(2)}) %all-to-all-start.3) | async-done | bytes 786464 | tf_op jit(solution)/shard_map/all_to_all | solution.py:619
  106.1 8.5 %input_gradient.1 = (bf16[1,16,8,256,128]{4,3,2,1,0:T(8,128)(2,1)}, f32[16,16]{1,0:T(8,128)}, f32[1,16]{1,0:T(1,128)}) custom-call(bf16[128,24,128]{2,1,0:T(8,128)(2,1)S(1)} %all-to-all-done.3.in_ref, bf16[8,16,256,128]{3,2,1,0:T(8,128)(2,1)} %point_map_back.1.mapped_hbm, bf16[256,64]{1,0:T(8,128)(2,1)S(1)} %copy-done.7, bf16[256,512]{1,0:T(8,128)(2,1)S(1)} %copy-done), custom_call_target="tpu_custom_call" | custom-call | flops 4000000000 | bytes 16777216 | tf_op jit(solution)/shard_map/input_gradient/pallas_call | solution.py:697
Async XLA Ops:
  0.6 18.4 %copy-start.2 = (bf16[16,16]{1,0:T(8,128)(2,1)S(1)}, bf16[16,16]{1,0:T(8,128)(2,1)}, u32[]{:S(2)}) copy-start(bf16[16,16]{1,0:T(8,128)(2,1)} %weight_ref.7) | copy-start | bytes 1540
  0.6 18.4 %copy-start.3 = (f32[16]{0:T(128)S(1)}, f32[16]{0:T(128)}, u32[]{:S(2)}) copy-start(f32[16]{0:T(128)} %param.14) | copy-start | bytes 196
  7.6 25.7 %all-to-all-start = ((bf16[128,16,128]{2,1,0:T(8,128)(2,1)}), bf16[128,16,128]{2,1,0:T(8,128)(2,1)S(1)}, u32[]{:S(2)}, u32[]{:S(2)}) async-start(bf16[128,16,128]{2,1,0:T(8,128)(2,1)} %field_planes.1), calls=%async_computation | async-start | bytes 1048576 | tf_op jit(solution)/shard_map/all_to_all | solution.py:619
  19.1 14.1 %copy-start.4 = (bf16[16,2,16,512]{3,2,1,0:T(8,128)(2,1)S(1)}, bf16[16,2,16,512]{3,2,1,0:T(8,128)(2,1)}, u32[]{:S(2)}) copy-start(bf16[16,2,16,512]{3,2,1,0:T(8,128)(2,1)} %weight_ref.6) | copy-start | bytes 1572868
  19.1 14.1 %copy-start.5 = (bf16[512,1024]{1,0:T(8,128)(2,1)S(1)}, bf16[512,1024]{1,0:T(8,128)(2,1)}, u32[]{:S(2)}) copy-start(bf16[512,1024]{1,0:T(8,128)(2,1)} %constant.17.clone.tx_ref) | copy-start | bytes 3145732
  19.1 14.1 %copy-start.6 = (bf16[1024,128]{1,0:T(8,128)(2,1)S(1)}, bf16[1024,128]{1,0:T(8,128)(2,1)}, u32[]{:S(2)}) copy-start(bf16[1024,128]{1,0:T(8,128)(2,1)} %constant.18.clone.txi_ref) | copy-start | bytes 786436
  19.1 33.6 %copy-start = (bf16[256,512]{1,0:T(8,128)(2,1)S(1)}, bf16[256,512]{1,0:T(8,128)(2,1)}, u32[]{:S(2)}) copy-start(bf16[256,512]{1,0:T(8,128)(2,1)} %constant.16.clone.zb_hbm.zb_ref) | copy-start | bytes 786436
  19.1 33.6 %copy-start.1 = (bf16[64,256]{1,0:T(8,128)(2,1)S(1)}, bf16[64,256]{1,0:T(8,128)(2,1)}, u32[]{:S(2)}) copy-start(bf16[64,256]{1,0:T(8,128)(2,1)} %constant.14.clone.ty_hbm.ty_ref) | copy-start | bytes 98308
  19.2 33.6 %copy-start.7 = (bf16[256,64]{1,0:T(8,128)(2,1)S(1)}, bf16[256,64]{1,0:T(8,128)(2,1)}, u32[]{:S(2)}) copy-start(bf16[256,64]{1,0:T(8,128)(2,1)} %constant.15.clone.tyt_ref) | copy-start | bytes 98308
  64.7 18.1 %all-to-all-start.2 = ((bf16[128,16,128]{2,1,0:T(8,128)(2,1)}), bf16[128,16,128]{2,1,0:T(8,128)(2,1)S(1)}, u32[]{:S(2)}, u32[]{:S(2)}) async-start(bf16[128,16,128]{2,1,0:T(8,128)(2,1)} %get-tuple-element.25), calls=%async_computation.2 | async-start | bytes 1048576 | tf_op jit(solution)/shard_map/all_to_all | solution.py:619
  85.1 21.0 %all-to-all-start.3 = ((bf16[128,24,128]{2,1,0:T(8,128)(2,1)}), bf16[128,24,128]{2,1,0:T(8,128)(2,1)S(1)}, u32[]{:S(2)}, u32[]{:S(2)}) async-start(bf16[128,24,128]{2,1,0:T(8,128)(2,1)} %bitcast.5), calls=%async_computation.3 | async-start | bytes 1572864 | tf_op jit(solution)/shard_map/all_to_all | solution.py:619
  89.0 8.7 %collective-permute-start = (bf16[128,128]{1,0:T(8,128)(2,1)S(1)}, bf16[128,128]{1,0:T(8,128)(2,1)S(1)}, u32[]{:S(2)}, u32[]{:S(2)}) collective-permute-start(bf16[128,128]{1,0:T(8,128)(2,1)S(1)} %get-tuple-element.35), channel_id=1, source_target_pairs={{0,1},{1,0},{2,3},{3,2},{4,5},{5,4},{6,7},{7,6},{8,9},{9,8},{10,11... | collective-permute-start | bytes 98312 | tf_op jit(solution)/shard_map/ppermute | solution.py:686
  90.8 7.0 %collective-permute-start.1 = (bf16[32,512]{1,0:T(8,128)(2,1)S(1)}, bf16[32,512]{1,0:T(8,128)(2,1)S(1)}, u32[]{:S(2)}, u32[]{:S(2)}) collective-permute-start(bf16[32,512]{1,0:T(8,128)(2,1)S(1)} %get-tuple-element.37), channel_id=1, source_target_pairs={{0,1},{1,0},{2,3},{3,2},{4,5},{5,4},{6,7},{7,6},{8,9},{9,8},{10,11... | collective-permute-start | bytes 98312 | tf_op jit(solution)/shard_map/ppermute | solution.py:687

commit v4 on v3

--- a/solution.py
+++ b/solution.py
@@ -28,8 +28,9 @@
 BF16 = jnp.bfloat16
 MIB = 1 << 20
 LIMIT = 48
-CUT = 4
+CUT = 8
 AHEAD = 4
+Z_CUTS = (4, 8)
 PARTS = 8
 
 
@@ -99,12 +100,13 @@
     return lax.broadcasted_iota(jnp.int32, (rows, 128), 1) % 64 < 32
 
 
-def z_forward(planes_ref, zf_ref, wide_ref, stage_ref, out_hbm, sem):
-    low = low_lanes(256)
+def z_part(planes_ref, zf_ref, wide_ref, start, count):
+    low = low_lanes(count * 32)
     for half in range(2):
+        row = half * 256 + start * 32
         first, second = (
             dot(
-                planes_ref[half * 256 : (half + 1) * 256, group * 1024 : (group + 1) * 1024],
+                planes_ref[row : row + count * 32, group * 1024 : (group + 1) * 1024],
                 zf_ref[group * 1024 : (group + 1) * 1024, :],
             )
             for group in range(2)
@@ -112,12 +114,14 @@
         for t in range(2):
             one, two = first[:, t * 128 : (t + 1) * 128], second[:, t * 128 : (t + 1) * 128]
             for j, value in enumerate((jnp.where(low, one, two), jnp.where(low, two, one))):
-                for x in range(X):
-                    wide_ref[pl.ds((2 * t + j) * 16 + half * 8 + x, 32, stride=64), :] = value[
-                        x * 32 : (x + 1) * 32
-                    ]
+                for x in range(count):
+                    place = (2 * t + j) * 16 + half * 8 + start + x
+                    wide_ref[pl.ds(place, 32, stride=64), :] = value[x * 32 : (x + 1) * 32]
+
+
+def z_send(wide_ref, stage_ref, out_hbm, sem):
+    rows = 128 // PARTS
     for i in range(PARTS):
-        rows = 128 // PARTS
         stage_ref[i * rows : (i + 1) * rows] = (
             wide_ref[i * rows * 16 : (i + 1) * rows * 16, :].astype(BF16).reshape(rows, 16, 128)
         )
@@ -218,7 +222,10 @@
         for op in range(8):
             pair = jnp.concatenate([field_ref[x, 2 * op], field_ref[x, 2 * op + 1]], axis=1)
             y_forward(ty_ref, pair, planes_ref, x, op)
-    z_forward(planes_ref, zf_ref, wide_ref, stage_ref, out_hbm, sent_sem)
+        if x + 1 in Z_CUTS:
+            start = max([0] + [cut for cut in Z_CUTS if cut < x + 1])
+            z_part(planes_ref, zf_ref, wide_ref, start, x + 1 - start)
+    z_send(wide_ref, stage_ref, out_hbm, sent_sem)
     finish(stage_ref, out_hbm, sent_sem)
 
 
@@ -320,7 +327,8 @@
         return 0
 
     lax.fori_loop(0, X, step, 0)
-    z_forward(planes_ref, zf_ref, wide_ref, stage_ref, out_hbm, sent_sem)
+    z_part(planes_ref, zf_ref, wide_ref, 0, X)
+    z_send(wide_ref, stage_ref, out_hbm, sent_sem)
     for x in range(X):
         store.wait(x)
     finish(stage_ref, out_hbm, sent_sem)

time: 115 us -> 115 us (level)
  no operation moved by 1% of the time
where the time goes in v4:
time: 115 us; the launch traced here: 114 us
  Pallas kernels  53 us (46%)
  waiting for transfers between devices  21.3 us (19%)
  starting transfers between devices  21.1 us (18%)
  blocking collectives  17.9 us (16%)
    all_to_all x3, waiting for transfers between devices, exchange(): return lax.all_to_all(buffer, BOTH, 0, 0, tiled=True)  21.3 us
    all_to_all x3, starting transfers between devices, exchange(): return lax.all_to_all(buffer, BOTH, 0, 0, tiled=True)  19.3 us
    all_to_all x1, blocking collectives, exchange(): return lax.all_to_all(buffer, BOTH, 0, 0, tiled=True)  17.9 us
    pallas_call x1, Pallas kernels, body(): call(signal_kernel, (struct(PLANES, BF16), struct(BUFFER, BF16), struct((...  12 us
    pallas_call x1, Pallas kernels, body(): call(final_kernel, (struct(GIVEN, BF16), struct((C, C), F32), struct((1,...  8.55 us
    pallas_call x1, Pallas kernels, body(): call(pre_kernel, struct(PLANES, BF16), [HBM, VMEM, VMEM], HBM, [held, hel...  7.05 us
    pallas_call x1, Pallas kernels, body(): call(back_kernel, struct(PLANES, BF16), [HBM, VMEM], HBM, [held, held, se...  6.89 us
    pallas_call x1, Pallas kernels, body(): call(point_kernel, (struct((8, 128), F32), struct((128, 128), BF16)), [HB...  6.69 us
  transfers between devices with their start and end apart: 5, of which 3 were waited for; matrix products, arithmetic and copies ran while one was open for 0% of the time, Pallas kernels for 19%

profile of v4, /device:TPU:1, one launch (start us, length us, event | category | flops | bytes accessed | tf_op | source)
XLA Modules:
  0.0 114.4 jit_solution(17281371380227313753)
XLA Ops:
  0.6 0.0 copy-start.2
  0.6 0.0 copy-start.3
  0.7 6.5 %field_planes.1 = bf16[128,16,128]{2,1,0:T(8,128)(2,1)} custom-call(bf16[1,16,8,256,128]{4,3,2,1,0:T(8,128)(2,1)} %field_hbm.3, bf16[64,256]{1,0:T(8,128)(2,1)} %constant.14.clone.ty_hbm.ty_ref, bf16[256,512]{1,0:T(8,128)(2,1)} %constant.16.clone.zb_hbm.zb_ref), custom_call_target="tpu_custom_call" | custom-call | flops 2000000000 | bytes 8388608 | tf_op jit(solution)/shard_map/field_planes/pallas_call | solution.py:651
  7.1 11.5 %all-to-all-start = ((bf16[128,16,128]{2,1,0:T(8,128)(2,1)}), bf16[128,16,128]{2,1,0:T(8,128)(2,1)S(1)}, u32[]{:S(2)}, u32[]{:S(2)}) async-start(bf16[128,16,128]{2,1,0:T(8,128)(2,1)} %field_planes.1), calls=%async_computation | async-start | bytes 1048576 | tf_op jit(solution)/shard_map/all_to_all | solution.py:627
  18.6 0.0 copy-done.2
  18.6 0.0 copy-done.3
  18.6 0.0 copy-start.4
  18.7 0.0 copy-start.5
  18.7 0.0 copy-start.6
  18.7 0.0 copy-start
  18.7 0.0 copy-start.1
  18.7 0.0 copy-start.7
  18.7 7.1 %point_map.1.pre_hbm = bf16[8,16,256,128]{3,2,1,0:T(8,128)(2,1)} custom-call(bf16[1,16,8,256,128]{4,3,2,1,0:T(8,128)(2,1)} %field_hbm.3, bf16[16,16]{1,0:T(8,128)(2,1)S(1)} %copy-done.2, f32[1,16]{1,0:T(1,128)S(1)} %bitcast.10), custom_call_target="tpu_custom_call" | custom-call | flops 2000000000 | bytes 16777216 | tf_op jit(solution)/shard_map/point_map/pallas_call | solution.py:657
  25.8 7.0 %all-to-all-done = bf16[128,16,128]{2,1,0:T(8,128)(2,1)S(1)} async-done(((bf16[128,16,128]{2,1,0:T(8,128)(2,1)}), bf16[128,16,128]{2,1,0:T(8,128)(2,1)S(1)}, u32[]{:S(2)}, u32[]{:S(2)}) %all-to-all-start) | async-done | bytes 524320 | tf_op jit(solution)/shard_map/all_to_all | solution.py:627
  32.8 0.0 copy-done.4
  32.8 0.0 copy-done.5
  32.8 0.0 copy-done.6
  32.8 1.6 %mix_modes.1 = (bf16[64,2,16,128]{3,2,1,0:T(8,128)(2,1)S(1)}, f32[512,128]{1,0:T(8,128)S(1)}) custom-call(s32[1]{0:T(128)} %bitcast.which_ref, bf16[64,2,16,128]{3,2,1,0:T(8,128)(2,1)S(1)} %bitcast.8, bf16[16,2,16,512]{3,2,1,0:T(8,128)(2,1)S(1)} %copy-done.4, bf16[512,1024]{1,0:T(8,128)(2,1)S(1)} %copy-done.5, bf16[1024,128]{1,0:T(8,128)(2,1)S(1)} %copy-done.6), custom_call_target="tpu_custom_call" | custom-call | flops 1000000000 | bytes 3145728 | tf_op jit(solution)/shard_map/mix_modes/pallas_call | solution.py:662
  34.4 17.9 %all_to_all.20.in_ref = bf16[128,16,128]{2,1,0:T(8,128)(2,1)S(1)} all-to-all(bf16[128,16,128]{2,1,0:T(8,128)(2,1)S(1)} %bitcast.9), channel_id=1, replica_groups=mesh['slab'=64,'batch'=2] {'slab','batch'}, dimensions={0} | all-to-all | bytes 1048576 | tf_op jit(solution)/shard_map/all_to_all | solution.py:627
  52.3 0.0 copy-done
  52.3 0.0 copy-done.1
  52.3 0.0 copy-done.7
  52.3 12.0 %signal.1 = (bf16[8,16,256,128]{3,2,1,0:T(8,128)(2,1)}, bf16[128,16,128]{2,1,0:T(8,128)(2,1)}, f32[8,256]{1,0:T(8,128)S(1)}) custom-call(bf16[128,16,128]{2,1,0:T(8,128)(2,1)S(1)} %all_to_all.20.in_ref, bf16[8,16,256,128]{3,2,1,0:T(8,128)(2,1)} %point_map.1.pre_hbm, bf16[1,16,8,256,128]{4,3,2,1,0:T(8,128)(2,1)} %cot_hbm.1, bf16[64,256]{1,0:T(8,128)(2,1)S(1)} %copy-done.1, ...), custom_call_target="tpu_custom_call" | custom-call | flops 6000000000 | bytes 25165824 | tf_op jit(solution)/shard_map/signal/pallas_call | solution.py:670
  64.3 3.9 %all-to-all-start.2 = ((bf16[128,16,128]{2,1,0:T(8,128)(2,1)}), bf16[128,16,128]{2,1,0:T(8,128)(2,1)S(1)}, u32[]{:S(2)}, u32[]{:S(2)}) async-start(bf16[128,16,128]{2,1,0:T(8,128)(2,1)} %get-tuple-element.25), calls=%async_computation.2 | async-start | bytes 1048576 | tf_op jit(solution)/shard_map/all_to_all | solution.py:627
  68.2 6.7 %point_gradient.1 = (f32[8,128]{1,0:T(8,128)S(1)}, bf16[128,128]{1,0:T(8,128)(2,1)S(1)}) custom-call(bf16[1,16,8,256,128]{4,3,2,1,0:T(8,128)(2,1)} %field_hbm.3, bf16[8,16,256,128]{3,2,1,0:T(8,128)(2,1)} %get-tuple-element.33.dpre_hbm.in_hbm, f32[8,256]{1,0:T(8,128)S(1)} %get-tuple-element.27.bias_ref, f32[512,128]{1,0:T(8,128)S(1)} %get-tuple-element.28.modes_ref.u_ref), custom_call_target="tpu_custom_call" | custom-call | flops 2000000000 | bytes 16777216 | tf_op jit(solution)/shard_map/point_gradient/pallas_call | solution.py:678
  74.9 7.5 %all-to-all-done.2 = bf16[128,16,128]{2,1,0:T(8,128)(2,1)S(1)} async-done(((bf16[128,16,128]{2,1,0:T(8,128)(2,1)}), bf16[128,16,128]{2,1,0:T(8,128)(2,1)S(1)}, u32[]{:S(2)}, u32[]{:S(2)}) %all-to-all-start.2) | async-done | bytes 524320 | tf_op jit(solution)/shard_map/all_to_all | solution.py:627
  82.3 2.3 %adjoint_modes.1 = (bf16[64,2,24,128]{3,2,1,0:T(8,128)(2,1)}, f32[32,512]{1,0:T(8,128)S(1)}, bf16[32,512]{1,0:T(8,128)(2,1)S(1)}) custom-call(s32[1]{0:T(128)} %bitcast.which_ref, bf16[64,2,16,128]{3,2,1,0:T(8,128)(2,1)S(1)} %bitcast.7, bf16[16,2,16,512]{3,2,1,0:T(8,128)(2,1)S(1)} %copy-done.4, bf16[512,1024]{1,0:T(8,128)(2,1)S(1)} %copy-done.5, ...), custom_call_target="tpu_custom_call" | custom-call | flops 1000000000 | bytes 3145728 | tf_op jit(solution)/shard_map/adjoint_modes/pallas_call | solution.py:684
  84.7 3.9 %all-to-all-start.3 = ((bf16[128,24,128]{2,1,0:T(8,128)(2,1)}), bf16[128,24,128]{2,1,0:T(8,128)(2,1)S(1)}, u32[]{:S(2)}, u32[]{:S(2)}) async-start(bf16[128,24,128]{2,1,0:T(8,128)(2,1)} %bitcast.5), calls=%async_computation.3 | async-start | bytes 1572864 | tf_op jit(solution)/shard_map/all_to_all | solution.py:627
  88.6 1.7 %collective-permute-start = (bf16[128,128]{1,0:T(8,128)(2,1)S(1)}, bf16[128,128]{1,0:T(8,128)(2,1)S(1)}, u32[]{:S(2)}, u32[]{:S(2)}) collective-permute-start(bf16[128,128]{1,0:T(8,128)(2,1)S(1)} %get-tuple-element.35), channel_id=1, source_target_pairs={{0,1},{1,0},{2,3},{3,2},{4,5},{5,4},{6,7},{7,6},{8,9},{9,8},{10,11... | collective-permute-start | bytes 98312 | tf_op jit(solution)/shard_map/ppermute | solution.py:694
  90.3 0.1 collective-permute-start.1
  90.4 6.9 %point_map_back.1.mapped_hbm = bf16[8,16,256,128]{3,2,1,0:T(8,128)(2,1)} custom-call(bf16[8,16,256,128]{3,2,1,0:T(8,128)(2,1)} %get-tuple-element.33.dpre_hbm.in_hbm, bf16[16,16]{1,0:T(8,128)(2,1)S(1)} %copy-done.2), custom_call_target="tpu_custom_call" | custom-call | flops 2000000000 | bytes 16777216 | tf_op jit(solution)/shard_map/point_map_back/pallas_call | solution.py:696
  97.3 0.0 collective-permute-done.v_bf_ref
  97.3 0.0 collective-permute-done.1.e_bf_ref
  97.3 1.5 %spectral_gradient.1 = f32[16,2,16,512]{3,2,1,0:T(8,128)} custom-call(s32[1]{0:T(128)} %bitcast.which_ref, f32[512,128]{1,0:T(8,128)S(1)} %get-tuple-element.28.modes_ref.u_ref, bf16[128,128]{1,0:T(8,128)(2,1)S(1)} %collective-permute-done.v_bf_ref, f32[32,512]{1,0:T(8,128)S(1)} %get-tuple-element.36.d_ref, bf16[32,512]{1,0:T(8,128)(2,1)S(1)} %collective-permute-done.1.e_bf_ref), custom_call_target="tpu_custom_call" | custom-call | flops 10000000 | bytes 2097152 | tf_op jit(solution)/shard_map/spectral_gradient/pallas_call | solution.py:700
  98.8 6.9 %all-to-all-done.3.in_ref = bf16[128,24,128]{2,1,0:T(8,128)(2,1)S(1)} async-done(((bf16[128,24,128]{2,1,0:T(8,128)(2,1)}), bf16[128,24,128]{2,1,0:T(8,128)(2,1)S(1)}, u32[]{:S(2)}, u32[]{:S(2)}) %all-to-all-start.3) | async-done | bytes 786464 | tf_op jit(solution)/shard_map/all_to_all | solution.py:627
  105.7 8.6 %input_gradient.1 = (bf16[1,16,8,256,128]{4,3,2,1,0:T(8,128)(2,1)}, f32[16,16]{1,0:T(8,128)}, f32[1,16]{1,0:T(1,128)}) custom-call(bf16[128,24,128]{2,1,0:T(8,128)(2,1)S(1)} %all-to-all-done.3.in_ref, bf16[8,16,256,128]{3,2,1,0:T(8,128)(2,1)} %point_map_back.1.mapped_hbm, bf16[256,64]{1,0:T(8,128)(2,1)S(1)} %copy-done.7, bf16[256,512]{1,0:T(8,128)(2,1)S(1)} %copy-done), custom_call_target="tpu_custom_call" | custom-call | flops 4000000000 | bytes 16777216 | tf_op jit(solution)/shard_map/input_gradient/pallas_call | solution.py:705
Async XLA Ops:
  0.6 18.0 %copy-start.2 = (bf16[16,16]{1,0:T(8,128)(2,1)S(1)}, bf16[16,16]{1,0:T(8,128)(2,1)}, u32[]{:S(2)}) copy-start(bf16[16,16]{1,0:T(8,128)(2,1)} %weight_ref.7) | copy-start | bytes 1540
  0.6 18.0 %copy-start.3 = (f32[16]{0:T(128)S(1)}, f32[16]{0:T(128)}, u32[]{:S(2)}) copy-start(f32[16]{0:T(128)} %param.14) | copy-start | bytes 196
  7.1 25.7 %all-to-all-start = ((bf16[128,16,128]{2,1,0:T(8,128)(2,1)}), bf16[128,16,128]{2,1,0:T(8,128)(2,1)S(1)}, u32[]{:S(2)}, u32[]{:S(2)}) async-start(bf16[128,16,128]{2,1,0:T(8,128)(2,1)} %field_planes.1), calls=%async_computation | async-start | bytes 1048576 | tf_op jit(solution)/shard_map/all_to_all | solution.py:627
  18.6 14.1 %copy-start.4 = (bf16[16,2,16,512]{3,2,1,0:T(8,128)(2,1)S(1)}, bf16[16,2,16,512]{3,2,1,0:T(8,128)(2,1)}, u32[]{:S(2)}) copy-start(bf16[16,2,16,512]{3,2,1,0:T(8,128)(2,1)} %weight_ref.6) | copy-start | bytes 1572868
  18.7 14.1 %copy-start.5 = (bf16[512,1024]{1,0:T(8,128)(2,1)S(1)}, bf16[512,1024]{1,0:T(8,128)(2,1)}, u32[]{:S(2)}) copy-start(bf16[512,1024]{1,0:T(8,128)(2,1)} %constant.17.clone.tx_ref) | copy-start | bytes 3145732
  18.7 14.1 %copy-start.6 = (bf16[1024,128]{1,0:T(8,128)(2,1)S(1)}, bf16[1024,128]{1,0:T(8,128)(2,1)}, u32[]{:S(2)}) copy-start(bf16[1024,128]{1,0:T(8,128)(2,1)} %constant.18.clone.txi_ref) | copy-start | bytes 786436
  18.7 33.6 %copy-start = (bf16[256,512]{1,0:T(8,128)(2,1)S(1)}, bf16[256,512]{1,0:T(8,128)(2,1)}, u32[]{:S(2)}) copy-start(bf16[256,512]{1,0:T(8,128)(2,1)} %constant.16.clone.zb_hbm.zb_ref) | copy-start | bytes 786436
  18.7 33.6 %copy-start.1 = (bf16[64,256]{1,0:T(8,128)(2,1)S(1)}, bf16[64,256]{1,0:T(8,128)(2,1)}, u32[]{:S(2)}) copy-start(bf16[64,256]{1,0:T(8,128)(2,1)} %constant.14.clone.ty_hbm.ty_ref) | copy-start | bytes 98308
  18.7 33.6 %copy-start.7 = (bf16[256,64]{1,0:T(8,128)(2,1)S(1)}, bf16[256,64]{1,0:T(8,128)(2,1)}, u32[]{:S(2)}) copy-start(bf16[256,64]{1,0:T(8,128)(2,1)} %constant.15.clone.tyt_ref) | copy-start | bytes 98308
  64.3 18.1 %all-to-all-start.2 = ((bf16[128,16,128]{2,1,0:T(8,128)(2,1)}), bf16[128,16,128]{2,1,0:T(8,128)(2,1)S(1)}, u32[]{:S(2)}, u32[]{:S(2)}) async-start(bf16[128,16,128]{2,1,0:T(8,128)(2,1)} %get-tuple-element.25), calls=%async_computation.2 | async-start | bytes 1048576 | tf_op jit(solution)/shard_map/all_to_all | solution.py:627
  84.7 21.0 %all-to-all-start.3 = ((bf16[128,24,128]{2,1,0:T(8,128)(2,1)}), bf16[128,24,128]{2,1,0:T(8,128)(2,1)S(1)}, u32[]{:S(2)}, u32[]{:S(2)}) async-start(bf16[128,24,128]{2,1,0:T(8,128)(2,1)} %bitcast.5), calls=%async_computation.3 | async-start | bytes 1572864 | tf_op jit(solution)/shard_map/all_to_all | solution.py:627
  88.6 8.7 %collective-permute-start = (bf16[128,128]{1,0:T(8,128)(2,1)S(1)}, bf16[128,128]{1,0:T(8,128)(2,1)S(1)}, u32[]{:S(2)}, u32[]{:S(2)}) collective-permute-start(bf16[128,128]{1,0:T(8,128)(2,1)S(1)} %get-tuple-element.35), channel_id=1, source_target_pairs={{0,1},{1,0},{2,3},{3,2},{4,5},{5,4},{6,7},{7,6},{8,9},{9,8},{10,11... | collective-permute-start | bytes 98312 | tf_op jit(solution)/shard_map/ppermute | solution.py:694
  90.3 7.0 %collective-permute-start.1 = (bf16[32,512]{1,0:T(8,128)(2,1)S(1)}, bf16[32,512]{1,0:T(8,128)(2,1)S(1)}, u32[]{:S(2)}, u32[]{:S(2)}) collective-permute-start(bf16[32,512]{1,0:T(8,128)(2,1)S(1)} %get-tuple-element.37), channel_id=1, source_target_pairs={{0,1},{1,0},{2,3},{3,2},{4,5},{5,4},{6,7},{7,6},{8,9},{9,8},{10,11... | collective-permute-start | bytes 98312 | tf_op jit(solution)/shard_map/ppermute | solution.py:695

commit v5 on v4

--- a/solution.py
+++ b/solution.py
@@ -31,6 +31,7 @@
 CUT = 8
 AHEAD = 4
 Z_CUTS = (4, 8)
+HOLD = 3
 PARTS = 8
 
 
@@ -195,6 +196,16 @@
     def start(self, x):
         for c in range(0, C, CUT):
             self.copy(x, pl.ds(c, CUT)).start()
+
+    def start_held(self, x, held):
+        @pl.when(x == held - 1)
+        def _():
+            for first in range(held):
+                self.start(first)
+
+        @pl.when(x >= held)
+        def _():
+            self.start(x)
 
     def wait(self, x):
         self.copy(x, pl.ds(0, C)).wait()
@@ -353,7 +364,7 @@
                 o = 2 * op + j
                 mapped = mapped_ref[x, o].astype(F32)
                 out_ref[x, o] = (back[:, j * 128 : (j + 1) * 128] + mapped).astype(BF16)
-        store.start(x)
+        store.start_held(x, HOLD)
         return 0
 
     lax.fori_loop(0, X, step, 0)

time: 115 us -> 114 us (level)
  transfers between devices with their start and end apart: 5 -> 5, of which waited for: 3 -> 3; matrix products, arithmetic and copies ran while one was open for 0% -> 0% of each run, Pallas kernels for 19% -> 20%
where the time goes in v5:
time: 114 us; the launch traced here: 113 us
  Pallas kernels  51.9 us (46%)
  waiting for transfers between devices  21.3 us (19%)
  starting transfers between devices  21.1 us (19%)
  blocking collectives  17.9 us (16%)
    all_to_all x3, waiting for transfers between devices, exchange(): return lax.all_to_all(buffer, BOTH, 0, 0, tiled=True)  21.3 us
    all_to_all x3, starting transfers between devices, exchange(): return lax.all_to_all(buffer, BOTH, 0, 0, tiled=True)  19.3 us
    all_to_all x1, blocking collectives, exchange(): return lax.all_to_all(buffer, BOTH, 0, 0, tiled=True)  17.9 us
    pallas_call x1, Pallas kernels, body(): call(signal_kernel, (struct(PLANES, BF16), struct(BUFFER, BF16), struct((...  12 us
    pallas_call x1, Pallas kernels, body(): call(final_kernel, (struct(GIVEN, BF16), struct((C, C), F32), struct((1,...  7.46 us
    pallas_call x1, Pallas kernels, body(): call(pre_kernel, struct(PLANES, BF16), [HBM, VMEM, VMEM], HBM, [held, hel...  7.05 us
    pallas_call x1, Pallas kernels, body(): call(back_kernel, struct(PLANES, BF16), [HBM, VMEM], HBM, [held, held, se...  6.89 us
    pallas_call x1, Pallas kernels, body(): call(point_kernel, (struct((8, 128), F32), struct((128, 128), BF16)), [HB...  6.69 us
  transfers between devices with their start and end apart: 5, of which 3 were waited for; matrix products, arithmetic and copies ran while one was open for 0% of the time, Pallas kernels for 20%

profile of v5, /device:TPU:1, one launch (start us, length us, event | category | flops | bytes accessed | tf_op | source)
XLA Modules:
  0.0 113.3 jit_solution(18128775787924007769)
XLA Ops:
  0.6 0.0 copy-start.2
  0.6 0.0 copy-start.3
  0.7 6.5 %field_planes.1 = bf16[128,16,128]{2,1,0:T(8,128)(2,1)} custom-call(bf16[1,16,8,256,128]{4,3,2,1,0:T(8,128)(2,1)} %field_hbm.3, bf16[64,256]{1,0:T(8,128)(2,1)} %constant.14.clone.ty_hbm.ty_ref, bf16[256,512]{1,0:T(8,128)(2,1)} %constant.16.clone.zb_hbm.zb_ref), custom_call_target="tpu_custom_call" | custom-call | flops 2000000000 | bytes 8388608 | tf_op jit(solution)/shard_map/field_planes/pallas_call | solution.py:662
  7.1 11.5 %all-to-all-start = ((bf16[128,16,128]{2,1,0:T(8,128)(2,1)}), bf16[128,16,128]{2,1,0:T(8,128)(2,1)S(1)}, u32[]{:S(2)}, u32[]{:S(2)}) async-start(bf16[128,16,128]{2,1,0:T(8,128)(2,1)} %field_planes.1), calls=%async_computation | async-start | bytes 1048576 | tf_op jit(solution)/shard_map/all_to_all | solution.py:638
  18.6 0.0 copy-done.2
  18.6 0.0 copy-done.3
  18.6 0.0 copy-start.4
  18.7 0.0 copy-start.5
  18.7 0.0 copy-start.6
  18.7 0.0 copy-start
  18.7 0.0 copy-start.1
  18.7 0.0 copy-start.7
  18.7 7.1 %point_map.1.pre_hbm = bf16[8,16,256,128]{3,2,1,0:T(8,128)(2,1)} custom-call(bf16[1,16,8,256,128]{4,3,2,1,0:T(8,128)(2,1)} %field_hbm.3, bf16[16,16]{1,0:T(8,128)(2,1)S(1)} %copy-done.2, f32[1,16]{1,0:T(1,128)S(1)} %bitcast.10), custom_call_target="tpu_custom_call" | custom-call | flops 2000000000 | bytes 16777216 | tf_op jit(solution)/shard_map/point_map/pallas_call | solution.py:668
  25.8 7.0 %all-to-all-done = bf16[128,16,128]{2,1,0:T(8,128)(2,1)S(1)} async-done(((bf16[128,16,128]{2,1,0:T(8,128)(2,1)}), bf16[128,16,128]{2,1,0:T(8,128)(2,1)S(1)}, u32[]{:S(2)}, u32[]{:S(2)}) %all-to-all-start) | async-done | bytes 524320 | tf_op jit(solution)/shard_map/all_to_all | solution.py:638
  32.8 0.0 copy-done.4
  32.8 0.0 copy-done.5
  32.8 0.0 copy-done.6
  32.8 1.6 %mix_modes.1 = (bf16[64,2,16,128]{3,2,1,0:T(8,128)(2,1)S(1)}, f32[512,128]{1,0:T(8,128)S(1)}) custom-call(s32[1]{0:T(128)} %bitcast.which_ref, bf16[64,2,16,128]{3,2,1,0:T(8,128)(2,1)S(1)} %bitcast.8, bf16[16,2,16,512]{3,2,1,0:T(8,128)(2,1)S(1)} %copy-done.4, bf16[512,1024]{1,0:T(8,128)(2,1)S(1)} %copy-done.5, bf16[1024,128]{1,0:T(8,128)(2,1)S(1)} %copy-done.6), custom_call_target="tpu_custom_call" | custom-call | flops 1000000000 | bytes 3145728 | tf_op jit(solution)/shard_map/mix_modes/pallas_call | solution.py:673
  34.4 17.9 %all_to_all.20.in_ref = bf16[128,16,128]{2,1,0:T(8,128)(2,1)S(1)} all-to-all(bf16[128,16,128]{2,1,0:T(8,128)(2,1)S(1)} %bitcast.9), channel_id=1, replica_groups=mesh['slab'=64,'batch'=2] {'slab','batch'}, dimensions={0} | all-to-all | bytes 1048576 | tf_op jit(solution)/shard_map/all_to_all | solution.py:638
  52.3 0.0 copy-done
  52.3 0.0 copy-done.1
  52.3 0.0 copy-done.7
  52.3 12.0 %signal.1 = (bf16[8,16,256,128]{3,2,1,0:T(8,128)(2,1)}, bf16[128,16,128]{2,1,0:T(8,128)(2,1)}, f32[8,256]{1,0:T(8,128)S(1)}) custom-call(bf16[128,16,128]{2,1,0:T(8,128)(2,1)S(1)} %all_to_all.20.in_ref, bf16[8,16,256,128]{3,2,1,0:T(8,128)(2,1)} %point_map.1.pre_hbm, bf16[1,16,8,256,128]{4,3,2,1,0:T(8,128)(2,1)} %cot_hbm.1, bf16[64,256]{1,0:T(8,128)(2,1)S(1)} %copy-done.1, ...), custom_call_target="tpu_custom_call" | custom-call | flops 6000000000 | bytes 25165824 | tf_op jit(solution)/shard_map/signal/pallas_call | solution.py:681
  64.3 3.9 %all-to-all-start.2 = ((bf16[128,16,128]{2,1,0:T(8,128)(2,1)}), bf16[128,16,128]{2,1,0:T(8,128)(2,1)S(1)}, u32[]{:S(2)}, u32[]{:S(2)}) async-start(bf16[128,16,128]{2,1,0:T(8,128)(2,1)} %get-tuple-element.25), calls=%async_computation.2 | async-start | bytes 1048576 | tf_op jit(solution)/shard_map/all_to_all | solution.py:638
  68.2 6.7 %point_gradient.1 = (f32[8,128]{1,0:T(8,128)S(1)}, bf16[128,128]{1,0:T(8,128)(2,1)S(1)}) custom-call(bf16[1,16,8,256,128]{4,3,2,1,0:T(8,128)(2,1)} %field_hbm.3, bf16[8,16,256,128]{3,2,1,0:T(8,128)(2,1)} %get-tuple-element.33.dpre_hbm.in_hbm, f32[8,256]{1,0:T(8,128)S(1)} %get-tuple-element.27.bias_ref, f32[512,128]{1,0:T(8,128)S(1)} %get-tuple-element.28.modes_ref.u_ref), custom_call_target="tpu_custom_call" | custom-call | flops 2000000000 | bytes 16777216 | tf_op jit(solution)/shard_map/point_gradient/pallas_call | solution.py:689
  74.9 7.5 %all-to-all-done.2 = bf16[128,16,128]{2,1,0:T(8,128)(2,1)S(1)} async-done(((bf16[128,16,128]{2,1,0:T(8,128)(2,1)}), bf16[128,16,128]{2,1,0:T(8,128)(2,1)S(1)}, u32[]{:S(2)}, u32[]{:S(2)}) %all-to-all-start.2) | async-done | bytes 524320 | tf_op jit(solution)/shard_map/all_to_all | solution.py:638
  82.3 2.3 %adjoint_modes.1 = (bf16[64,2,24,128]{3,2,1,0:T(8,128)(2,1)}, f32[32,512]{1,0:T(8,128)S(1)}, bf16[32,512]{1,0:T(8,128)(2,1)S(1)}) custom-call(s32[1]{0:T(128)} %bitcast.which_ref, bf16[64,2,16,128]{3,2,1,0:T(8,128)(2,1)S(1)} %bitcast.7, bf16[16,2,16,512]{3,2,1,0:T(8,128)(2,1)S(1)} %copy-done.4, bf16[512,1024]{1,0:T(8,128)(2,1)S(1)} %copy-done.5, ...), custom_call_target="tpu_custom_call" | custom-call | flops 1000000000 | bytes 3145728 | tf_op jit(solution)/shard_map/adjoint_modes/pallas_call | solution.py:695
  84.7 3.9 %all-to-all-start.3 = ((bf16[128,24,128]{2,1,0:T(8,128)(2,1)}), bf16[128,24,128]{2,1,0:T(8,128)(2,1)S(1)}, u32[]{:S(2)}, u32[]{:S(2)}) async-start(bf16[128,24,128]{2,1,0:T(8,128)(2,1)} %bitcast.5), calls=%async_computation.3 | async-start | bytes 1572864 | tf_op jit(solution)/shard_map/all_to_all | solution.py:638
  88.6 1.7 %collective-permute-start = (bf16[128,128]{1,0:T(8,128)(2,1)S(1)}, bf16[128,128]{1,0:T(8,128)(2,1)S(1)}, u32[]{:S(2)}, u32[]{:S(2)}) collective-permute-start(bf16[128,128]{1,0:T(8,128)(2,1)S(1)} %get-tuple-element.35), channel_id=1, source_target_pairs={{0,1},{1,0},{2,3},{3,2},{4,5},{5,4},{6,7},{7,6},{8,9},{9,8},{10,11... | collective-permute-start | bytes 98312 | tf_op jit(solution)/shard_map/ppermute | solution.py:705
  90.3 0.1 collective-permute-start.1
  90.4 6.9 %point_map_back.1.mapped_hbm = bf16[8,16,256,128]{3,2,1,0:T(8,128)(2,1)} custom-call(bf16[8,16,256,128]{3,2,1,0:T(8,128)(2,1)} %get-tuple-element.33.dpre_hbm.in_hbm, bf16[16,16]{1,0:T(8,128)(2,1)S(1)} %copy-done.2), custom_call_target="tpu_custom_call" | custom-call | flops 2000000000 | bytes 16777216 | tf_op jit(solution)/shard_map/point_map_back/pallas_call | solution.py:707
  97.3 0.0 collective-permute-done.v_bf_ref
  97.3 0.0 collective-permute-done.1.e_bf_ref
  97.3 1.5 %spectral_gradient.1 = f32[16,2,16,512]{3,2,1,0:T(8,128)} custom-call(s32[1]{0:T(128)} %bitcast.which_ref, f32[512,128]{1,0:T(8,128)S(1)} %get-tuple-element.28.modes_ref.u_ref, bf16[128,128]{1,0:T(8,128)(2,1)S(1)} %collective-permute-done.v_bf_ref, f32[32,512]{1,0:T(8,128)S(1)} %get-tuple-element.36.d_ref, bf16[32,512]{1,0:T(8,128)(2,1)S(1)} %collective-permute-done.1.e_bf_ref), custom_call_target="tpu_custom_call" | custom-call | flops 10000000 | bytes 2097152 | tf_op jit(solution)/shard_map/spectral_gradient/pallas_call | solution.py:711
  98.8 6.9 %all-to-all-done.3.in_ref = bf16[128,24,128]{2,1,0:T(8,128)(2,1)S(1)} async-done(((bf16[128,24,128]{2,1,0:T(8,128)(2,1)}), bf16[128,24,128]{2,1,0:T(8,128)(2,1)S(1)}, u32[]{:S(2)}, u32[]{:S(2)}) %all-to-all-start.3) | async-done | bytes 786464 | tf_op jit(solution)/shard_map/all_to_all | solution.py:638
  105.7 7.5 %input_gradient.1 = (bf16[1,16,8,256,128]{4,3,2,1,0:T(8,128)(2,1)}, f32[16,16]{1,0:T(8,128)}, f32[1,16]{1,0:T(1,128)}) custom-call(bf16[128,24,128]{2,1,0:T(8,128)(2,1)S(1)} %all-to-all-done.3.in_ref, bf16[8,16,256,128]{3,2,1,0:T(8,128)(2,1)} %point_map_back.1.mapped_hbm, bf16[256,64]{1,0:T(8,128)(2,1)S(1)} %copy-done.7, bf16[256,512]{1,0:T(8,128)(2,1)S(1)} %copy-done), custom_call_target="tpu_custom_call" | custom-call | flops 4000000000 | bytes 16777216 | tf_op jit(solution)/shard_map/input_gradient/pallas_call | solution.py:716
Async XLA Ops:
  0.6 18.0 %copy-start.2 = (bf16[16,16]{1,0:T(8,128)(2,1)S(1)}, bf16[16,16]{1,0:T(8,128)(2,1)}, u32[]{:S(2)}) copy-start(bf16[16,16]{1,0:T(8,128)(2,1)} %weight_ref.7) | copy-start | bytes 1540
  0.6 18.0 %copy-start.3 = (f32[16]{0:T(128)S(1)}, f32[16]{0:T(128)}, u32[]{:S(2)}) copy-start(f32[16]{0:T(128)} %param.14) | copy-start | bytes 196
  7.1 25.7 %all-to-all-start = ((bf16[128,16,128]{2,1,0:T(8,128)(2,1)}), bf16[128,16,128]{2,1,0:T(8,128)(2,1)S(1)}, u32[]{:S(2)}, u32[]{:S(2)}) async-start(bf16[128,16,128]{2,1,0:T(8,128)(2,1)} %field_planes.1), calls=%async_computation | async-start | bytes 1048576 | tf_op jit(solution)/shard_map/all_to_all | solution.py:638
  18.6 14.1 %copy-start.4 = (bf16[16,2,16,512]{3,2,1,0:T(8,128)(2,1)S(1)}, bf16[16,2,16,512]{3,2,1,0:T(8,128)(2,1)}, u32[]{:S(2)}) copy-start(bf16[16,2,16,512]{3,2,1,0:T(8,128)(2,1)} %weight_ref.6) | copy-start | bytes 1572868
  18.7 14.1 %copy-start.5 = (bf16[512,1024]{1,0:T(8,128)(2,1)S(1)}, bf16[512,1024]{1,0:T(8,128)(2,1)}, u32[]{:S(2)}) copy-start(bf16[512,1024]{1,0:T(8,128)(2,1)} %constant.17.clone.tx_ref) | copy-start | bytes 3145732
  18.7 14.1 %copy-start.6 = (bf16[1024,128]{1,0:T(8,128)(2,1)S(1)}, bf16[1024,128]{1,0:T(8,128)(2,1)}, u32[]{:S(2)}) copy-start(bf16[1024,128]{1,0:T(8,128)(2,1)} %constant.18.clone.txi_ref) | copy-start | bytes 786436
  18.7 33.6 %copy-start = (bf16[256,512]{1,0:T(8,128)(2,1)S(1)}, bf16[256,512]{1,0:T(8,128)(2,1)}, u32[]{:S(2)}) copy-start(bf16[256,512]{1,0:T(8,128)(2,1)} %constant.16.clone.zb_hbm.zb_ref) | copy-start | bytes 786436
  18.7 33.6 %copy-start.1 = (bf16[64,256]{1,0:T(8,128)(2,1)S(1)}, bf16[64,256]{1,0:T(8,128)(2,1)}, u32[]{:S(2)}) copy-start(bf16[64,256]{1,0:T(8,128)(2,1)} %constant.14.clone.ty_hbm.ty_ref) | copy-start | bytes 98308
  18.7 33.6 %copy-start.7 = (bf16[256,64]{1,0:T(8,128)(2,1)S(1)}, bf16[256,64]{1,0:T(8,128)(2,1)}, u32[]{:S(2)}) copy-start(bf16[256,64]{1,0:T(8,128)(2,1)} %constant.15.clone.tyt_ref) | copy-start | bytes 98308
  64.3 18.1 %all-to-all-start.2 = ((bf16[128,16,128]{2,1,0:T(8,128)(2,1)}), bf16[128,16,128]{2,1,0:T(8,128)(2,1)S(1)}, u32[]{:S(2)}, u32[]{:S(2)}) async-start(bf16[128,16,128]{2,1,0:T(8,128)(2,1)} %get-tuple-element.25), calls=%async_computation.2 | async-start | bytes 1048576 | tf_op jit(solution)/shard_map/all_to_all | solution.py:638
  84.7 21.0 %all-to-all-start.3 = ((bf16[128,24,128]{2,1,0:T(8,128)(2,1)}), bf16[128,24,128]{2,1,0:T(8,128)(2,1)S(1)}, u32[]{:S(2)}, u32[]{:S(2)}) async-start(bf16[128,24,128]{2,1,0:T(8,128)(2,1)} %bitcast.5), calls=%async_computation.3 | async-start | bytes 1572864 | tf_op jit(solution)/shard_map/all_to_all | solution.py:638
  88.6 8.7 %collective-permute-start = (bf16[128,128]{1,0:T(8,128)(2,1)S(1)}, bf16[128,128]{1,0:T(8,128)(2,1)S(1)}, u32[]{:S(2)}, u32[]{:S(2)}) collective-permute-start(bf16[128,128]{1,0:T(8,128)(2,1)S(1)} %get-tuple-element.35), channel_id=1, source_target_pairs={{0,1},{1,0},{2,3},{3,2},{4,5},{5,4},{6,7},{7,6},{8,9},{9,8},{10,11... | collective-permute-start | bytes 98312 | tf_op jit(solution)/shard_map/ppermute | solution.py:705
  90.3 7.0 %collective-permute-start.1 = (bf16[32,512]{1,0:T(8,128)(2,1)S(1)}, bf16[32,512]{1,0:T(8,128)(2,1)S(1)}, u32[]{:S(2)}, u32[]{:S(2)}) collective-permute-start(bf16[32,512]{1,0:T(8,128)(2,1)S(1)} %get-tuple-element.37), channel_id=1, source_target_pairs={{0,1},{1,0},{2,3},{3,2},{4,5},{5,4},{6,7},{7,6},{8,9},{9,8},{10,11... | collective-permute-start | bytes 98312 | tf_op jit(solution)/shard_map/ppermute | solution.py:706

commit v6 on v5

--- a/solution.py
+++ b/solution.py
@@ -131,7 +131,7 @@
 
 def z_inverse(in_ref, zf_ref, wide_ref, gather_ref, rolled_ref):
     rows = in_ref.shape[1]
-    wide_ref[...] = in_ref[...].astype(F32).reshape(128 * rows, 128)
+    wide_ref[0 : 128 * rows, :] = in_ref[...].astype(F32).reshape(128 * rows, 128)
     low = low_lanes(32)
     for half in range(2):
         for x in range(X):
@@ -368,7 +368,7 @@
         return 0
 
     lax.fori_loop(0, X, step, 0)
-    total = jnp.sum(wide_ref[...].reshape(128, 24, 128)[:, 16:24, :], axis=0) * (0.5 * SCALE_P)
+    total = jnp.sum(wide_ref[0:3072, :].reshape(128, 24, 128)[:, 16:24, :], axis=0) * (0.5 * SCALE_P)
     lane = lax.broadcasted_iota(jnp.int32, (16, 128), 1)
     row = lax.broadcasted_iota(jnp.int32, (16, 128), 0)
     point = jnp.where(row < 8, total[0:1] + total[2:3], total[1:2] + total[3:4])
@@ -651,7 +651,7 @@
     which = lax.axis_index("batch").astype(jnp.int32).reshape(1)
     zf = pltpu.VMEM((2048, 256), BF16)
     planes = pltpu.VMEM((512, 2048), BF16)
-    wide = pltpu.VMEM((2048, 128), F32)
+    wide = pltpu.VMEM((2048 + 64, 128), F32)
     gather = pltpu.VMEM((512, 512), BF16)
     held = pltpu.VMEM(PLANES, BF16)
     stage = pltpu.VMEM(BUFFER, BF16)
@@ -672,7 +672,7 @@
     got, pre = lax.optimization_barrier((got, pre))
     back, modes_u = call(
         mix_kernel,
-        (struct((SLABS, 2, 16, 128), BF16), struct((512, 128), F32)),
+        (struct((SLABS, 2, 16, 128), BF16), struct((520, 128), F32)),
         [SMEM] + [VMEM] * 4, (VMEM, VMEM),
         [pltpu.VMEM((32, 512), F32)],
         10**9, 3 * MIB, 32, "mix_modes",
@@ -696,7 +696,7 @@
         adjoint_kernel,
         (struct((SLABS, 2, 24, 128), BF16), struct((32, 512), F32), struct((32, 512), BF16)),
         [SMEM] + [VMEM] * 5, (HBM, VMEM, VMEM),
-        [pltpu.VMEM((512, 128), F32), pltpu.VMEM((512, 128), F32),
+        [pltpu.VMEM((520, 128), F32), pltpu.VMEM((520, 128), F32),
          pltpu.VMEM((SLABS, 2, 24, 128), BF16), sems],
         10**9, 3 * MIB, 32, "adjoint_modes",
     )(which, grouped(got), spectral_weight, tx, txi, extra)
@@ -710,13 +710,13 @@
     )(dpre, point_weight)
     grad_spec = call(
         spec_kernel, struct((16, 2, C, 512), F32), [SMEM] + [VMEM] * 4, VMEM,
-        [pltpu.VMEM((512, 128), F32), pltpu.VMEM((32, 512), F32)],
+        [pltpu.VMEM((520, 128), F32), pltpu.VMEM((32, 512), F32)],
         10**7, 2 * MIB, 32, "spectral_gradient",
     )(which, modes_u, other_u, rows_d, other_d)
     input_grad, grad_point, grad_bias = call(
         final_kernel, (struct(GIVEN, BF16), struct((C, C), F32), struct((1, C), F32)),
         [VMEM, HBM, VMEM, VMEM], (HBM, VMEM, VMEM),
-        [zf, pltpu.VMEM((3072, 128), F32), gather, planes, held, held, sems, sems],
+        [zf, pltpu.VMEM((3072 + 96, 128), F32), gather, planes, held, held, sems, sems],
         4 * 10**9, 2 * big, LIMIT, "input_gradient",
     )(got, mapped, tyt, zb)
     return input_grad, grad_spec, grad_point, grad_bias.reshape(C)

time: 114 us -> 114 us (level)
  no operation moved by 1% of the time
where the time goes in v6:
time: 114 us; the launch traced here: 113 us
  Pallas kernels  52 us (46%)
  waiting for transfers between devices  21.3 us (19%)
  starting transfers between devices  21.1 us (19%)
  blocking collectives  17.9 us (16%)
    all_to_all x3, waiting for transfers between devices, exchange(): return lax.all_to_all(buffer, BOTH, 0, 0, tiled=True)  21.3 us
    all_to_all x3, starting transfers between devices, exchange(): return lax.all_to_all(buffer, BOTH, 0, 0, tiled=True)  19.3 us
    all_to_all x1, blocking collectives, exchange(): return lax.all_to_all(buffer, BOTH, 0, 0, tiled=True)  17.9 us
    pallas_call x1, Pallas kernels, body(): call(signal_kernel, (struct(PLANES, BF16), struct(BUFFER, BF16), struct((...  12 us
    pallas_call x1, Pallas kernels, body(): call(final_kernel, (struct(GIVEN, BF16), struct((C, C), F32), struct((1,...  7.46 us
    pallas_call x1, Pallas kernels, body(): call(pre_kernel, struct(PLANES, BF16), [HBM, VMEM, VMEM], HBM, [held, hel...  7.07 us
    pallas_call x1, Pallas kernels, body(): call(back_kernel, struct(PLANES, BF16), [HBM, VMEM], HBM, [held, held, se...  6.88 us
    pallas_call x1, Pallas kernels, body(): call(point_kernel, (struct((8, 128), F32), struct((128, 128), BF16)), [HB...  6.7 us
  transfers between devices with their start and end apart: 5, of which 3 were waited for; matrix products, arithmetic and copies ran while one was open for 0% of the time, Pallas kernels for 20%

profile of v6, /device:TPU:1, one launch (start us, length us, event | category | flops | bytes accessed | tf_op | source)
XLA Modules:
  0.0 113.3 jit_solution(1578486861493461601)
XLA Ops:
  0.6 0.0 copy-start.2
  0.6 0.0 copy-start.3
  0.7 6.5 %field_planes.1 = bf16[128,16,128]{2,1,0:T(8,128)(2,1)} custom-call(bf16[1,16,8,256,128]{4,3,2,1,0:T(8,128)(2,1)} %field_hbm.3, bf16[64,256]{1,0:T(8,128)(2,1)} %constant.14.clone.ty_hbm.ty_ref, bf16[256,512]{1,0:T(8,128)(2,1)} %constant.16.clone.zb_hbm.zb_ref), custom_call_target="tpu_custom_call" | custom-call | flops 2000000000 | bytes 8388608 | tf_op jit(solution)/shard_map/field_planes/pallas_call | solution.py:662
  7.1 11.5 %all-to-all-start = ((bf16[128,16,128]{2,1,0:T(8,128)(2,1)}), bf16[128,16,128]{2,1,0:T(8,128)(2,1)S(1)}, u32[]{:S(2)}, u32[]{:S(2)}) async-start(bf16[128,16,128]{2,1,0:T(8,128)(2,1)} %field_planes.1), calls=%async_computation | async-start | bytes 1048576 | tf_op jit(solution)/shard_map/all_to_all | solution.py:638
  18.6 0.0 copy-done.2
  18.6 0.0 copy-done.3
  18.6 0.0 copy-start.4
  18.7 0.0 copy-start.5
  18.7 0.0 copy-start.6
  18.7 0.0 copy-start
  18.7 0.0 copy-start.1
  18.7 0.0 copy-start.7
  18.7 7.1 %point_map.1.pre_hbm = bf16[8,16,256,128]{3,2,1,0:T(8,128)(2,1)} custom-call(bf16[1,16,8,256,128]{4,3,2,1,0:T(8,128)(2,1)} %field_hbm.3, bf16[16,16]{1,0:T(8,128)(2,1)S(1)} %copy-done.2, f32[1,16]{1,0:T(1,128)S(1)} %bitcast.10), custom_call_target="tpu_custom_call" | custom-call | flops 2000000000 | bytes 16777216 | tf_op jit(solution)/shard_map/point_map/pallas_call | solution.py:668
  25.8 7.0 %all-to-all-done = bf16[128,16,128]{2,1,0:T(8,128)(2,1)S(1)} async-done(((bf16[128,16,128]{2,1,0:T(8,128)(2,1)}), bf16[128,16,128]{2,1,0:T(8,128)(2,1)S(1)}, u32[]{:S(2)}, u32[]{:S(2)}) %all-to-all-start) | async-done | bytes 524320 | tf_op jit(solution)/shard_map/all_to_all | solution.py:638
  32.8 0.0 copy-done.4
  32.8 0.0 copy-done.5
  32.8 0.0 copy-done.6
  32.8 1.6 %mix_modes.1 = (bf16[64,2,16,128]{3,2,1,0:T(8,128)(2,1)S(1)}, f32[520,128]{1,0:T(8,128)S(1)}) custom-call(s32[1]{0:T(128)} %bitcast.which_ref, bf16[64,2,16,128]{3,2,1,0:T(8,128)(2,1)S(1)} %bitcast.8, bf16[16,2,16,512]{3,2,1,0:T(8,128)(2,1)S(1)} %copy-done.4, bf16[512,1024]{1,0:T(8,128)(2,1)S(1)} %copy-done.5, bf16[1024,128]{1,0:T(8,128)(2,1)S(1)} %copy-done.6), custom_call_target="tpu_custom_call" | custom-call | flops 1000000000 | bytes 3145728 | tf_op jit(solution)/shard_map/mix_modes/pallas_call | solution.py:673
  34.4 17.9 %all_to_all.20.in_ref = bf16[128,16,128]{2,1,0:T(8,128)(2,1)S(1)} all-to-all(bf16[128,16,128]{2,1,0:T(8,128)(2,1)S(1)} %bitcast.9), channel_id=1, replica_groups=mesh['slab'=64,'batch'=2] {'slab','batch'}, dimensions={0} | all-to-all | bytes 1048576 | tf_op jit(solution)/shard_map/all_to_all | solution.py:638
  52.3 0.0 copy-done
  52.3 0.0 copy-done.1
  52.3 0.0 copy-done.7
  52.3 12.0 %signal.1 = (bf16[8,16,256,128]{3,2,1,0:T(8,128)(2,1)}, bf16[128,16,128]{2,1,0:T(8,128)(2,1)}, f32[8,256]{1,0:T(8,128)S(1)}) custom-call(bf16[128,16,128]{2,1,0:T(8,128)(2,1)S(1)} %all_to_all.20.in_ref, bf16[8,16,256,128]{3,2,1,0:T(8,128)(2,1)} %point_map.1.pre_hbm, bf16[1,16,8,256,128]{4,3,2,1,0:T(8,128)(2,1)} %cot_hbm.1, bf16[64,256]{1,0:T(8,128)(2,1)S(1)} %copy-done.1, ...), custom_call_target="tpu_custom_call" | custom-call | flops 6000000000 | bytes 25165824 | tf_op jit(solution)/shard_map/signal/pallas_call | solution.py:681
  64.3 3.9 %all-to-all-start.2 = ((bf16[128,16,128]{2,1,0:T(8,128)(2,1)}), bf16[128,16,128]{2,1,0:T(8,128)(2,1)S(1)}, u32[]{:S(2)}, u32[]{:S(2)}) async-start(bf16[128,16,128]{2,1,0:T(8,128)(2,1)} %get-tuple-element.25), calls=%async_computation.2 | async-start | bytes 1048576 | tf_op jit(solution)/shard_map/all_to_all | solution.py:638
  68.2 6.7 %point_gradient.1 = (f32[8,128]{1,0:T(8,128)S(1)}, bf16[128,128]{1,0:T(8,128)(2,1)S(1)}) custom-call(bf16[1,16,8,256,128]{4,3,2,1,0:T(8,128)(2,1)} %field_hbm.3, bf16[8,16,256,128]{3,2,1,0:T(8,128)(2,1)} %get-tuple-element.33.dpre_hbm.in_hbm, f32[8,256]{1,0:T(8,128)S(1)} %get-tuple-element.27.bias_ref, f32[520,128]{1,0:T(8,128)S(1)} %get-tuple-element.28.modes_ref.u_ref), custom_call_target="tpu_custom_call" | custom-call | flops 2000000000 | bytes 16777216 | tf_op jit(solution)/shard_map/point_gradient/pallas_call | solution.py:689
  74.9 7.5 %all-to-all-done.2 = bf16[128,16,128]{2,1,0:T(8,128)(2,1)S(1)} async-done(((bf16[128,16,128]{2,1,0:T(8,128)(2,1)}), bf16[128,16,128]{2,1,0:T(8,128)(2,1)S(1)}, u32[]{:S(2)}, u32[]{:S(2)}) %all-to-all-start.2) | async-done | bytes 524320 | tf_op jit(solution)/shard_map/all_to_all | solution.py:638
  82.4 2.3 %adjoint_modes.1 = (bf16[64,2,24,128]{3,2,1,0:T(8,128)(2,1)}, f32[32,512]{1,0:T(8,128)S(1)}, bf16[32,512]{1,0:T(8,128)(2,1)S(1)}) custom-call(s32[1]{0:T(128)} %bitcast.which_ref, bf16[64,2,16,128]{3,2,1,0:T(8,128)(2,1)S(1)} %bitcast.7, bf16[16,2,16,512]{3,2,1,0:T(8,128)(2,1)S(1)} %copy-done.4, bf16[512,1024]{1,0:T(8,128)(2,1)S(1)} %copy-done.5, ...), custom_call_target="tpu_custom_call" | custom-call | flops 1000000000 | bytes 3145728 | tf_op jit(solution)/shard_map/adjoint_modes/pallas_call | solution.py:695
  84.7 3.9 %all-to-all-start.3 = ((bf16[128,24,128]{2,1,0:T(8,128)(2,1)}), bf16[128,24,128]{2,1,0:T(8,128)(2,1)S(1)}, u32[]{:S(2)}, u32[]{:S(2)}) async-start(bf16[128,24,128]{2,1,0:T(8,128)(2,1)} %bitcast.5), calls=%async_computation.3 | async-start | bytes 1572864 | tf_op jit(solution)/shard_map/all_to_all | solution.py:638
  88.6 1.7 %collective-permute-start = (bf16[128,128]{1,0:T(8,128)(2,1)S(1)}, bf16[128,128]{1,0:T(8,128)(2,1)S(1)}, u32[]{:S(2)}, u32[]{:S(2)}) collective-permute-start(bf16[128,128]{1,0:T(8,128)(2,1)S(1)} %get-tuple-element.35), channel_id=1, source_target_pairs={{0,1},{1,0},{2,3},{3,2},{4,5},{5,4},{6,7},{7,6},{8,9},{9,8},{10,11... | collective-permute-start | bytes 98312 | tf_op jit(solution)/shard_map/ppermute | solution.py:705
  90.3 0.1 collective-permute-start.1
  90.4 6.9 %point_map_back.1.mapped_hbm = bf16[8,16,256,128]{3,2,1,0:T(8,128)(2,1)} custom-call(bf16[8,16,256,128]{3,2,1,0:T(8,128)(2,1)} %get-tuple-element.33.dpre_hbm.in_hbm, bf16[16,16]{1,0:T(8,128)(2,1)S(1)} %copy-done.2), custom_call_target="tpu_custom_call" | custom-call | flops 2000000000 | bytes 16777216 | tf_op jit(solution)/shard_map/point_map_back/pallas_call | solution.py:707
  97.3 0.0 collective-permute-done.v_bf_ref
  97.3 0.0 collective-permute-done.1.e_bf_ref
  97.3 1.5 %spectral_gradient.1 = f32[16,2,16,512]{3,2,1,0:T(8,128)} custom-call(s32[1]{0:T(128)} %bitcast.which_ref, f32[520,128]{1,0:T(8,128)S(1)} %get-tuple-element.28.modes_ref.u_ref, bf16[128,128]{1,0:T(8,128)(2,1)S(1)} %collective-permute-done.v_bf_ref, f32[32,512]{1,0:T(8,128)S(1)} %get-tuple-element.36.d_ref, bf16[32,512]{1,0:T(8,128)(2,1)S(1)} %collective-permute-done.1.e_bf_ref), custom_call_target="tpu_custom_call" | custom-call | flops 10000000 | bytes 2097152 | tf_op jit(solution)/shard_map/spectral_gradient/pallas_call | solution.py:711
  98.8 6.9 %all-to-all-done.3.in_ref = bf16[128,24,128]{2,1,0:T(8,128)(2,1)S(1)} async-done(((bf16[128,24,128]{2,1,0:T(8,128)(2,1)}), bf16[128,24,128]{2,1,0:T(8,128)(2,1)S(1)}, u32[]{:S(2)}, u32[]{:S(2)}) %all-to-all-start.3) | async-done | bytes 786464 | tf_op jit(solution)/shard_map/all_to_all | solution.py:638
  105.7 7.5 %input_gradient.1 = (bf16[1,16,8,256,128]{4,3,2,1,0:T(8,128)(2,1)}, f32[16,16]{1,0:T(8,128)}, f32[1,16]{1,0:T(1,128)}) custom-call(bf16[128,24,128]{2,1,0:T(8,128)(2,1)S(1)} %all-to-all-done.3.in_ref, bf16[8,16,256,128]{3,2,1,0:T(8,128)(2,1)} %point_map_back.1.mapped_hbm, bf16[256,64]{1,0:T(8,128)(2,1)S(1)} %copy-done.7, bf16[256,512]{1,0:T(8,128)(2,1)S(1)} %copy-done), custom_call_target="tpu_custom_call" | custom-call | flops 4000000000 | bytes 16777216 | tf_op jit(solution)/shard_map/input_gradient/pallas_call | solution.py:716
Async XLA Ops:
  0.6 18.0 %copy-start.2 = (bf16[16,16]{1,0:T(8,128)(2,1)S(1)}, bf16[16,16]{1,0:T(8,128)(2,1)}, u32[]{:S(2)}) copy-start(bf16[16,16]{1,0:T(8,128)(2,1)} %weight_ref.7) | copy-start | bytes 1540
  0.6 18.0 %copy-start.3 = (f32[16]{0:T(128)S(1)}, f32[16]{0:T(128)}, u32[]{:S(2)}) copy-start(f32[16]{0:T(128)} %param.14) | copy-start | bytes 196
  7.1 25.7 %all-to-all-start = ((bf16[128,16,128]{2,1,0:T(8,128)(2,1)}), bf16[128,16,128]{2,1,0:T(8,128)(2,1)S(1)}, u32[]{:S(2)}, u32[]{:S(2)}) async-start(bf16[128,16,128]{2,1,0:T(8,128)(2,1)} %field_planes.1), calls=%async_computation | async-start | bytes 1048576 | tf_op jit(solution)/shard_map/all_to_all | solution.py:638
  18.6 14.1 %copy-start.4 = (bf16[16,2,16,512]{3,2,1,0:T(8,128)(2,1)S(1)}, bf16[16,2,16,512]{3,2,1,0:T(8,128)(2,1)}, u32[]{:S(2)}) copy-start(bf16[16,2,16,512]{3,2,1,0:T(8,128)(2,1)} %weight_ref.6) | copy-start | bytes 1572868
  18.7 14.1 %copy-start.5 = (bf16[512,1024]{1,0:T(8,128)(2,1)S(1)}, bf16[512,1024]{1,0:T(8,128)(2,1)}, u32[]{:S(2)}) copy-start(bf16[512,1024]{1,0:T(8,128)(2,1)} %constant.17.clone.tx_ref) | copy-start | bytes 3145732
  18.7 14.1 %copy-start.6 = (bf16[1024,128]{1,0:T(8,128)(2,1)S(1)}, bf16[1024,128]{1,0:T(8,128)(2,1)}, u32[]{:S(2)}) copy-start(bf16[1024,128]{1,0:T(8,128)(2,1)} %constant.18.clone.txi_ref) | copy-start | bytes 786436
  18.7 33.6 %copy-start = (bf16[256,512]{1,0:T(8,128)(2,1)S(1)}, bf16[256,512]{1,0:T(8,128)(2,1)}, u32[]{:S(2)}) copy-start(bf16[256,512]{1,0:T(8,128)(2,1)} %constant.16.clone.zb_hbm.zb_ref) | copy-start | bytes 786436
  18.7 33.6 %copy-start.1 = (bf16[64,256]{1,0:T(8,128)(2,1)S(1)}, bf16[64,256]{1,0:T(8,128)(2,1)}, u32[]{:S(2)}) copy-start(bf16[64,256]{1,0:T(8,128)(2,1)} %constant.14.clone.ty_hbm.ty_ref) | copy-start | bytes 98308
  18.7 33.6 %copy-start.7 = (bf16[256,64]{1,0:T(8,128)(2,1)S(1)}, bf16[256,64]{1,0:T(8,128)(2,1)}, u32[]{:S(2)}) copy-start(bf16[256,64]{1,0:T(8,128)(2,1)} %constant.15.clone.tyt_ref) | copy-start | bytes 98308
  64.3 18.1 %all-to-all-start.2 = ((bf16[128,16,128]{2,1,0:T(8,128)(2,1)}), bf16[128,16,128]{2,1,0:T(8,128)(2,1)S(1)}, u32[]{:S(2)}, u32[]{:S(2)}) async-start(bf16[128,16,128]{2,1,0:T(8,128)(2,1)} %get-tuple-element.25), calls=%async_computation.2 | async-start | bytes 1048576 | tf_op jit(solution)/shard_map/all_to_all | solution.py:638
  84.7 21.0 %all-to-all-start.3 = ((bf16[128,24,128]{2,1,0:T(8,128)(2,1)}), bf16[128,24,128]{2,1,0:T(8,128)(2,1)S(1)}, u32[]{:S(2)}, u32[]{:S(2)}) async-start(bf16[128,24,128]{2,1,0:T(8,128)(2,1)} %bitcast.5), calls=%async_computation.3 | async-start | bytes 1572864 | tf_op jit(solution)/shard_map/all_to_all | solution.py:638
  88.6 8.7 %collective-permute-start = (bf16[128,128]{1,0:T(8,128)(2,1)S(1)}, bf16[128,128]{1,0:T(8,128)(2,1)S(1)}, u32[]{:S(2)}, u32[]{:S(2)}) collective-permute-start(bf16[128,128]{1,0:T(8,128)(2,1)S(1)} %get-tuple-element.35), channel_id=1, source_target_pairs={{0,1},{1,0},{2,3},{3,2},{4,5},{5,4},{6,7},{7,6},{8,9},{9,8},{10,11... | collective-permute-start | bytes 98312 | tf_op jit(solution)/shard_map/ppermute | solution.py:705
  90.3 7.0 %collective-permute-start.1 = (bf16[32,512]{1,0:T(8,128)(2,1)S(1)}, bf16[32,512]{1,0:T(8,128)(2,1)S(1)}, u32[]{:S(2)}, u32[]{:S(2)}) collective-permute-start(bf16[32,512]{1,0:T(8,128)(2,1)S(1)} %get-tuple-element.37), channel_id=1, source_target_pairs={{0,1},{1,0},{2,3},{3,2},{4,5},{5,4},{6,7},{7,6},{8,9},{9,8},{10,11... | collective-permute-start | bytes 98312 | tf_op jit(solution)/shard_map/ppermute | solution.py:706
